TPU v7x, 32 devices: a whole 2x2x4 slice. The times are simulated.
32 devices in a mesh: row: 8 (over z, x), col: 4 (over y, core).
Axes of the slice: x: 2, y: 2, z: 4, core: 2. Of those that a mesh axis runs over, the one named last changes fastest.
Arguments:
- tokens: bfloat16 [8192, 2048], P('row', 'col'), may hold values from -6 to 6
- lengths: int32 [8], P('row'), may hold values from 512 to 1024, as said below
- norm_in: float32 [2048], replicated, may hold values from 0.25 to 2.9
- q_weight: bfloat16 [2048, 2048], P('row', 'col'), may hold values from -0.125 to 0.125
- k_weight: bfloat16 [2048, 2048], P('row', 'col'), may hold values from -0.125 to 0.125
- v_weight: bfloat16 [2048, 2048], P('row', 'col'), may hold values from -0.125 to 0.125
- conv_q: float32 [4, 2048], P(None, 'col'), may hold values from -3 to 3
- conv_k: float32 [4, 2048], P(None, 'col'), may hold values from -3 to 3
- conv_v: float32 [4, 2048], P(None, 'col'), may hold values from -3 to 3
- beta_weight: bfloat16 [2048, 16], P('row', 'col'), may hold values from -0.125 to 0.125
- head_gain: float32 [128], replicated, may hold values from 0.5 to 1.5
- out_weight: bfloat16 [2048, 2048], P('col', 'row'), may hold values from -0.125 to 0.125
- norm_mid: float32 [2048], replicated, may hold values from 0.25 to 2.9
- gate_weight: bfloat16 [2048, 5632], P('row', 'col'), may hold values from -0.125 to 0.125
- up_weight: bfloat16 [2048, 5632], P('row', 'col'), may hold values from -0.125 to 0.125
- down_weight: bfloat16 [5632, 2048], P('col', 'row'), may hold values from -0.078125 to 0.078125
- cotangent: bfloat16 [8192, 2048], P('row', 'col'), may hold values from -6 to 6
Outputs:
- layer_out: bfloat16 [8192, 2048], P('row', 'col')
- grad_tokens: float32 [8192, 2048], P('row', 'col')
- grad_norm_in: float32 [2048], replicated
- grad_q: float32 [2048, 2048], P('row', 'col')
- grad_k: float32 [2048, 2048], P('row', 'col')
- grad_v: float32 [2048, 2048], P('row', 'col')
- grad_conv_q: float32 [4, 2048], P(None, 'col')
- grad_conv_k: float32 [4, 2048], P(None, 'col')
- grad_conv_v: float32 [4, 2048], P(None, 'col')
- grad_beta: float32 [2048, 16], P('row', 'col')
- grad_head_gain: float32 [128], replicated
- grad_out: float32 [2048, 2048], P('col', 'row')
- grad_norm_mid: float32 [2048], replicated
- grad_gate: float32 [2048, 5632], P('row', 'col')
- grad_up: float32 [2048, 5632], P('row', 'col')
- grad_down: float32 [5632, 2048], P('col', 'row')
Inputs may be any that keep to these rules, and one draw needn't show every extreme that they name: `lengths`: each slot's live rows come first. Some slot is full and some slot holds exactly 512 live rows.
All inputs are finite; a program needn't handle non-finite values.
Results may differ from a plain program's by a relative error of at most 0.015.
Values may be sent and summed in bfloat16 or wider, within the bound.
No kernel may reach another device: no remote copies, remote signals or barrier semaphores. Data moves between devices by JAX's collectives and lax.ppermute only.
A program may use at most 320 MiB of HBM per device.

v0:
```python
import jax
import jax.numpy as jnp
from jax import lax
from jax.sharding import PartitionSpec as P

BLOCK = 64


epsilon = 1e-06
highest = lax.Precision.HIGHEST


def causal_conv(projected, kernel):
    length = projected.shape[0]
    padded = jnp.pad(projected, ((3, 0), (0, 0)))
    summed = kernel[0] * padded[0:length]
    for offset in range(1, 4):
        summed = summed + kernel[offset] * padded[offset : offset + length]
    return summed


def delta_block(states, blocks):
    queries, keys_in, values_in, strength = blocks
    block_len = keys_in.shape[1]
    key_width = keys_in.shape[2]
    row_ids = lax.broadcasted_iota(jnp.int32, (block_len, block_len), 0)
    col_ids = lax.broadcasted_iota(jnp.int32, (block_len, block_len), 1)
    strict_lower = (row_ids > col_ids).astype(jnp.float32)
    upto_lower = (row_ids >= col_ids).astype(jnp.float32)
    key_gram = jnp.einsum("hcd,hed->hce", keys_in, keys_in, precision=highest)
    system = jnp.eye(block_len, dtype=jnp.float32) + strength[:, :, None] * key_gram * strict_lower
    right_side = strength[:, :, None] * jnp.concatenate([keys_in, values_in], axis=2)
    solved = lax.linalg.triangular_solve(
        system, right_side, left_side=True, lower=True, unit_diagonal=True
    )
    w_factors = solved[:, :, :key_width]
    u_factors = solved[:, :, key_width:]
    fresh_vals = u_factors - jnp.einsum("hcd,hde->hce", w_factors, states, precision=highest)
    scores = jnp.einsum("hcd,hed->hce", queries, keys_in, precision=highest) * upto_lower
    output = jnp.einsum("hcd,hde->hce", queries, states, precision=highest)
    output = output + jnp.einsum("hce,hed->hcd", scores, fresh_vals, precision=highest)
    states = states + jnp.einsum("hcd,hce->hde", keys_in, fresh_vals, precision=highest)
    return (states, output)


def delta_mixer(q_proj, k_proj, v_proj, beta_logit, conv_q, conv_k, conv_v, head_gain):
    head_dim = head_gain.shape[0]
    head_count = beta_logit.shape[1]
    length = q_proj.shape[0]
    block_count = length // BLOCK
    queries = jax.nn.silu(causal_conv(q_proj, conv_q)) * head_dim ** (-0.5)
    keys_raw = jax.nn.silu(causal_conv(k_proj, conv_k)).reshape(length, head_count, head_dim)
    keys_unit = keys_raw * lax.rsqrt(jnp.sum(keys_raw * keys_raw, axis=2, keepdims=True) + epsilon)
    values = jax.nn.silu(causal_conv(v_proj, conv_v))
    strength = jax.nn.sigmoid(beta_logit)

    def split_blocks(tensor):
        return tensor.reshape(block_count, BLOCK, head_count, head_dim).transpose(0, 2, 1, 3)

    blocks = (
        split_blocks(queries),
        split_blocks(keys_unit),
        split_blocks(values),
        strength.reshape(block_count, BLOCK, head_count).transpose(0, 2, 1),
    )
    start_state = jnp.zeros((head_count, head_dim, head_dim), jnp.float32)
    final_state, pieces = lax.scan(jax.checkpoint(delta_block), start_state, blocks)
    merged = pieces.transpose(0, 2, 1, 3).reshape(length, head_count, head_dim)
    normed = (
        merged * lax.rsqrt(jnp.mean(merged * merged, axis=2, keepdims=True) + epsilon) * head_gain
    )
    return normed.reshape(length, head_count * head_dim)


def product(left, right, form):
    return jnp.einsum(form, left, right, preferred_element_type=jnp.float32)


def rms_factor(rows_in):
    return lax.rsqrt(jnp.mean(rows_in * rows_in, axis=1, keepdims=True) + epsilon)


def gather_features(shard):
    return lax.all_gather(shard, "col", axis=1, tiled=True)


def sum_features(partial_value):
    return lax.psum_scatter(partial_value, "col", scatter_dimension=1, tiled=True)


def fetch_weights(shards):
    return (
        lax.all_gather(shards[0], "row", axis=0, tiled=True),
        lax.all_gather(shards[1], "row", axis=0, tiled=True),
        lax.all_gather(shards[2], "row", axis=0, tiled=True),
        lax.all_gather(shards[3], "row", axis=0, tiled=True),
        lax.all_gather(shards[4], "row", axis=0, tiled=True),
        lax.all_gather(shards[5], "row", axis=0, tiled=True),
        lax.all_gather(shards[6], "row", axis=1, tiled=True),
        lax.all_gather(shards[7], "row", axis=1, tiled=True),
    )


def norm_back_shard(partial_value, rows_in, factor, gain_vec):
    shard_width = partial_value.shape[1] // lax.axis_size("col")
    feat_start = lax.axis_index("col") * shard_width
    cot_shard = sum_features(partial_value)
    rows_shard = lax.dynamic_slice_in_dim(rows_in, feat_start, shard_width, 1)
    gain_shard = lax.dynamic_slice_in_dim(gain_vec, feat_start, shard_width, 0)
    inner_sum = lax.psum(jnp.sum(rows_shard * gain_shard * cot_shard, axis=1, keepdims=True), "col")
    return (
        factor * gain_shard * cot_shard
        - rows_shard * factor**3 * inner_sum / partial_value.shape[1]
    )


def forward(tokens, live_rows, weights, smalls):
    full_q, full_k, full_v, full_beta, full_gate, full_up, full_out, full_down = weights
    norm_in, conv_q, conv_k, conv_v, head_gain, norm_mid = smalls
    whole_in = gather_features(tokens).astype(jnp.float32)
    factor_in = rms_factor(whole_in)
    normed = (whole_in * factor_in * norm_in).astype(jnp.bfloat16)
    q_proj = product(normed, full_q, "td,dh->th")
    k_proj = product(normed, full_k, "td,dh->th")
    v_proj = product(normed, full_v, "td,dh->th")
    beta_logit = product(normed, full_beta, "td,dh->th")
    mixed_f32, mixer_back = jax.vjp(
        delta_mixer, q_proj, k_proj, v_proj, beta_logit, conv_q, conv_k, conv_v, head_gain
    )
    mixed = mixed_f32.astype(jnp.bfloat16)
    branch = sum_features(product(mixed, full_out, "th,hd->td"))
    middle = tokens.astype(jnp.float32) + live_rows * branch
    whole_mid = gather_features(middle.astype(jnp.bfloat16)).astype(jnp.float32)
    factor_mid = rms_factor(whole_mid)
    normed_mid = (whole_mid * factor_mid * norm_mid).astype(jnp.bfloat16)
    gate_val = product(normed_mid, full_gate, "td,df->tf")
    up_val = product(normed_mid, full_up, "td,df->tf")
    hidden = (jax.nn.silu(gate_val) * up_val).astype(jnp.bfloat16)
    result = middle + live_rows * sum_features(product(hidden, full_down, "tf,fd->td"))
    return (
        whole_in,
        factor_in,
        normed,
        mixed,
        mixer_back,
        whole_mid,
        factor_mid,
        normed_mid,
        gate_val,
        up_val,
        hidden,
        result,
    )


def per_device(
    tokens,
    lengths,
    norm_in,
    q_weight,
    k_weight,
    v_weight,
    conv_q,
    conv_k,
    conv_v,
    beta_weight,
    head_gain,
    out_weight,
    norm_mid,
    gate_weight,
    up_weight,
    down_weight,
    cotangent,
):
    slot_rows = tokens.shape[0]
    live_rows = (jnp.arange(slot_rows, dtype=jnp.int32) < lengths[0]).astype(jnp.float32)[:, None]
    smalls = (norm_in, conv_q, conv_k, conv_v, head_gain, norm_mid)
    shards = (
        q_weight,
        k_weight,
        v_weight,
        beta_weight,
        gate_weight,
        up_weight,
        out_weight,
        down_weight,
    )
    weights = fetch_weights(shards)
    kept_values = forward(tokens, live_rows, weights, smalls)
    layer_out = kept_values[11].astype(jnp.bfloat16)
    (
        whole_in,
        factor_in,
        normed,
        mixed,
        mixer_back,
        whole_mid,
        factor_mid,
        normed_mid,
        gate_val,
        up_val,
        hidden,
        result,
    ) = kept_values
    full_q, full_k, full_v, full_beta, full_gate, full_up, full_out, full_down = weights
    cot_whole = gather_features(cotangent)
    ffn_cot = cot_whole * live_rows.astype(jnp.bfloat16)
    grad_down = product(hidden, ffn_cot, "tf,td->fd")
    hidden_cot = product(ffn_cot, full_down, "td,fd->tf")
    gate_sig = jax.nn.sigmoid(gate_val)
    gate_cot = (hidden_cot * up_val * gate_sig * (1.0 + gate_val * (1.0 - gate_sig))).astype(
        jnp.bfloat16
    )
    up_cot = (hidden_cot * gate_val * gate_sig).astype(jnp.bfloat16)
    grad_gate = product(normed_mid, gate_cot, "td,tf->df")
    grad_up = product(normed_mid, up_cot, "td,tf->df")
    mid_part = product(gate_cot, full_gate, "tf,df->td") + product(up_cot, full_up, "tf,df->td")
    gain_mid_part = jnp.sum(mid_part * whole_mid * factor_mid, axis=0)
    cot_f32 = cotangent.astype(jnp.float32)
    middle_cot = cot_f32 + norm_back_shard(mid_part, whole_mid, factor_mid, norm_mid)
    branch_cot = gather_features((live_rows * middle_cot).astype(jnp.bfloat16))
    grad_out = product(mixed, branch_cot, "th,td->hd")
    mixed_cot = product(branch_cot, full_out, "td,hd->th")
    q_cot, k_cot, v_cot, beta_cot, grad_conv_q, grad_conv_k, grad_conv_v, grad_head = mixer_back(
        mixed_cot
    )
    q_low = q_cot.astype(jnp.bfloat16)
    k_low = k_cot.astype(jnp.bfloat16)
    v_low = v_cot.astype(jnp.bfloat16)
    beta_low = beta_cot.astype(jnp.bfloat16)
    grad_q = product(normed, q_low, "td,th->dh")
    grad_k = product(normed, k_low, "td,th->dh")
    grad_v = product(normed, v_low, "td,th->dh")
    grad_beta = product(normed, beta_low, "td,th->dh")
    in_part = product(q_low, full_q, "th,dh->td") + product(k_low, full_k, "th,dh->td")
    in_part = (
        in_part + product(v_low, full_v, "th,dh->td") + product(beta_low, full_beta, "th,dh->td")
    )
    gain_in_part = jnp.sum(in_part * whole_in * factor_in, axis=0)
    grad_tokens = middle_cot + norm_back_shard(in_part, whole_in, factor_in, norm_in)
    weight_sums = (
        lax.psum_scatter(
            grad_q.astype(jnp.bfloat16), "row", scatter_dimension=0, tiled=True
        ).astype(jnp.float32),
        lax.psum_scatter(
            grad_k.astype(jnp.bfloat16), "row", scatter_dimension=0, tiled=True
        ).astype(jnp.float32),
        lax.psum_scatter(
            grad_v.astype(jnp.bfloat16), "row", scatter_dimension=0, tiled=True
        ).astype(jnp.float32),
        lax.psum_scatter(
            grad_beta.astype(jnp.bfloat16), "row", scatter_dimension=0, tiled=True
        ).astype(jnp.float32),
        lax.psum_scatter(
            grad_gate.astype(jnp.bfloat16), "row", scatter_dimension=0, tiled=True
        ).astype(jnp.float32),
        lax.psum_scatter(
            grad_up.astype(jnp.bfloat16), "row", scatter_dimension=0, tiled=True
        ).astype(jnp.float32),
        lax.psum_scatter(
            grad_out.astype(jnp.bfloat16), "row", scatter_dimension=1, tiled=True
        ).astype(jnp.float32),
        lax.psum_scatter(
            grad_down.astype(jnp.bfloat16), "row", scatter_dimension=1, tiled=True
        ).astype(jnp.float32),
    )
    gain_sums = lax.psum((gain_in_part, gain_mid_part, grad_head), ("row", "col"))
    conv_sums = lax.psum((grad_conv_q, grad_conv_k, grad_conv_v), "row")
    return (
        layer_out,
        grad_tokens,
        gain_sums[0],
        weight_sums[0],
        weight_sums[1],
        weight_sums[2],
        conv_sums[0],
        conv_sums[1],
        conv_sums[2],
        weight_sums[3],
        gain_sums[2],
        weight_sums[6],
        gain_sums[1],
        weight_sums[4],
        weight_sums[5],
        weight_sums[7],
    )


def solution(mesh):
    return jax.shard_map(
        per_device,
        mesh=mesh,
        in_specs=(
            P("row", "col"),
            P("row"),
            P(),
            P("row", "col"),
            P("row", "col"),
            P("row", "col"),
            P(None, "col"),
            P(None, "col"),
            P(None, "col"),
            P("row", "col"),
            P(),
            P("col", "row"),
            P(),
            P("row", "col"),
            P("row", "col"),
            P("col", "row"),
            P("row", "col"),
        ),
        out_specs=(
            P("row", "col"),
            P("row", "col"),
            P(),
            P("row", "col"),
            P("row", "col"),
            P("row", "col"),
            P(None, "col"),
            P(None, "col"),
            P(None, "col"),
            P("row", "col"),
            P(),
            P("col", "row"),
            P(),
            P("row", "col"),
            P("row", "col"),
            P("col", "row"),
        ),
        check_vma=False,
    )
```

profile of v0, /device:TPU:0, one launch (start us, length us, event | category | flops | bytes accessed | tf_op | source)
XLA Modules:
  0.0 2422.6 jit_solution(638106343618657701)
XLA Ops:
  10.9 27.8 %all_gather.38 = bf16[2048,4]{0,1:T(4,128)(2,1)S(1)} all-gather(bf16[256,4]{0,1:T(4,128)(2,1)S(1)} %copy-done.87), channel_id=1, replica_groups=mesh['row'=8,'col'=4] {'row'}, dimensions={0}, use_global_device_ids=true | all-gather | bytes 18432 | tf_op jit(solution)/shard_map/all_gather | solution.py:96
  53.7 44.6 %all-gather.14.cloned.1.call-done = bf16[2048,512]{1,0:T(8,128)(2,1)} async-done(((bf16[256,512]{1,0:T(8,128)(2,1)}), bf16[2048,512]{1,0:T(8,128)(2,1)}) %all-gather.14.cloned.1.call-update) | async-done | bytes 2097168 | tf_op jit(solution)/shard_map/all_gather | solution.py:94
  114.7 33.5 %all-gather.16.cloned.1.call-done = bf16[2048,512]{1,0:T(8,128)(2,1)} async-done(((bf16[256,512]{1,0:T(8,128)(2,1)}), bf16[2048,512]{1,0:T(8,128)(2,1)}) %all-gather.16.cloned.1.call-update) | async-done | bytes 2097168 | tf_op jit(solution)/shard_map/all_gather | solution.py:95
  157.8 40.2 %all-gather.18.cloned.1.call-done = bf16[2048,512]{1,0:T(8,128)(2,1)} async-done(((bf16[256,512]{1,0:T(8,128)(2,1)}), bf16[2048,512]{1,0:T(8,128)(2,1)}) %all-gather.18.cloned.1.call-update) | async-done | bytes 2097168 | tf_op jit(solution)/shard_map/all_gather | solution.py:93
  217.8 429.4 %while.38 = (s32[]{:T(128)}, f32[4,128,128]{2,1,0:T(8,128)S(1)}, f32[16,4,64,128]{3,2,1,0:T(8,128)S(1)}, f32[16,4,128,128]{3,2,1,0:T(8,128)}, f32[16,4,64,128]{3...) while((s32[]{:T(128)}, f32[4,128,128]{2,1,0:T(8,128)S(1)}, ...), condition=%wide.region_3.5_spmd.clone, body=%wide.region_2.4_spmd.clone.sunk | while | flops 277483584 | bytes 4733562 | solution.py:67
  660.7 69.7 %reduce-scatter.15.cloned.1.call-done = f32[1024,512]{1,0:T(8,128)} async-done(((f32[1024,2048]{1,0:T(8,128)}), f32[1024,512]{1,0:T(8,128)}) %reduce-scatter.15.cloned.1.call-update) | async-done | bytes 2097168 | tf_op jit(solution)/shard_map/reduce_scatter | solution.py:88
  736.1 31.8 %all-gather.22.cloned.1.call-done = bf16[1024,2048]{1,0:T(8,128)(2,1)} async-done(((bf16[1024,512]{1,0:T(8,128)(2,1)}), bf16[1024,2048]{1,0:T(8,128)(2,1)}) %all-gather.22.cloned.1.call-update) | async-done | bytes 4194320 | tf_op jit(solution)/shard_map/all_gather | solution.py:84
  771.0 92.0 %all-gather.26.cloned.1.call-done = bf16[2048,1408]{1,0:T(8,128)(2,1)} async-done(((bf16[256,1408]{1,0:T(8,128)(2,1)}), bf16[2048,1408]{1,0:T(8,128)(2,1)}) %all-gather.26.cloned.1.call-update) | async-done | bytes 5767184 | tf_op jit(solution)/shard_map/all_gather | solution.py:98
  875.3 80.9 %all-gather.24.cloned.1.call-done = bf16[2048,1408]{1,0:T(8,128)(2,1)} async-done(((bf16[256,1408]{1,0:T(8,128)(2,1)}), bf16[2048,1408]{1,0:T(8,128)(2,1)}) %all-gather.24.cloned.1.call-update) | async-done | bytes 5767184 | tf_op jit(solution)/shard_map/all_gather | solution.py:97
  968.2 22.3 all-gather.30.cloned.1.call-done
  990.5 95.9 %all-gather.28.cloned.1.call-done = bf16[1408,2048]{1,0:T(8,128)(2,1)} async-done(((bf16[1408,256]{1,0:T(8,128)(2,1)}), bf16[1408,2048]{1,0:T(8,128)(2,1)}) %all-gather.28.cloned.1.call-update) | async-done | bytes 5767184 | tf_op jit(solution)/shard_map/all_gather | solution.py:100
  1146.6 51.1 %reduce-scatter.19.cloned.1.call-done = f32[1024,512]{1,0:T(8,128)} async-done(((f32[1024,2048]{1,0:T(8,128)}), f32[1024,512]{1,0:T(8,128)}) %reduce-scatter.19.cloned.1.call-update) | async-done | bytes 2097168 | tf_op jit(solution)/shard_map/reduce_scatter | solution.py:88
  1206.0 66.1 %reduce-scatter.17.cloned.1.call-done = f32[1024,512]{1,0:T(8,128)} async-done(((f32[1024,2048]{1,0:T(8,128)}), f32[1024,512]{1,0:T(8,128)}) %reduce-scatter.17.cloned.1.call-update) | async-done | bytes 2097168 | tf_op jit(solution)/shard_map/reduce_scatter | solution.py:88
  1332.8 633.9 %while.39 = (s32[]{:T(128)}, f32[4,128,128]{2,1,0:T(8,128)}, f32[16,4,64,128]{3,2,1,0:T(8,128)}, f32[16,4,64,128]{3,2,1,0:T(8,128)S(1)}, f32[16,4,64,128]{3,2,1,...) while((s32[]{:T(128)}, f32[4,128,128]{2,1,0:T(8,128)}, ...), condition=%wide.region_15.17_spmd.clone, body=%wide.region_12.16_spmd.clone.sunk | while | flops 718376768 | bytes 13362995 | solution.py:67
  1341.2 20.4 custom-call.28
  1380.9 20.4 custom-call.28
  1420.6 20.4 custom-call.28
  1460.2 20.4 custom-call.28
  1499.9 20.4 custom-call.28
  1539.6 20.4 custom-call.28
  1579.3 20.4 custom-call.28
  1619.0 20.4 custom-call.28
  1658.6 20.4 custom-call.28
  1698.3 20.4 custom-call.28
  1738.0 20.4 custom-call.28
  1777.6 20.4 custom-call.28
  2066.3 40.3 %all-reduce.29 = (f32[2048]{0:T(1024)}, f32[128]{0:T(128)}, f32[2048]{0:T(1024)}) all-reduce(f32[2048]{0:T(1024)S(1)} %get-tuple-element.525, f32[128]{0:T(128)S(1)} %bitcast_reduce_fusion, f32[2048]{0:T(1024)S(1)} %copy-done.84), channel_id=1, replica_groups=mesh['row'=8,'col'=4] {'row','col'}, use_global_device_ids=true, to_apply=%region_21.23 | all-reduce | flops 4224 | bytes 33792 | tf_op jit(solution)/shard_map/psum | solution.py:267
  2106.6 37.6 %all-reduce.30 = (f32[4,512]{1,0:T(4,128)}, f32[4,512]{1,0:T(4,128)}, f32[4,512]{1,0:T(4,128)}) all-reduce(f32[4,512]{1,0:T(4,128)S(1)} %pad_add_fusion.14, f32[4,512]{1,0:T(4,128)S(1)} %pad_add_fusion.13, f32[4,512]{1,0:T(4,128)S(1)} %pad_add_fusion.12), channel_id=1, replica_groups=mesh['row'=8,'col'=4] {'row'}, use_global_device_ids=true, to_apply=%region_29.31 | all-reduce | flops 6144 | bytes 49152 | tf_op jit(solution)/shard_map/psum | solution.py:268
  2147.6 41.1 %reduce-scatter.23.cloned.1.call-done = bf16[256,512]{1,0:T(8,128)(2,1)} async-done(((bf16[2048,512]{1,0:T(8,128)(2,1)}), bf16[256,512]{1,0:T(8,128)(2,1)}) %reduce-scatter.23.cloned.1.call-update) | async-done | bytes 262160 | tf_op jit(solution)/shard_map/reduce_scatter | solution.py:242
  2190.5 69.0 %reduce-scatter.29.cloned.1.call-done = bf16[512,256]{1,0:T(8,128)(2,1)} async-done(((bf16[512,2048]{1,0:T(8,128)(2,1)}), bf16[512,256]{1,0:T(8,128)(2,1)}) %reduce-scatter.29.cloned.1.call-update) | async-done | bytes 262160 | tf_op jit(solution)/shard_map/reduce_scatter | solution.py:260
  2261.3 68.4 %reduce-scatter.27.cloned.1.call-done = bf16[256,512]{1,0:T(8,128)(2,1)} async-done(((bf16[2048,512]{1,0:T(8,128)(2,1)}), bf16[256,512]{1,0:T(8,128)(2,1)}) %reduce-scatter.27.cloned.1.call-update) | async-done | bytes 262160 | tf_op jit(solution)/shard_map/reduce_scatter | solution.py:248
  2331.5 71.6 %reduce-scatter.21.cloned.1.call-done = f32[1024,512]{1,0:T(8,128)} async-done(((f32[1024,2048]{1,0:T(8,128)}), f32[1024,512]{1,0:T(8,128)}) %reduce-scatter.21.cloned.1.call-update) | async-done | bytes 2097168 | tf_op jit(solution)/shard_map/reduce_scatter | solution.py:88
  (1250 shorter events, 1172.3 us)
Async XLA Ops:
  7.2 39.6 %all-gather.12.cloned.1.call-start = ((), (), s32[]{:S(2)}) async-start(), calls=%async_computation.12 | async-start | bytes 5242880 | tf_op jit(solution)/shard_map/all_gather | solution.py:84
  8.0 90.3 %all-gather.14.cloned.1.call-start = ((), (), s32[]{:S(2)}) async-start(), calls=%async_computation.13 | async-start | bytes 2359296 | tf_op jit(solution)/shard_map/all_gather | solution.py:94
  8.7 139.5 %all-gather.16.cloned.1.call-start = ((), (), s32[]{:S(2)}) async-start(), calls=%async_computation.14 | async-start | bytes 2359296 | tf_op jit(solution)/shard_map/all_gather | solution.py:95
  9.5 188.6 %all-gather.18.cloned.1.call-start = ((), (), s32[]{:S(2)}) async-start(), calls=%async_computation.15 | async-start | bytes 2359296 | tf_op jit(solution)/shard_map/all_gather | solution.py:93
  10.0 642.2 %all-gather.20.cloned.1.call-start = ((), (), s32[]{:S(2)}) async-start(), calls=%async_computation.16 | async-start | bytes 2359296 | tf_op jit(solution)/shard_map/all_gather | solution.py:99
  10.6 719.7 %reduce-scatter.15.cloned.1.call-start = ((), (), s32[]{:S(2)}) async-start(), calls=%async_computation.17 | async-start | bytes 10485760 | tf_op jit(solution)/shard_map/reduce_scatter | solution.py:88
  10.8 142.7 %copy-start.55 = (f32[1,512]{1,0:T(1,128)}, f32[1,512]{1,0:T(1,128)S(1)}, u32[]{:S(2)}) copy-start(f32[1,512]{1,0:T(1,128)S(1)} %get-tuple-element.512) | copy-start | bytes 6148
  10.8 142.7 %copy-start.57 = (f32[1,512]{1,0:T(1,128)}, f32[1,512]{1,0:T(1,128)S(1)}, u32[]{:S(2)}) copy-start(f32[1,512]{1,0:T(1,128)S(1)} %get-tuple-element.513) | copy-start | bytes 6148
  10.8 142.7 %copy-start.59 = (f32[1,512]{1,0:T(1,128)}, f32[1,512]{1,0:T(1,128)S(1)}, u32[]{:S(2)}) copy-start(f32[1,512]{1,0:T(1,128)S(1)} %get-tuple-element.514) | copy-start | bytes 6148
  10.8 142.7 %copy-start.61 = (f32[1,512]{1,0:T(1,128)}, f32[1,512]{1,0:T(1,128)S(1)}, u32[]{:S(2)}) copy-start(f32[1,512]{1,0:T(1,128)S(1)} %get-tuple-element.515) | copy-start | bytes 6148
  10.9 192.4 %copy-start.63 = (f32[1,512]{1,0:T(1,128)}, f32[1,512]{1,0:T(1,128)S(1)}, u32[]{:S(2)}) copy-start(f32[1,512]{1,0:T(1,128)S(1)} %get-tuple-element.508) | copy-start | bytes 6148
  10.9 192.4 %copy-start.65 = (f32[1,512]{1,0:T(1,128)}, f32[1,512]{1,0:T(1,128)S(1)}, u32[]{:S(2)}) copy-start(f32[1,512]{1,0:T(1,128)S(1)} %get-tuple-element.509) | copy-start | bytes 6148
  10.9 192.4 %copy-start.67 = (f32[1,512]{1,0:T(1,128)}, f32[1,512]{1,0:T(1,128)S(1)}, u32[]{:S(2)}) copy-start(f32[1,512]{1,0:T(1,128)S(1)} %get-tuple-element.510) | copy-start | bytes 6148
  10.9 192.4 %copy-start.69 = (f32[1,512]{1,0:T(1,128)}, f32[1,512]{1,0:T(1,128)S(1)}, u32[]{:S(2)}) copy-start(f32[1,512]{1,0:T(1,128)S(1)} %get-tuple-element.511) | copy-start | bytes 6148
  38.7 168.9 %copy-start.46 = (bf16[2048,4]{0,1:T(4,128)(2,1)}, bf16[2048,4]{0,1:T(4,128)(2,1)S(1)}, u32[]{:S(2)}) copy-start(bf16[2048,4]{0,1:T(4,128)(2,1)S(1)} %all_gather.38) | copy-start | bytes 49156
  659.9 108.0 %all-gather.22.cloned.1.call-start = ((), (), s32[]{:S(2)}) async-start(), calls=%async_computation.18 | async-start | bytes 5242880 | tf_op jit(solution)/shard_map/all_gather | solution.py:84
  733.3 129.7 %all-gather.26.cloned.1.call-start = ((), (), s32[]{:S(2)}) async-start(), calls=%async_computation.20 | async-start | bytes 6488064 | tf_op jit(solution)/shard_map/all_gather | solution.py:98
  734.0 222.3 %all-gather.24.cloned.1.call-start = ((), (), s32[]{:S(2)}) async-start(), calls=%async_computation.19 | async-start | bytes 6488064 | tf_op jit(solution)/shard_map/all_gather | solution.py:97
  734.7 255.7 %all-gather.30.cloned.1.call-start = ((), (), s32[]{:S(2)}) async-start(), calls=%async_computation.23 | async-start | bytes 5242880 | tf_op jit(solution)/shard_map/all_gather | solution.py:84
  735.3 351.0 %all-gather.28.cloned.1.call-start = ((), (), s32[]{:S(2)}) async-start(), calls=%async_computation.21 | async-start | bytes 6488064 | tf_op jit(solution)/shard_map/all_gather | solution.py:100
  736.1 461.6 %reduce-scatter.19.cloned.1.call-start = ((), (), s32[]{:S(2)}) async-start(), calls=%async_computation.24 | async-start | bytes 10485760 | tf_op jit(solution)/shard_map/reduce_scatter | solution.py:88
  1127.6 144.5 %reduce-scatter.17.cloned.1.call-start = ((), (), s32[]{:S(2)}) async-start(), calls=%async_computation.22 | async-start | bytes 10485760 | tf_op jit(solution)/shard_map/reduce_scatter | solution.py:88
  1139.6 173.8 %all-gather.32.cloned.1.call-start = ((), (), s32[]{:S(2)}) async-start(), calls=%async_computation.25 | async-start | bytes 5242880 | tf_op jit(solution)/shard_map/all_gather | solution.py:84
  1277.8 781.5 %reduce-scatter.31.cloned.1.call-start = ((), (), s32[]{:S(2)}) async-start(), calls=%async_computation.31 | async-start | bytes 6488064 | tf_op jit(solution)/shard_map/reduce_scatter | solution.py:254
  1289.3 772.4 %reduce-scatter.33.cloned.1.call-start = ((), (), s32[]{:S(2)}) async-start(), calls=%async_computation.32 | async-start | bytes 6488064 | tf_op jit(solution)/shard_map/reduce_scatter | solution.py:257
  1301.0 763.0 %reduce-scatter.35.cloned.1.call-start = ((), (), s32[]{:S(2)}) async-start(), calls=%async_computation.33 | async-start | bytes 6488064 | tf_op jit(solution)/shard_map/reduce_scatter | solution.py:263
  1313.4 830.8 %reduce-scatter.37.cloned.1.call-start = ((), (), s32[]{:S(2)}) async-start(), calls=%async_computation.34 | async-start | bytes 589824
  1984.8 160.9 %reduce-scatter.25.cloned.1.call-start = ((), (), s32[]{:S(2)}) async-start(), calls=%async_computation.28 | async-start | bytes 2359296 | tf_op jit(solution)/shard_map/reduce_scatter | solution.py:245
  1992.8 195.9 %reduce-scatter.23.cloned.1.call-start = ((), (), s32[]{:S(2)}) async-start(), calls=%async_computation.27 | async-start | bytes 2359296 | tf_op jit(solution)/shard_map/reduce_scatter | solution.py:242
  2006.4 253.2 %reduce-scatter.29.cloned.1.call-start = ((), (), s32[]{:S(2)}) async-start(), calls=%async_computation.30 | async-start | bytes 2359296 | tf_op jit(solution)/shard_map/reduce_scatter | solution.py:260
  2013.5 316.2 %reduce-scatter.27.cloned.1.call-start = ((), (), s32[]{:S(2)}) async-start(), calls=%async_computation.29 | async-start | bytes 2359296 | tf_op jit(solution)/shard_map/reduce_scatter | solution.py:248
  2026.7 376.3 %reduce-scatter.21.cloned.1.call-start = ((), (), s32[]{:S(2)}) async-start(), calls=%async_computation.26 | async-start | bytes 10485760 | tf_op jit(solution)/shard_map/reduce_scatter | solution.py:88
  (144 other events, 1122.2 us)
Sparse Core Ops, SparseCore 0:
  9.6 37.1 all-gather.11
  49.0 49.2 all-gather.13
  100.4 47.7 all-gather.15
  150.2 47.7 all-gather.17
  199.9 50.3 all-gather.19
  660.0 70.3 reduce-scatter.14
  733.4 34.4 all-gather.21
  770.3 92.6 all-gather.25
  865.4 90.8 all-gather.23
  957.8 32.6 all-gather.29
  992.7 93.5 all-gather.27
  1127.7 69.9 reduce-scatter.18
  1200.3 71.7 reduce-scatter.16
  1277.9 34.6 all-gather.31
  1316.6 109.9 reduce-scatter.30
  1430.5 110.6 reduce-scatter.32
  1545.1 109.5 reduce-scatter.34
  1984.9 62.4 reduce-scatter.36
  2050.9 66.9 reduce-scatter.24
  2121.9 66.7 reduce-scatter.22
  2192.2 67.2 reduce-scatter.28
  2263.1 66.5 reduce-scatter.26
  2332.3 70.7 reduce-scatter.20
where the time goes:
time: 2430 us; the launch traced here: 2420 us
  waiting for transfers between devices  892 us (37%)
  other arithmetic  785 us (32%)
  matrix products  418 us (17%)
  local copies, waits for them, and re-layouts  187 us (8%)
  blocking collectives  117 us (5%)
    another operation x112, other arithmetic, delta_block(): lax.linalg.triangular_solve(system, right_side, left_side=True, lower=Tru...  656 us
    reduce_scatter x4, waiting for transfers between devices, sum_features(): lax.psum_scatter(partial_value, 'col', scatter_dimension=1, tiled=True)  258 us
    dot_general x24, matrix products, product(): return jnp.einsum(form, left, right, preferred_element_type=jnp.float32)  190 us
    all_gather x1, waiting for transfers between devices, fetch_weights(): lax.all_gather(shards[7], 'row', axis=1, tiled=True)  95.9 us
    all_gather x1, waiting for transfers between devices, fetch_weights(): lax.all_gather(shards[5], 'row', axis=0, tiled=True)  92 us
    squeeze x80, local copies, waits for them, and re-layouts, delta_mixer(): lax.scan(jax.checkpoint(delta_block), start_state, blocks)  84.6 us
    all_gather x1, waiting for transfers between devices, fetch_weights(): lax.all_gather(shards[4], 'row', axis=0, tiled=True)  80.9 us
    reduce_scatter x1, waiting for transfers between devices, per_device(): lax.psum_scatter(grad_out.astype(jnp.bfloat16), 'row', scatter_dimension=...  69 us
  transfers between devices with their start and end apart: 23, of which 16 were waited for; matrix products, arithmetic and copies ran while one was open for 53% of the time, Pallas kernels for 0%

commit v1 on v0

v1 whole, which is shorter than its diff:
```python
import functools
import jax
import jax.numpy as jnp
from jax import lax
from jax.experimental import pallas as pl
from jax.experimental.pallas import tpu as pltpu
from jax.sharding import PartitionSpec as P

CHUNK = 128
EPS = 1e-6
bf16 = jnp.bfloat16
f32 = jnp.float32


def split(x):
    high = x.astype(bf16)
    return high, (x - high.astype(f32)).astype(bf16)


def mm(a, b, ca=1, cb=0):
    def dg(u, v):
        return lax.dot_general(u, v, (((ca,), (cb,)), ((), ())), preferred_element_type=f32)

    return dg(a[0], b[0]) + (dg(a[0], b[1]) + dg(a[1], b[0]))


def sigmoid(x):
    return 1.0 / (1.0 + jnp.exp(-x))


def masks(n):
    r = lax.broadcasted_iota(jnp.int32, (n, n), 0)
    c = lax.broadcasted_iota(jnp.int32, (n, n), 1)
    return r, c


def unit_lower_inverse(lows, r, c):
    n = lows[0].shape[0]
    eye = jnp.where(r == c, 1.0, 0.0)
    invs = [eye - jnp.where(r // 2 == c // 2, low, 0.0) for low in lows]
    size = 2
    while size < n:
        mask = (r // (2 * size) == c // (2 * size)) & (r // size != c // size)
        offs = [split(jnp.where(mask, low, 0.0)) for low in lows]
        parts = [split(inv) for inv in invs]
        right = [split(mm(off, part)) for off, part in zip(offs, parts)]
        invs = [inv - mm(part, x) for inv, part, x in zip(invs, parts, right)]
        size *= 2
    return invs


def conv_rows(padded, taps, first):
    out = taps[0:1] * padded[first : first + CHUNK]
    for j in range(1, 4):
        out = out + taps[j : j + 1] * padded[first + j : first + j + CHUNK]
    return out


def fwd_kernel(heads, dh, x_ref, conv_ref, gain_ref, mixed_ref, o_ref, n_ref, t_ref, s_ref, state, halo):
    hd = heads * dh

    @pl.when(pl.program_id(0) == 0)
    def _():
        state[...] = jnp.zeros_like(state)
        halo[...] = jnp.zeros_like(halo)

    r, c = masks(CHUNK)
    each = range(heads)
    acts = []
    for p in range(3):
        for h in each:
            cols = slice(p * hd + h * dh, p * hd + (h + 1) * dh)
            y = conv_rows(jnp.concatenate([halo[:, cols], x_ref[:, cols]], 0), conv_ref[:, cols], 5)
            acts.append(y * sigmoid(y))
    qs = [split(acts[h] * dh ** -0.5) for h in each]
    ks = []
    for h in each:
        k = acts[heads + h]
        ks.append(split(k * lax.rsqrt(jnp.sum(k * k, axis=1, keepdims=True) + EPS)))
    b = [sigmoid(x_ref[:, 3 * hd + h : 3 * hd + h + 1]) for h in each]
    lows = [jnp.where(r > c, b[h] * mm(ks[h], ks[h], 1, 1), 0.0) for h in each]
    invs = unit_lower_inverse(lows, r, c)
    scores = [split(jnp.where(r >= c, mm(qs[h], ks[h], 1, 1), 0.0)) for h in each]
    s = [state[h] for h in each]
    ss = [split(s[h]) for h in each]
    right = [split(b[h] * (acts[2 * heads + h] - mm(ks[h], ss[h]))) for h in each]
    fresh = [mm(split(invs[h]), right[h]) for h in each]
    fs = [split(fresh[h]) for h in each]
    outs = [mm(qs[h], ss[h]) + mm(scores[h], fs[h]) for h in each]
    for h in each:
        state[h] = s[h] + mm(ks[h], fs[h], 0, 0)
        cols = slice(h * dh, (h + 1) * dh)
        s_ref[0, h] = s[h]
        t_ref[0, h] = invs[h]
        n_ref[:, cols] = fresh[h]
        o = outs[h]
        o_ref[:, cols] = o
        norm = lax.rsqrt(jnp.mean(o * o, axis=1, keepdims=True) + EPS)
        mixed_ref[:, cols] = (o * norm * gain_ref[...]).astype(bf16)
    halo[...] = x_ref[CHUNK - 8 :, : 3 * hd]


def bwd_kernel(heads, dh, x_ref, prev_ref, conv_ref, gain_ref, m_ref, o_ref, n_ref, t_ref, s_ref,
               low_ref, gconv_ref, ggain_ref, inner_ref, dstate, ghead):
    hd = heads * dh
    step = pl.program_id(0)

    @pl.when(step == 0)
    def _():
        dstate[...] = jnp.zeros_like(dstate)
        ghead[...] = jnp.zeros_like(ghead)
        gconv_ref[...] = jnp.zeros_like(gconv_ref)
        ggain_ref[...] = jnp.zeros_like(ggain_ref)

    has_prev = jnp.where(step == pl.num_programs(0) - 1, 0.0, 1.0)
    r, c = masks(CHUNK)
    lane = lax.broadcasted_iota(jnp.int32, (CHUNK, 128), 1)
    each = range(heads)
    scale = dh ** -0.5
    cuts = [slice(h * dh, (h + 1) * dh) for h in each]
    ys, sigs = [], []
    for p in range(3):
        for h in each:
            cols = slice(p * hd + h * dh, p * hd + (h + 1) * dh)
            padded = jnp.concatenate([prev_ref[:, cols] * has_prev, x_ref[:, cols]], 0)
            y = conv_rows(padded, conv_ref[:, cols], 5)
            ys.append(y)
            sigs.append(sigmoid(y))
    qs = [split(ys[h] * sigs[h] * scale) for h in each]
    kr = [ys[heads + h] * sigs[heads + h] for h in each]
    kinv = [lax.rsqrt(jnp.sum(kr[h] * kr[h], axis=1, keepdims=True) + EPS) for h in each]
    ks = [split(kr[h] * kinv[h]) for h in each]
    b = [sigmoid(x_ref[:, 3 * hd + h : 3 * hd + h + 1]) for h in each]
    dos = []
    ggain = jnp.zeros((1, dh), f32)
    for h in each:
        o = o_ref[:, cuts[h]]
        mc = m_ref[:, cuts[h]]
        norm = lax.rsqrt(jnp.mean(o * o, axis=1, keepdims=True) + EPS)
        ggain = ggain + jnp.sum(mc * (o * norm), axis=0, keepdims=True)
        dn_ = mc * gain_ref[...]
        do = norm * dn_ - o * (norm * norm * norm * jnp.mean(dn_ * o, axis=1, keepdims=True))
        dos.append(split(do))
    scores = [split(jnp.where(r >= c, mm(qs[h], ks[h], 1, 1), 0.0)) for h in each]
    part = [mm(scores[h], dos[h], 0, 0) for h in each]
    d = [dstate[h] for h in each]
    ds = [split(d[h]) for h in each]
    dfresh = [split(part[h] + mm(ks[h], ds[h])) for h in each]
    db_ = [mm(split(t_ref[0, h]), dfresh[h], 0, 0) for h in each]
    dr = [b[h] * db_[h] for h in each]
    drs = [split(dr[h]) for h in each]
    for h in each:
        dstate[h] = d[h] + (mm(qs[h], dos[h], 0, 0) - mm(ks[h], drs[h], 0, 0))
    ss = [split(s_ref[0, h]) for h in each]
    fs = [split(n_ref[:, cuts[h]]) for h in each]
    resid = [ys[2 * heads + h] * sigs[2 * heads + h] - mm(ks[h], ss[h]) for h in each]
    gram = [mm(ks[h], ks[h], 1, 1) for h in each]
    da = [jnp.where(r > c, -mm(split(db_[h]), fs[h], 1, 1), 0.0) for h in each]
    dsc = [split(jnp.where(r >= c, mm(dos[h], fs[h], 1, 1), 0.0)) for h in each]
    dq = [mm(dos[h], ss[h], 1, 1) + mm(dsc[h], ks[h]) for h in each]
    dgs = [split(b[h] * da[h]) for h in each]
    dk = [mm(dsc[h], qs[h], 0, 0) + mm(fs[h], ds[h], 1, 1) for h in each]
    dk = [dk[h] - mm(drs[h], ss[h], 1, 1) for h in each]
    dk = [dk[h] + (mm(dgs[h], ks[h]) + mm(dgs[h], ks[h], 0, 0)) for h in each]
    beta_low = jnp.zeros((CHUNK, 128), f32)
    inner = jnp.zeros((CHUNK, dh), f32)
    for h in each:
        dbeta = jnp.sum(db_[h] * resid[h], axis=1, keepdims=True) + jnp.sum(da[h] * gram[h], axis=1, keepdims=True)
        beta_low = jnp.where(lane == h, dbeta * b[h] * (1.0 - b[h]), beta_low)
    dkr = [kinv[h] * dk[h] - kr[h] * (kinv[h] * kinv[h] * kinv[h] * jnp.sum(dk[h] * kr[h], axis=1, keepdims=True)) for h in each]
    cots = [dq[h] * scale for h in each] + dkr + dr
    for p in range(3):
        for h in each:
            i = p * heads + h
            cols = slice(p * hd + h * dh, p * hd + (h + 1) * dh)
            g = cots[i] * sigs[i] * (1.0 + ys[i] * (1.0 - sigs[i]))
            taps = conv_ref[:, cols]
            gp = jnp.concatenate([g, ghead[:, cols]], 0)
            padded = jnp.concatenate([prev_ref[:, cols] * has_prev, x_ref[:, cols]], 0)
            out = taps[3:4] * g
            for j in range(3):
                out = out + taps[j : j + 1] * gp[3 - j : 3 - j + CHUNK]
            low_ref[:, cols] = out.astype(bf16)
            inner = inner + out * x_ref[:, cols]
            for j in range(4):
                gconv_ref[j : j + 1, cols] += jnp.sum(g * padded[5 + j : 5 + j + CHUNK], axis=0, keepdims=True)
            ghead[:, cols] = g[0:8]
    low_ref[:, 3 * hd :] = beta_low.astype(bf16)
    inner = inner + beta_low * x_ref[:, 3 * hd :]
    inner_ref[...] = jnp.sum(inner, axis=1, keepdims=True)
    ggain_ref[...] += ggain


def mixer_forward(proj, conv, gain, heads, dh):
    rows, width = proj.shape
    hd = heads * dh
    steps = rows // CHUNK
    square = pl.BlockSpec((1, heads, dh, dh), lambda i: (i, 0, 0, 0))
    wide = pl.BlockSpec((CHUNK, hd), lambda i: (i, 0))
    flops = rows * heads * (20 * 3 * 2 * 128 * 128)
    return pl.pallas_call(
        functools.partial(fwd_kernel, heads, dh),
        grid=(steps,),
        in_specs=[
            pl.BlockSpec((CHUNK, width), lambda i: (i, 0)),
            pl.BlockSpec((4, 3 * hd), lambda i: (0, 0)),
            pl.BlockSpec((1, dh), lambda i: (0, 0)),
        ],
        out_specs=[wide, wide, wide, pl.BlockSpec((1, heads, CHUNK, CHUNK), lambda i: (i, 0, 0, 0)), square],
        out_shape=[
            jax.ShapeDtypeStruct((rows, hd), bf16),
            jax.ShapeDtypeStruct((rows, hd), f32),
            jax.ShapeDtypeStruct((rows, hd), f32),
            jax.ShapeDtypeStruct((steps, heads, CHUNK, CHUNK), f32),
            jax.ShapeDtypeStruct((steps, heads, dh, dh), f32),
        ],
        scratch_shapes=[pltpu.VMEM((heads, dh, dh), f32), pltpu.VMEM((8, 3 * hd), f32)],
        compiler_params=pltpu.CompilerParams(vmem_limit_bytes=40 * 2**20),
        cost_estimate=pl.CostEstimate(flops=flops, bytes_accessed=rows * (width * 4 + hd * 18), transcendentals=0),
        name="mixer_forward",
    )(proj, conv, gain)


def mixer_backward(proj, conv, gain, mixed_cot, kept, heads, dh):
    o, fresh, inv, states = kept
    rows, width = proj.shape
    hd = heads * dh
    steps = rows // CHUNK
    last = steps - 1
    per = CHUNK // 8
    square = pl.BlockSpec((1, heads, dh, dh), lambda i: (last - i, 0, 0, 0))
    wide = pl.BlockSpec((CHUNK, hd), lambda i: (last - i, 0))
    flops = rows * heads * (15 * 3 * 2 * 128 * 128)
    return pl.pallas_call(
        functools.partial(bwd_kernel, heads, dh),
        grid=(steps,),
        in_specs=[
            pl.BlockSpec((CHUNK, width), lambda i: (last - i, 0)),
            pl.BlockSpec((8, width), lambda i: (jnp.maximum((last - i) * per - 1, 0), 0)),
            pl.BlockSpec((4, 3 * hd), lambda i: (0, 0)),
            pl.BlockSpec((1, dh), lambda i: (0, 0)),
            wide, wide, wide,
            pl.BlockSpec((1, heads, CHUNK, CHUNK), lambda i: (last - i, 0, 0, 0)),
            square,
        ],
        out_specs=[
            pl.BlockSpec((CHUNK, width), lambda i: (last - i, 0)),
            pl.BlockSpec((4, 3 * hd), lambda i: (0, 0)),
            pl.BlockSpec((1, dh), lambda i: (0, 0)),
            pl.BlockSpec((CHUNK, 1), lambda i: (last - i, 0)),
        ],
        out_shape=[
            jax.ShapeDtypeStruct((rows, width), bf16),
            jax.ShapeDtypeStruct((4, 3 * hd), f32),
            jax.ShapeDtypeStruct((1, dh), f32),
            jax.ShapeDtypeStruct((rows, 1), f32),
        ],
        scratch_shapes=[pltpu.VMEM((heads, dh, dh), f32), pltpu.VMEM((8, 3 * hd), f32)],
        compiler_params=pltpu.CompilerParams(vmem_limit_bytes=40 * 2**20),
        cost_estimate=pl.CostEstimate(flops=flops, bytes_accessed=rows * (width * 6 + hd * 18), transcendentals=0),
        name="mixer_backward",
    )(proj, proj, conv, gain, mixed_cot, o, fresh, inv, states)


def live_column(length, rows):
    return (lax.broadcasted_iota(jnp.int32, (rows, 1), 0) < length).astype(f32)


def swap(x, axis, bit):
    n = lax.axis_size(axis)
    return lax.ppermute(x, axis, [(i, i ^ bit) for i in range(n)])


def bits_down(n):
    bits = []
    while n > 1:
        n //= 2
        bits.append(n)
    return bits


def sum_all(x, axis):
    for bit in bits_down(lax.axis_size(axis)):
        x = x + swap(x, axis, bit)
    return x


def spread_cols(shard):
    n = lax.axis_size("col")
    pieces = {0: shard}
    for bit in bits_down(n):
        for j in list(pieces):
            pieces[j | bit] = swap(pieces[j], "col", bit)
    return [pieces[j] for j in range(n)]


def sum_cols(piece):
    n = lax.axis_size("col")
    away = {}
    bit = 1
    kept = list(range(n))
    got = {}
    while bit < n:
        for j in [j for j in kept if j & bit]:
            mine = piece(j) + got[j] if j in got else piece(j)
            got_j = swap(mine.astype(bf16), "col", bit).astype(f32)
            base = j ^ bit
            got[base] = got[base] + got_j if base in got else got_j
        kept = [j for j in kept if not j & bit]
        bit *= 2
    return piece(0) + got[0]


def norm_kernel(width, me_ref, *refs):
    pieces, (gain_ref, normed_ref, factor_ref) = refs[:-3], refs[-3:]
    total = len(pieces) * width
    values = [p[...].astype(f32) for p in pieces]
    square = values[0] * values[0]
    for v in values[1:]:
        square = square + v * v
    factor = lax.rsqrt(jnp.sum(square, axis=1, keepdims=True) / total + EPS)
    factor_ref[...] = factor
    for j, v in enumerate(values):
        cols = pl.ds(pl.multiple_of((me_ref[0] ^ j) * width, width), width)
        normed_ref[:, cols] = (v * factor * gain_ref[:, cols]).astype(bf16)


def join_kernel(width, me_ref, *refs):
    pieces, out_ref = refs[:-1], refs[-1]
    for j, p in enumerate(pieces):
        out_ref[:, pl.ds(pl.multiple_of((me_ref[0] ^ j) * width, width), width)] = p[...]


TILE = 256


def join_call(kernel, pieces, extra, outs, name):
    rows, width = pieces[0].shape
    me = lax.axis_index("col").astype(jnp.int32).reshape(1)
    return pl.pallas_call(
        functools.partial(kernel, width),
        grid_spec=pltpu.PrefetchScalarGridSpec(
            num_scalar_prefetch=1,
            grid=(rows // TILE,),
            in_specs=[pl.BlockSpec((TILE, width), lambda i, m: (i, 0))] * len(pieces)
            + [pl.BlockSpec(e.shape, lambda i, m: (0, 0)) for e in extra],
            out_specs=[pl.BlockSpec((TILE, o.shape[1]), lambda i, m: (i, 0)) for o in outs],
        ),
        out_shape=outs,
        compiler_params=pltpu.CompilerParams(vmem_limit_bytes=24 * 2**20),
        cost_estimate=pl.CostEstimate(flops=rows * width * 16, bytes_accessed=rows * width * len(pieces) * 4, transcendentals=0),
        name=name,
    )(me, *pieces, *extra)


def join_norm(pieces, gain):
    rows, width = pieces[0].shape
    outs = [jax.ShapeDtypeStruct((rows, width * len(pieces)), bf16), jax.ShapeDtypeStruct((rows, 1), f32)]
    return join_call(norm_kernel, pieces, [gain.reshape(1, -1)], outs, "join_norm")


def join(pieces):
    rows, width = pieces[0].shape
    return join_call(join_kernel, pieces, [], [jax.ShapeDtypeStruct((rows, width * len(pieces)), bf16)], "join")[0]


def dot(a, b, ca=1, cb=0):
    return lax.dot_general(a, b, (((ca,), (cb,)), ((), ())), preferred_element_type=f32)


def gather_rows(shard):
    return lax.all_gather(shard, "row", axis=0, tiled=True)


def scatter_rows(grad):
    return lax.psum_scatter(grad.astype(bf16), "row", scatter_dimension=0, tiled=True)


def per_device(tokens, lengths, norm_in, q_weight, k_weight, v_weight, conv_q, conv_k, conv_v, beta_weight,
               head_gain, out_weight, norm_mid, gate_weight, up_weight, down_weight, cotangent):
    rows, width = tokens.shape
    dh = head_gain.shape[0]
    hd = q_weight.shape[1]
    heads = hd // dh
    ff = gate_weight.shape[1]
    col = lax.axis_index("col")
    feat = lax.axis_size("col") * width
    live = live_column(lengths[0], rows)
    live_low = live.astype(bf16)
    beta_pad = jnp.pad(beta_weight, ((0, 0), (0, 128 - beta_weight.shape[1])))
    w_in = gather_rows(jnp.concatenate([q_weight, k_weight, v_weight, beta_pad], 1))
    w_out = gather_rows(out_weight.T)
    w_ff = gather_rows(jnp.concatenate([gate_weight, up_weight], 1))
    w_down = gather_rows(down_weight.T)
    conv = jnp.concatenate([conv_q, conv_k, conv_v], 1)
    gain = head_gain.reshape(1, dh)
    gain_in = lax.dynamic_slice_in_dim(norm_in, col * width, width)
    gain_mid = lax.dynamic_slice_in_dim(norm_mid, col * width, width)
    tokens32 = tokens.astype(f32)

    def block(w, j):
        return lax.dynamic_slice_in_dim(w, (col ^ j) * width, width, 0)

    normed, factor_in = join_norm(spread_cols(tokens), norm_in)
    ffn_cot = join(spread_cols(cotangent * live_low))
    proj = dot(normed, w_in)
    mixed, *kept = mixer_forward(proj, conv, gain, heads, dh)
    branch = sum_cols(lambda j: dot(mixed, block(w_out, j), 1, 1))
    middle = tokens32 + live * branch
    mid_low = middle.astype(bf16)
    normed_mid, factor_mid = join_norm(spread_cols(mid_low), norm_mid)
    gate = dot(normed_mid, w_ff[:, :ff])
    up = dot(normed_mid, w_ff[:, ff:])
    gate_sig = jax.nn.sigmoid(gate)
    hidden = (gate * gate_sig * up).astype(bf16)
    grad_down = scatter_rows(dot(ffn_cot, hidden, 0, 0))
    hidden_cot = dot(ffn_cot, w_down)
    gate_cot = (hidden_cot * up * gate_sig * (1.0 + gate * (1.0 - gate_sig))).astype(bf16)
    up_cot = (hidden_cot * gate * gate_sig).astype(bf16)
    grad_gate = scatter_rows(dot(normed_mid, gate_cot, 0, 0))
    grad_up = scatter_rows(dot(normed_mid, up_cot, 0, 0))
    inner_mid = jnp.sum(gate_cot.astype(f32) * gate + up_cot.astype(f32) * up, axis=1, keepdims=True)
    inner_mid = sum_all(inner_mid.reshape(rows // 128, 128), "col").reshape(rows, 1) / factor_mid
    both_cot = jnp.concatenate([gate_cot, up_cot], 1)
    mid_cot = sum_cols(lambda j: dot(both_cot, block(w_ff, j), 1, 1))
    result = sum_cols(lambda j: dot(hidden, block(w_down, j), 1, 1))
    layer_out = (middle + live * result).astype(bf16)

    mid32 = mid_low.astype(f32)
    gmid_part = jnp.sum(mid_cot * mid32 * factor_mid, axis=0)
    middle_cot = cotangent.astype(f32) + factor_mid * gain_mid * mid_cot - mid32 * (factor_mid**3 * inner_mid / feat)
    branch_cot = join(spread_cols((live * middle_cot).astype(bf16)))
    mixed_cot = dot(branch_cot, w_out)
    grad_out = scatter_rows(dot(branch_cot, mixed, 0, 0))
    low, gconv, ghead, inner_in = mixer_backward(proj, conv, gain, mixed_cot, kept, heads, dh)
    grad_in = scatter_rows(dot(normed, low, 0, 0))
    inner_in = sum_all(inner_in.reshape(rows // 128, 128), "col").reshape(rows, 1) / factor_in
    in_cot = sum_cols(lambda j: dot(low, block(w_in, j), 1, 1))
    gin_part = jnp.sum(in_cot * tokens32 * factor_in, axis=0)
    grad_tokens = middle_cot + factor_in * gain_in * in_cot - tokens32 * (factor_in**3 * inner_in / feat)

    def own_cols(part):
        return lax.dynamic_update_slice_in_dim(jnp.zeros((feat,), f32), part, col * width, 0)

    sizes = [feat, feat, dh]
    wide = sum_all(jnp.concatenate([own_cols(gin_part), own_cols(gmid_part), ghead[0]]).reshape(-1, 128), "col")
    small = sum_all(jnp.concatenate([wide, gconv.reshape(-1, 128)], 0), "row")
    wide, gconv = small[: wide.shape[0]].reshape(-1), small[wide.shape[0] :].reshape(gconv.shape)
    g_in = grad_in.astype(f32)
    return (
        layer_out,
        grad_tokens,
        wide[:feat],
        g_in[:, :hd],
        g_in[:, hd : 2 * hd],
        g_in[:, 2 * hd : 3 * hd],
        gconv[:, :hd],
        gconv[:, hd : 2 * hd],
        gconv[:, 2 * hd :],
        g_in[:, 3 * hd : 3 * hd + beta_weight.shape[1]],
        wide[2 * feat :],
        grad_out.astype(f32).T,
        wide[feat : 2 * feat],
        grad_gate.astype(f32),
        grad_up.astype(f32),
        grad_down.astype(f32).T,
    )


def solution(mesh):
    split_both, features, turned = P("row", "col"), P(None, "col"), P("col", "row")
    return jax.shard_map(
        per_device,
        mesh=mesh,
        in_specs=(split_both, P("row"), P(), split_both, split_both, split_both, features, features, features,
                  split_both, P(), turned, P(), split_both, split_both, turned, split_both),
        out_specs=(split_both, split_both, P(), split_both, split_both, split_both, features, features, features,
                   split_both, P(), turned, P(), split_both, split_both, turned),
        check_vma=False,
    )
```

time: 2430 us -> 1090 us (0.45)
  other arithmetic: 785 us -> 23.1 us
  matrix products: 418 us -> 170 us
  local copies, waits for them, and re-layouts: 187 us -> 31.3 us
  waiting for transfers between devices: 892 us -> 744 us
  blocking collectives: 117 us -> 0 us
  Pallas kernels: 0 us -> 79.7 us
    another operation x131 -> x0, other arithmetic: 677 us -> none  [the longest x112 656 us: delta_block(): lax.linalg.triangular_solve(system, right_side, left_side=True, lower=Tru...]
    all_gather x11 -> x4, waiting for transfers between devices: 449 us -> 229 us  [gather_rows(): return lax.all_gather(shard, 'row', axis=0, tiled=True)]
    dot_general x376 -> x26, matrix products: 388 us -> 170 us  [dot(): lax.dot_general(a, b, (((ca,), (cb,)), ((), ())), preferred_element_type=...]
    ppermute x0 -> x33, waiting for transfers between devices: none -> 177 us  [swap(): return lax.ppermute(x, axis, [(i, i ^ bit) for i in range(n)])]
    reduce_scatter x11 -> x5, waiting for transfers between devices: 437 us -> 337 us  [scatter_rows(): lax.psum_scatter(grad.astype(bf16), 'row', scatter_dimension=0, tiled=True)]
    psum x4 -> x0, blocking collectives: 89.4 us -> none  [the longest x1 40.3 us: per_device(): lax.psum((gain_in_part, gain_mid_part, grad_head), ('row', 'col'))]
    squeeze x80 -> x0, local copies, waits for them, and re-layouts: 84.6 us -> none  [delta_mixer(): lax.scan(jax.checkpoint(delta_block), start_state, blocks)]
    pallas_call x0 -> x6, Pallas kernels: none -> 79.7 us  [the longest x1 36.7 us: mixer_backward(): pl.pallas_call(functools.partial(bwd_kernel, heads, dh), grid=(steps,), i...]
  transfers between devices with their start and end apart: 23 -> 42, of which waited for: 16 -> 21; matrix products, arithmetic and copies ran while one was open for 53% -> 14% of each run, Pallas kernels for 0% -> 7%
where the time goes in v1:
time: 1090 us; the launch traced here: 1080 us
  waiting for transfers between devices  744 us (68%)
  matrix products  170 us (16%)
  Pallas kernels  79.7 us (7%)
  local copies, waits for them, and re-layouts  31.3 us (3%)
  other arithmetic  23.1 us (2%)
  starting transfers between devices  17.7 us (2%)
  between operations  15.6 us (1%)
    reduce_scatter x5, waiting for transfers between devices, scatter_rows(): lax.psum_scatter(grad.astype(bf16), 'row', scatter_dimension=0, tiled=True)  337 us
    all_gather x4, waiting for transfers between devices, gather_rows(): return lax.all_gather(shard, 'row', axis=0, tiled=True)  229 us
    ppermute x33, waiting for transfers between devices, swap(): return lax.ppermute(x, axis, [(i, i ^ bit) for i in range(n)])  177 us
    dot_general x26, matrix products, dot(): lax.dot_general(a, b, (((ca,), (cb,)), ((), ())), preferred_element_type=...  170 us
    pallas_call x1, Pallas kernels, mixer_backward(): pl.pallas_call(functools.partial(bwd_kernel, heads, dh), grid=(steps,), i...  36.7 us
    pallas_call x1, Pallas kernels, mixer_forward(): pl.pallas_call(functools.partial(fwd_kernel, heads, dh), grid=(steps,), i...  33.5 us
    unnamed x94, local copies, waits for them, and re-layouts  24.5 us
  transfers between devices with their start and end apart: 42, of which 21 were waited for; matrix products, arithmetic and copies ran while one was open for 14% of the time, Pallas kernels for 7%

profile of v1, /device:TPU:0, one launch (start us, length us, event | category | flops | bytes accessed | tf_op | source)
XLA Modules:
  0.0 1081.4 jit_solution(7054359454187102214)
XLA Ops:
  16.2 23.2 %collective-permute-done.1.refs_2_ = bf16[1024,512]{1,0:T(8,128)(2,1)S(1)} collective-permute-done((bf16[1024,512]{1,0:T(8,128)(2,1)S(1)}, bf16[1024,512]{1,0:T(8,128)(2,1)S(1)}, u32[]{:S(2)}, u32[]{:S(2)}) %collective-permute-start.1) | collective-permute-done | bytes 1048608 | tf_op jit(solution)/shard_map/ppermute | solution.py:271
  48.2 70.8 %all-gather.5.cloned.1.call-done = bf16[2048,1664]{1,0:T(8,128)(2,1)} async-done(((bf16[256,1664]{1,0:T(8,128)(2,1)}), bf16[2048,1664]{1,0:T(8,128)(2,1)}) %all-gather.5.cloned.1.call-update) | async-done | bytes 6815760 | tf_op jit(solution)/shard_map/all_gather | solution.py:372
  119.1 13.3 %fusion.92.x_ref.prev_ref = f32[1024,1664]{1,0:T(8,128)} fusion(bf16[1024,2048]{1,0:T(8,128)(2,1)} %copy-done.21, bf16[2048,1664]{1,0:T(8,128)(2,1)} %all-gather.5.cloned.1.call-done), kind=kOutput, calls=%fused_computation.121 | convolution fusion | flops 6979321856 | bytes 17825792 | tf_op jit(solution)/shard_map/dot_general | solution.py:368
  132.4 33.5 %mixer_forward.1 = (bf16[1024,512]{1,0:T(8,128)(2,1)S(1)}, f32[1024,512]{1,0:T(8,128)S(1)}, f32[1024,512]{1,0:T(8,128)S(1)}, f32[8,4,128,128]{3,2,1,0:T(8,128)S(1)}, f32[8,4,128,128]{3,2,1,0:T(8,128)S(1)}) custom-call(f32[1024,1664]{1,0:T(8,128)} %fusion.92.x_ref.prev_ref, f32[4,1536]{1,0:T(4,128)S(1)} %constant_dynamic-update-slice_fusion.conv_ref, ...), custom_call_target="tpu_custom_call" | custom-call | flops 8053063680 | bytes 16252928 | tf_op jit(solution)/shard_map/mixer_forward/pallas_call | solution.py:201
  183.4 17.9 %collective-permute-done.13.refs_2_ = bf16[1024,512]{1,0:T(8,128)(2,1)} collective-permute-done((bf16[1024,512]{1,0:T(8,128)(2,1)S(1)}, bf16[1024,512]{1,0:T(8,128)(2,1)}, u32[]{:S(2)}, u32[]{:S(2)}) %collective-permute-start.13) | collective-permute-done | bytes 1048608 | tf_op jit(solution)/shard_map/ppermute | solution.py:271
  201.3 22.1 %collective-permute-done.5 = bf16[1024,512]{1,0:T(8,128)(2,1)} collective-permute-done((bf16[1024,512]{1,0:T(8,128)(2,1)}, bf16[1024,512]{1,0:T(8,128)(2,1)}, u32[]{:S(2)}, u32[]{:S(2)}) %collective-permute-start.5) | collective-permute-done | bytes 1048608 | tf_op jit(solution)/shard_map/ppermute | solution.py:271
  233.5 18.9 %collective-permute-done.7.refs_2_ = bf16[1024,512]{1,0:T(8,128)(2,1)S(1)} collective-permute-done((bf16[1024,512]{1,0:T(8,128)(2,1)S(1)}, bf16[1024,512]{1,0:T(8,128)(2,1)S(1)}, u32[]{:S(2)}, u32[]{:S(2)}) %collective-permute-start.7) | collective-permute-done | bytes 1048608 | tf_op jit(solution)/shard_map/ppermute | solution.py:271
  252.4 11.9 %all-gather.11.cloned.1.call-done = bf16[2048,1408]{0,1:T(8,128)(2,1)} async-done(((bf16[256,1408]{0,1:T(8,128)(2,1)}), bf16[2048,1408]{0,1:T(8,128)(2,1)}) %all-gather.11.cloned.1.call-update) | async-done | bytes 5767184 | tf_op jit(solution)/shard_map/all_gather | solution.py:372
  264.3 12.0 %fusion.93 = f32[1024,1408]{1,0:T(8,128)} fusion(bf16[1024,2048]{1,0:T(8,128)(2,1)} %copy-done.2, bf16[2048,1408]{0,1:T(8,128)(2,1)} %all-gather.11.cloned.1.call-done), kind=kOutput, calls=%fused_computation.122 | convolution fusion | flops 5905580032 | bytes 15728640 | tf_op jit(solution)/shard_map/dot_general | solution.py:368
  282.4 146.4 %all-gather.9.cloned.1.call-done = bf16[2048,2816]{1,0:T(8,128)(2,1)} async-done(((bf16[256,2816]{1,0:T(8,128)(2,1)}), bf16[2048,2816]{1,0:T(8,128)(2,1)}) %all-gather.9.cloned.1.call-update) | async-done | bytes 11534352 | tf_op jit(solution)/shard_map/all_gather | solution.py:372
  428.8 11.8 %fusion.2 = f32[1024,1408]{1,0:T(8,128)} fusion(bf16[1024,2048]{1,0:T(8,128)(2,1)} %copy-done.23, bf16[2048,2816]{1,0:T(8,128)(2,1)} %all-gather.9.cloned.1.call-done), kind=kOutput, calls=%fused_computation.6 | convolution fusion | flops 5905580032 | bytes 15728640 | tf_op jit(solution)/shard_map/dot_general | solution.py:368
  440.6 14.5 %add_reduce_fusion = (f32[1024]{0:T(1024)S(1)}, bf16[1024,1408]{1,0:T(8,128)(2,1)S(1)}, bf16[1024,1408]{1,0:T(8,128)(2,1)S(1)}, bf16[1024,1408]{1,0:T(8,128)(2,1)}) fusion(f32[1024,1408]{1,0:T(8,128)} %fusion.2, f32[1024,1408]{1,0:T(8,128)} %fusion.93, bf16[1024,2048]{1,0:T(8,128)(2,1)S(1)} %copy-done.24, bf16[2048,2816]{1,0:T(8,128)(2,1)} %all-gather.9.cloned.1.call-done), kind=kOutput, calls=%fused_computation.9 | convolution fusion | flops 5937298432 | bytes 30150656 | tf_op jit(solution)/shard_map/dot_general | solution.py:368
  455.1 7.1 fusion.36
  478.2 19.9 %collective-permute-done.17 = bf16[1024,512]{1,0:T(8,128)(2,1)} collective-permute-done((bf16[1024,512]{1,0:T(8,128)(2,1)}, bf16[1024,512]{1,0:T(8,128)(2,1)}, u32[]{:S(2)}, u32[]{:S(2)}) %collective-permute-start.17) | collective-permute-done | bytes 1048608 | tf_op jit(solution)/shard_map/ppermute | solution.py:271
  502.5 24.0 %collective-permute-done.21.refs_2_ = bf16[1024,512]{1,0:T(8,128)(2,1)S(1)} collective-permute-done((bf16[1024,512]{1,0:T(8,128)(2,1)S(1)}, bf16[1024,512]{1,0:T(8,128)(2,1)S(1)}, u32[]{:S(2)}, u32[]{:S(2)}) %collective-permute-start.21) | collective-permute-done | bytes 1048608 | tf_op jit(solution)/shard_map/ppermute | solution.py:271
  535.4 11.0 %convolution_convert_fusion = bf16[2048,1408]{1,0:T(8,128)(2,1)} fusion(bf16[1024,2048]{1,0:T(8,128)(2,1)} %copy-done.2, bf16[1024,1408]{1,0:T(8,128)(2,1)S(1)} %copy-done.36), kind=kOutput, calls=%fused_computation | convolution fusion | flops 5908463616 | bytes 12845056 | tf_op jit(solution)/shard_map/dot_general | solution.py:368
  548.3 10.9 %convolution_convert_fusion.2 = bf16[2048,1408]{1,0:T(8,128)(2,1)} fusion(bf16[1024,2048]{1,0:T(8,128)(2,1)} %copy-done.23, bf16[1024,1408]{1,0:T(8,128)(2,1)S(1)} %copy-done.41), kind=kOutput, calls=%fused_computation.2 | convolution fusion | flops 5908463616 | bytes 12845056 | tf_op jit(solution)/shard_map/dot_general | solution.py:368
  561.0 11.0 %convolution_convert_fusion.1 = bf16[2048,1408]{1,0:T(8,128)(2,1)} fusion(bf16[1024,2048]{1,0:T(8,128)(2,1)} %copy-done.23, bf16[1024,1408]{1,0:T(8,128)(2,1)S(1)} %copy-done.39), kind=kOutput, calls=%fused_computation.1 | convolution fusion | flops 5908463616 | bytes 12845056 | tf_op jit(solution)/shard_map/dot_general | solution.py:368
  572.3 5.5 fusion.94.m_ref
  577.8 36.7 %mixer_backward.1 = (bf16[1024,1664]{1,0:T(8,128)(2,1)S(1)}, f32[4,1536]{1,0:T(4,128)S(1)}, f32[1,128]{1,0:T(1,128)S(1)}, f32[1024,1]{1,0:T(8,128)S(1)}) custom-call(f32[1024,1664]{1,0:T(8,128)} %fusion.92.x_ref.prev_ref, f32[1024,1664]{1,0:T(8,128)} %fusion.92.x_ref.prev_ref, f32[4,1536]{1,0:T(4,128)S(1)} %constant_dynamic-update-slice_fusion.conv_ref, ...), custom_call_target="tpu_custom_call" | custom-call | flops 6039797760 | bytes 19660800 | tf_op jit(solution)/shard_map/mixer_backward/pallas_call | solution.py:234
  616.3 10.1 convolution_convert_fusion.3
  635.0 4.6 fusion.30
  648.1 5.6 fusion.27
  653.7 4.8 add_convert_fusion
  659.5 12.4 %collective-permute-done.26 = f32[8,128]{1,0:T(8,128)S(1)} collective-permute-done((f32[8,128]{1,0:T(8,128)S(1)}, f32[8,128]{1,0:T(8,128)S(1)}, u32[]{:S(2)}, u32[]{:S(2)}) %collective-permute-start.26) | collective-permute-done | bytes 4128 | tf_op jit(solution)/shard_map/ppermute | solution.py:271
  672.0 5.1 fusion.24
  677.7 16.2 %collective-permute-done.25 = bf16[1024,512]{1,0:T(8,128)(2,1)} collective-permute-done((bf16[1024,512]{1,0:T(8,128)(2,1)}, bf16[1024,512]{1,0:T(8,128)(2,1)}, u32[]{:S(2)}, u32[]{:S(2)}) %collective-permute-start.25) | collective-permute-done | bytes 1048608 | tf_op jit(solution)/shard_map/ppermute | solution.py:271
  693.9 7.9 fusion.17
  708.7 5.8 collective-permute-done.30
  729.3 99.0 %reduce-scatter.10.cloned.1.call-done = bf16[256,1408]{1,0:T(8,128)(2,1)} async-done(((bf16[2048,1408]{1,0:T(8,128)(2,1)}), bf16[256,1408]{1,0:T(8,128)(2,1)}) %reduce-scatter.10.cloned.1.call-update) | async-done | bytes 720912 | tf_op jit(solution)/shard_map/reduce_scatter | solution.py:376
  830.6 111.1 %reduce-scatter.12.cloned.1.call-done = bf16[256,1408]{1,0:T(8,128)(2,1)} async-done(((bf16[2048,1408]{1,0:T(8,128)(2,1)}), bf16[256,1408]{1,0:T(8,128)(2,1)}) %reduce-scatter.12.cloned.1.call-update) | async-done | bytes 720912 | tf_op jit(solution)/shard_map/reduce_scatter | solution.py:376
  944.1 126.6 %reduce-scatter.6.cloned.1.call-done = bf16[256,1664]{1,0:T(8,128)(2,1)} async-done(((bf16[2048,1664]{1,0:T(8,128)(2,1)}), bf16[256,1664]{1,0:T(8,128)(2,1)}) %reduce-scatter.6.cloned.1.call-update) | async-done | bytes 851984 | tf_op jit(solution)/shard_map/reduce_scatter | solution.py:376
  (230 shorter events, 134.5 us)
Async XLA Ops:
  7.2 111.9 %all-gather.5.cloned.1.call-start = ((), (), s32[]{:S(2)}) async-start(), calls=%async_computation.5 | async-start | bytes 7667712 | tf_op jit(solution)/shard_map/all_gather | solution.py:372
  10.3 160.9 %all-gather.7.cloned.1.call-start = ((), (), s32[]{:S(2)}) async-start(), calls=%async_computation.6 | async-start | bytes 2359296 | tf_op jit(solution)/shard_map/all_gather | solution.py:372
  11.1 253.3 %all-gather.11.cloned.1.call-start = ((), (), s32[]{:S(2)}) async-start(), calls=%async_computation.8 | async-start | bytes 6488064 | tf_op jit(solution)/shard_map/all_gather | solution.py:372
  11.8 417.0 %all-gather.9.cloned.1.call-start = ((), (), s32[]{:S(2)}) async-start(), calls=%async_computation.7 | async-start | bytes 12976128 | tf_op jit(solution)/shard_map/all_gather | solution.py:372
  13.1 711.5 %reduce-scatter.8.cloned.1.call-start = ((), (), s32[]{:S(2)}) async-start(), calls=%async_computation.10 | async-start | bytes 2359296 | tf_op jit(solution)/shard_map/reduce_scatter | solution.py:376
  13.1 26.2 %collective-permute-start.1 = (bf16[1024,512]{1,0:T(8,128)(2,1)S(1)}, bf16[1024,512]{1,0:T(8,128)(2,1)S(1)}, u32[]{:S(2)}, u32[]{:S(2)}) collective-permute-start(bf16[1024,512]{1,0:T(8,128)(2,1)S(1)} %copy-done), channel_id=1, source_target_pairs={{0,2},{1,3},{2,0},{3,1},{4,6},{5,7},{6,4},{7,5},{8,10},{9,11},{10,... | collective-permute-start | bytes 3145736 | tf_op jit(solution)/shard_map/ppermute | solution.py:271
  16.2 23.2 %collective-permute-start = (bf16[1024,512]{1,0:T(8,128)(2,1)S(1)}, bf16[1024,512]{1,0:T(8,128)(2,1)S(1)}, u32[]{:S(2)}, u32[]{:S(2)}) collective-permute-start(bf16[1024,512]{1,0:T(8,128)(2,1)S(1)} %copy-done), channel_id=1, source_target_pairs={{0,1},{1,0},{2,3},{3,2},{4,5},{5,4},{6,7},{7,6},{8,9},{9,8},{10,11... | collective-permute-start | bytes 3145736 | tf_op jit(solution)/shard_map/ppermute | solution.py:271
  175.2 26.1 %collective-permute-start.13 = (bf16[1024,512]{1,0:T(8,128)(2,1)S(1)}, bf16[1024,512]{1,0:T(8,128)(2,1)}, u32[]{:S(2)}, u32[]{:S(2)}) collective-permute-start(bf16[1024,512]{1,0:T(8,128)(2,1)S(1)} %broadcast_multiply_fusion.refs_0_), channel_id=1, source_target_pairs={{0,2},{1,3},{2,0},{3,1},{4,6},{5,7},{6,4},{7,5},{8,10},{9,11},{10,... | collective-permute-start | bytes 3145736 | tf_op jit(solution)/shard_map/ppermute | solution.py:271
  179.5 21.8 %collective-permute-start.3 = (bf16[1024,512]{1,0:T(8,128)(2,1)}, bf16[1024,512]{1,0:T(8,128)(2,1)}, u32[]{:S(2)}, u32[]{:S(2)}) collective-permute-start(bf16[1024,512]{1,0:T(8,128)(2,1)} %convolution_convert_fusion.8), channel_id=1, source_target_pairs={{0,1},{1,0},{2,3},{3,2},{4,5},{5,4},{6,7},{7,6},{8,9},{9,8},{10,11... | collective-permute-start | bytes 3145736 | tf_op jit(solution)/shard_map/ppermute | solution.py:271
  182.9 40.6 %collective-permute-start.5 = (bf16[1024,512]{1,0:T(8,128)(2,1)}, bf16[1024,512]{1,0:T(8,128)(2,1)}, u32[]{:S(2)}, u32[]{:S(2)}) collective-permute-start(bf16[1024,512]{1,0:T(8,128)(2,1)} %add_convert_fusion.4), channel_id=1, source_target_pairs={{0,2},{1,3},{2,0},{3,1},{4,6},{5,7},{6,4},{7,5},{8,10},{9,11},{10,... | collective-permute-start | bytes 3145736 | tf_op jit(solution)/shard_map/ppermute | solution.py:271
  183.4 45.7 %collective-permute-start.12 = (bf16[1024,512]{1,0:T(8,128)(2,1)S(1)}, bf16[1024,512]{1,0:T(8,128)(2,1)}, u32[]{:S(2)}, u32[]{:S(2)}) collective-permute-start(bf16[1024,512]{1,0:T(8,128)(2,1)S(1)} %broadcast_multiply_fusion.refs_0_), channel_id=1, source_target_pairs={{0,1},{1,0},{2,3},{3,2},{4,5},{5,4},{6,7},{7,6},{8,9},{9,8},{10,11... | collective-permute-start | bytes 3145736 | tf_op jit(solution)/shard_map/ppermute | solution.py:271
  201.3 27.8 %collective-permute-start.14 = (bf16[1024,512]{1,0:T(8,128)(2,1)}, bf16[1024,512]{1,0:T(8,128)(2,1)S(1)}, u32[]{:S(2)}, u32[]{:S(2)}) collective-permute-start(bf16[1024,512]{1,0:T(8,128)(2,1)} %collective-permute-done.13.refs_2_), channel_id=1, source_target_pairs={{0,1},{1,0},{2,3},{3,2},{4,5},{5,4},{6,7},{7,6},{8,9},{9,8},{10,11... | collective-permute-start | bytes 3145736 | tf_op jit(solution)/shard_map/ppermute | solution.py:271
  227.6 24.8 %collective-permute-start.7 = (bf16[1024,512]{1,0:T(8,128)(2,1)S(1)}, bf16[1024,512]{1,0:T(8,128)(2,1)S(1)}, u32[]{:S(2)}, u32[]{:S(2)}) collective-permute-start(bf16[1024,512]{1,0:T(8,128)(2,1)S(1)} %get-tuple-element.96.refs_0_), channel_id=1, source_target_pairs={{0,2},{1,3},{2,0},{3,1},{4,6},{5,7},{6,4},{7,5},{8,10},{9,11},{10,... | collective-permute-start | bytes 3145736 | tf_op jit(solution)/shard_map/ppermute | solution.py:271
  233.5 42.8 %collective-permute-start.6 = (bf16[1024,512]{1,0:T(8,128)(2,1)S(1)}, bf16[1024,512]{1,0:T(8,128)(2,1)S(1)}, u32[]{:S(2)}, u32[]{:S(2)}) collective-permute-start(bf16[1024,512]{1,0:T(8,128)(2,1)S(1)} %get-tuple-element.96.refs_0_), channel_id=1, source_target_pairs={{0,1},{1,0},{2,3},{3,2},{4,5},{5,4},{6,7},{7,6},{8,9},{9,8},{10,11... | collective-permute-start | bytes 3145736 | tf_op jit(solution)/shard_map/ppermute | solution.py:271
  252.4 23.9 %collective-permute-start.8 = (bf16[1024,512]{1,0:T(8,128)(2,1)S(1)}, bf16[1024,512]{1,0:T(8,128)(2,1)}, u32[]{:S(2)}, u32[]{:S(2)}) collective-permute-start(bf16[1024,512]{1,0:T(8,128)(2,1)S(1)} %collective-permute-done.7.refs_2_), channel_id=1, source_target_pairs={{0,1},{1,0},{2,3},{3,2},{4,5},{5,4},{6,7},{7,6},{8,9},{9,8},{10,11... | collective-permute-start | bytes 3145736 | tf_op jit(solution)/shard_map/ppermute | solution.py:271
  462.4 10.5 collective-permute-start.18
  468.0 10.2 collective-permute-start.15
  472.4 25.7 %collective-permute-start.17 = (bf16[1024,512]{1,0:T(8,128)(2,1)}, bf16[1024,512]{1,0:T(8,128)(2,1)}, u32[]{:S(2)}, u32[]{:S(2)}) collective-permute-start(bf16[1024,512]{1,0:T(8,128)(2,1)} %add_convert_fusion.1), channel_id=1, source_target_pairs={{0,2},{1,3},{2,0},{3,1},{4,6},{5,7},{6,4},{7,5},{8,10},{9,11},{10,... | collective-permute-start | bytes 3145736 | tf_op jit(solution)/shard_map/ppermute | solution.py:271
  502.0 24.6 %collective-permute-start.21 = (bf16[1024,512]{1,0:T(8,128)(2,1)S(1)}, bf16[1024,512]{1,0:T(8,128)(2,1)S(1)}, u32[]{:S(2)}, u32[]{:S(2)}) collective-permute-start(bf16[1024,512]{1,0:T(8,128)(2,1)S(1)} %get-tuple-element.78.refs_0_), channel_id=1, source_target_pairs={{0,2},{1,3},{2,0},{3,1},{4,6},{5,7},{6,4},{7,5},{8,10},{9,11},{10,... | collective-permute-start | bytes 3145736 | tf_op jit(solution)/shard_map/ppermute | solution.py:271
  502.5 24.0 %collective-permute-start.20 = (bf16[1024,512]{1,0:T(8,128)(2,1)S(1)}, bf16[1024,512]{1,0:T(8,128)(2,1)S(1)}, u32[]{:S(2)}, u32[]{:S(2)}) collective-permute-start(bf16[1024,512]{1,0:T(8,128)(2,1)S(1)} %get-tuple-element.78.refs_0_), channel_id=1, source_target_pairs={{0,1},{1,0},{2,3},{3,2},{4,5},{5,4},{6,7},{7,6},{8,9},{9,8},{10,11... | collective-permute-start | bytes 3145736 | tf_op jit(solution)/shard_map/ppermute | solution.py:271
  535.4 191.2 %reduce-scatter.14.cloned.1.call-start = ((), (), s32[]{:S(2)}) async-start(), calls=%async_computation.13 | async-start | bytes 6488064 | tf_op jit(solution)/shard_map/reduce_scatter | solution.py:376
  546.5 281.9 %reduce-scatter.10.cloned.1.call-start = ((), (), s32[]{:S(2)}) async-start(), calls=%async_computation.11 | async-start | bytes 6488064 | tf_op jit(solution)/shard_map/reduce_scatter | solution.py:376
  559.2 382.6 %reduce-scatter.12.cloned.1.call-start = ((), (), s32[]{:S(2)}) async-start(), calls=%async_computation.12 | async-start | bytes 6488064 | tf_op jit(solution)/shard_map/reduce_scatter | solution.py:376
  572.0 498.6 %reduce-scatter.6.cloned.1.call-start = ((), (), s32[]{:S(2)}) async-start(), calls=%async_computation.9 | async-start | bytes 7667712 | tf_op jit(solution)/shard_map/reduce_scatter | solution.py:376
  631.6 11.2 %collective-permute-start.10 = (bf16[1024,512]{1,0:T(8,128)(2,1)S(1)}, bf16[1024,512]{1,0:T(8,128)(2,1)S(1)}, u32[]{:S(2)}, u32[]{:S(2)}) collective-permute-start(bf16[1024,512]{1,0:T(8,128)(2,1)S(1)} %convolution_convert_fusion.5), channel_id=1, source_target_pairs={{0,1},{1,0},{2,3},{3,2},{4,5},{5,4},{6,7},{7,6},{8,9},{9,8},{10,11... | collective-permute-start | bytes 3145736 | tf_op jit(solution)/shard_map/ppermute | solution.py:271
  634.7 43.0 %collective-permute-start.9 = (bf16[1024,512]{1,0:T(8,128)(2,1)}, bf16[1024,512]{1,0:T(8,128)(2,1)}, u32[]{:S(2)}, u32[]{:S(2)}) collective-permute-start(bf16[1024,512]{1,0:T(8,128)(2,1)} %convolution_convert_fusion.6), channel_id=1, source_target_pairs={{0,1},{1,0},{2,3},{3,2},{4,5},{5,4},{6,7},{7,6},{8,9},{9,8},{10,11... | collective-permute-start | bytes 3145736 | tf_op jit(solution)/shard_map/ppermute | solution.py:271
  639.5 14.2 %collective-permute-start.24 = (bf16[1024,512]{1,0:T(8,128)(2,1)}, bf16[1024,512]{1,0:T(8,128)(2,1)}, u32[]{:S(2)}, u32[]{:S(2)}) collective-permute-start(bf16[1024,512]{1,0:T(8,128)(2,1)} %fusion.30), channel_id=1, source_target_pairs={{0,1},{1,0},{2,3},{3,2},{4,5},{5,4},{6,7},{7,6},{8,9},{9,8},{10,11... | collective-permute-start | bytes 3145736 | tf_op jit(solution)/shard_map/ppermute | solution.py:271
  645.6 32.0 %collective-permute-start.11 = (bf16[1024,512]{1,0:T(8,128)(2,1)}, bf16[1024,512]{1,0:T(8,128)(2,1)}, u32[]{:S(2)}, u32[]{:S(2)}) collective-permute-start(bf16[1024,512]{1,0:T(8,128)(2,1)} %add_convert_fusion.3), channel_id=1, source_target_pairs={{0,2},{1,3},{2,0},{3,1},{4,6},{5,7},{6,4},{7,5},{8,10},{9,11},{10,... | collective-permute-start | bytes 3145736 | tf_op jit(solution)/shard_map/ppermute | solution.py:271
  646.7 25.3 %collective-permute-start.26 = (f32[8,128]{1,0:T(8,128)S(1)}, f32[8,128]{1,0:T(8,128)S(1)}, u32[]{:S(2)}, u32[]{:S(2)}) collective-permute-start(f32[8,128]{1,0:T(8,128)S(1)} %bitcast.75), channel_id=1, source_target_pairs={{0,2},{1,3},{2,0},{3,1},{4,6},{5,7},{6,4},{7,5},{8,10},{9,11},{10,... | collective-permute-start | bytes 12296 | tf_op jit(solution)/shard_map/ppermute | solution.py:271
  653.7 24.0 %collective-permute-start.23 = (bf16[1024,512]{1,0:T(8,128)(2,1)}, bf16[1024,512]{1,0:T(8,128)(2,1)}, u32[]{:S(2)}, u32[]{:S(2)}) collective-permute-start(bf16[1024,512]{1,0:T(8,128)(2,1)} %fusion.27), channel_id=1, source_target_pairs={{0,1},{1,0},{2,3},{3,2},{4,5},{5,4},{6,7},{7,6},{8,9},{9,8},{10,11... | collective-permute-start | bytes 3145736 | tf_op jit(solution)/shard_map/ppermute | solution.py:271
  658.6 35.3 %collective-permute-start.25 = (bf16[1024,512]{1,0:T(8,128)(2,1)}, bf16[1024,512]{1,0:T(8,128)(2,1)}, u32[]{:S(2)}, u32[]{:S(2)}) collective-permute-start(bf16[1024,512]{1,0:T(8,128)(2,1)} %add_convert_fusion), channel_id=1, source_target_pairs={{0,2},{1,3},{2,0},{3,1},{4,6},{5,7},{6,4},{7,5},{8,10},{9,11},{10,... | collective-permute-start | bytes 3145736 | tf_op jit(solution)/shard_map/ppermute | solution.py:271
  707.1 7.4 collective-permute-start.30
  (54 other events, 492.7 us)
Sparse Core Ops, SparseCore 0:
  10.8 108.2 all-gather.4
  121.1 49.2 all-gather.6
  172.5 91.7 all-gather.10
  266.9 161.8 all-gather.8
  535.5 65.0 reduce-scatter.7
  604.1 111.5 reduce-scatter.13
  719.3 108.9 reduce-scatter.9
  832.0 109.7 reduce-scatter.11
  945.4 125.1 reduce-scatter.5

commit v2 on v1

--- a/solution.py
+++ b/solution.py
@@ -8,6 +8,7 @@
 
 CHUNK = 128
 EPS = 1e-6
+FREE = pl.CostEstimate(flops=0, bytes_accessed=0, transcendentals=0)
 bf16 = jnp.bfloat16
 f32 = jnp.float32
 
@@ -197,7 +198,6 @@
     steps = rows // CHUNK
     square = pl.BlockSpec((1, heads, dh, dh), lambda i: (i, 0, 0, 0))
     wide = pl.BlockSpec((CHUNK, hd), lambda i: (i, 0))
-    flops = rows * heads * (20 * 3 * 2 * 128 * 128)
     return pl.pallas_call(
         functools.partial(fwd_kernel, heads, dh),
         grid=(steps,),
@@ -216,7 +216,7 @@
         ],
         scratch_shapes=[pltpu.VMEM((heads, dh, dh), f32), pltpu.VMEM((8, 3 * hd), f32)],
         compiler_params=pltpu.CompilerParams(vmem_limit_bytes=40 * 2**20),
-        cost_estimate=pl.CostEstimate(flops=flops, bytes_accessed=rows * (width * 4 + hd * 18), transcendentals=0),
+        cost_estimate=FREE,
         name="mixer_forward",
     )(proj, conv, gain)
 
@@ -230,7 +230,6 @@
     per = CHUNK // 8
     square = pl.BlockSpec((1, heads, dh, dh), lambda i: (last - i, 0, 0, 0))
     wide = pl.BlockSpec((CHUNK, hd), lambda i: (last - i, 0))
-    flops = rows * heads * (15 * 3 * 2 * 128 * 128)
     return pl.pallas_call(
         functools.partial(bwd_kernel, heads, dh),
         grid=(steps,),
@@ -257,7 +256,7 @@
         ],
         scratch_shapes=[pltpu.VMEM((heads, dh, dh), f32), pltpu.VMEM((8, 3 * hd), f32)],
         compiler_params=pltpu.CompilerParams(vmem_limit_bytes=40 * 2**20),
-        cost_estimate=pl.CostEstimate(flops=flops, bytes_accessed=rows * (width * 6 + hd * 18), transcendentals=0),
+        cost_estimate=FREE,
         name="mixer_backward",
     )(proj, proj, conv, gain, mixed_cot, o, fresh, inv, states)
 
@@ -294,21 +293,42 @@
     return [pieces[j] for j in range(n)]
 
 
-def sum_cols(piece):
-    n = lax.axis_size("col")
-    away = {}
-    bit = 1
-    kept = list(range(n))
-    got = {}
-    while bit < n:
-        for j in [j for j in kept if j & bit]:
-            mine = piece(j) + got[j] if j in got else piece(j)
-            got_j = swap(mine.astype(bf16), "col", bit).astype(f32)
-            base = j ^ bit
-            got[base] = got[base] + got_j if base in got else got_j
-        kept = [j for j in kept if not j & bit]
-        bit *= 2
-    return piece(0) + got[0]
+class ColSum:
+    def __init__(self, terms, block):
+        self.terms, self.block = terms, block
+        self.kept, self.got = list(range(lax.axis_size("col"))), {}
+
+    def pieces(self, js, dtype, earlier):
+        (left, pair), rest = self.terms[0], self.terms[1:]
+        gots = [self.got.get(j) for j in js]
+        return piece_call([(after(left, *earlier), pair)] + rest, self.block, js, gots, dtype)
+
+    def send(self, bit, *earlier):
+        js = [j for j in self.kept if j & bit]
+        sent = self.pieces(js, bf16, earlier)
+        for j, low in zip(js, sent):
+            got, base = swap(low, "col", bit), j ^ bit
+            self.got[base] = got if base not in self.got else self.got[base].astype(f32) + got.astype(f32)
+        self.kept = [j for j in self.kept if not j & bit]
+        return sent
+
+    def send_last(self, *earlier):
+        bit = 2
+        while 2 * bit < lax.axis_size("col"):
+            earlier = self.send(bit, *earlier)
+            bit *= 2
+        first = self.got.pop(0)
+        sent = self.send(bit, *earlier)
+        self.last = self.got[0]
+        self.got[0] = first
+        return sent
+
+    def set_base(self, *earlier):
+        self.base = self.pieces([0], f32, earlier)[0]
+        return self.base
+
+    def total(self):
+        return self.base + self.last.astype(f32)
 
 
 def norm_kernel(width, me_ref, *refs):
@@ -320,15 +340,21 @@
         square = square + v * v
     factor = lax.rsqrt(jnp.sum(square, axis=1, keepdims=True) / total + EPS)
     factor_ref[...] = factor
+    half = width // 2
     for j, v in enumerate(values):
-        cols = pl.ds(pl.multiple_of((me_ref[0] ^ j) * width, width), width)
-        normed_ref[:, cols] = (v * factor * gain_ref[:, cols]).astype(bf16)
+        for p in range(2):
+            start = p * (total // 2) + (me_ref[0] ^ j) * half
+            cols = pl.ds(pl.multiple_of(start, half), half)
+            normed_ref[:, cols] = (v[:, p * half : (p + 1) * half] * factor * gain_ref[:, cols]).astype(bf16)
 
 
 def join_kernel(width, me_ref, *refs):
     pieces, out_ref = refs[:-1], refs[-1]
-    for j, p in enumerate(pieces):
-        out_ref[:, pl.ds(pl.multiple_of((me_ref[0] ^ j) * width, width), width)] = p[...]
+    half = width // 2
+    for j, piece in enumerate(pieces):
+        for p in range(2):
+            start = p * len(pieces) * half + (me_ref[0] ^ j) * half
+            out_ref[:, pl.ds(pl.multiple_of(start, half), half)] = piece[:, p * half : (p + 1) * half]
 
 
 TILE = 256
@@ -348,7 +374,7 @@
         ),
         out_shape=outs,
         compiler_params=pltpu.CompilerParams(vmem_limit_bytes=24 * 2**20),
-        cost_estimate=pl.CostEstimate(flops=rows * width * 16, bytes_accessed=rows * width * len(pieces) * 4, transcendentals=0),
+        cost_estimate=FREE,
         name=name,
     )(me, *pieces, *extra)
 
@@ -368,12 +394,193 @@
     return lax.dot_general(a, b, (((ca,), (cb,)), ((), ())), preferred_element_type=f32)
 
 
-def gather_rows(shard):
-    return lax.all_gather(shard, "row", axis=0, tiled=True)
-
-
-def scatter_rows(grad):
-    return lax.psum_scatter(grad.astype(bf16), "row", scatter_dimension=0, tiled=True)
+FREE = pl.CostEstimate(flops=0, bytes_accessed=0, transcendentals=0)
+
+
+def tile_call(kernel, arrays, specs, outs, out_specs, grid, name, me=None):
+    params = dict(
+        compiler_params=pltpu.CompilerParams(vmem_limit_bytes=56 * 2**20), cost_estimate=FREE, name=name
+    )
+    if me is None:
+        return pl.pallas_call(kernel, grid=grid, in_specs=specs, out_specs=out_specs, out_shape=outs, **params)(*arrays)
+    grid_spec = pltpu.PrefetchScalarGridSpec(
+        num_scalar_prefetch=1, grid=grid, in_specs=specs, out_specs=out_specs
+    )
+    return pl.pallas_call(kernel, grid_spec=grid_spec, out_shape=outs, **params)(me, *arrays)
+
+
+def row_tile(width):
+    return pl.BlockSpec((TILE, width), lambda i, *_: (i, 0))
+
+
+def half_tile(width, which):
+    return pl.BlockSpec((TILE, width), lambda i, *_: (i, which))
+
+
+def whole(shape):
+    return pl.BlockSpec(shape, lambda i, *_: (0, 0))
+
+
+def halves_kernel(count, *refs):
+    out = refs[-1]
+    total = dot(refs[0][...], refs[1][...])
+    for i in range(1, count):
+        total = total + dot(refs[2 * i][...], refs[2 * i + 1][...])
+    out[...] = total.astype(out.dtype)
+
+
+def halves(left, pairs, dtype=f32):
+    rows, half, width = left.shape[0], left.shape[1] // 2, pairs[0][1].shape[1]
+    arrays, specs = [], []
+    for which, weight in pairs:
+        arrays += [left, weight]
+        specs += [half_tile(half, which), whole(weight.shape)]
+    return tile_call(functools.partial(halves_kernel, len(pairs)), arrays, specs,
+                     jax.ShapeDtypeStruct((rows, width), dtype), row_tile(width), (rows // TILE,), "halves")
+
+
+def both(refs):
+    return dot(refs[0][...], refs[2][...]) + dot(refs[1][...], refs[3][...])
+
+
+def hidden_kernel(*refs):
+    gate_ref, up_ref, hidden_ref = refs[4:]
+    up = both(refs)
+    gate = gate_ref[...].astype(f32)
+    up_ref[...] = up.astype(bf16)
+    hidden_ref[...] = (gate * sigmoid(gate) * up).astype(bf16)
+
+
+def both_specs(left, pair):
+    half = left.shape[1] // 2
+    return [left, left, *pair], [half_tile(half, 0), half_tile(half, 1), whole(pair[0].shape), whole(pair[1].shape)]
+
+
+def hidden_call(left, pair, gate):
+    rows, width = gate.shape
+    tile = row_tile(width)
+    arrays, specs = both_specs(left, pair)
+    outs = [jax.ShapeDtypeStruct((rows, width), bf16)] * 2
+    return tile_call(hidden_kernel, arrays + [gate], specs + [tile], outs, [tile, tile], (rows // TILE,), "hidden")
+
+
+def cots_kernel(*refs):
+    gate_ref, up_ref, gate_cot_ref, up_cot_ref, inner_ref = refs[4:]
+    cot = both(refs)
+    gate, up = gate_ref[...].astype(f32), up_ref[...].astype(f32)
+    sig = sigmoid(gate)
+    silu = gate * sig
+    gate_cot = cot * up * (sig + silu * (1.0 - sig))
+    up_cot = cot * silu
+    gate_cot_ref[...] = gate_cot.astype(bf16)
+    up_cot_ref[...] = up_cot.astype(bf16)
+    inner_ref[...] = jnp.sum(gate_cot * gate + up_cot * up, axis=1, keepdims=True)
+
+
+def cots_call(left, pair, gate, up):
+    rows, width = gate.shape
+    tile = row_tile(width)
+    arrays, specs = both_specs(left, pair)
+    outs = [jax.ShapeDtypeStruct((rows, width), bf16)] * 2 + [jax.ShapeDtypeStruct((rows, 1), f32)]
+    return tile_call(cots_kernel, arrays + [gate, up], specs + [tile, tile], outs, [tile, tile, row_tile(1)],
+                     (rows // TILE,), "cots")
+
+
+def piece_kernel(count, pieces, has_got, me_ref, *refs):
+    outs = refs[-pieces:]
+    stride = 1 + 2 * pieces
+    for n, out in enumerate(outs):
+        width = out.shape[1] // 2
+        for p in range(2):
+            total = None
+            for i in range(count):
+                term = dot(refs[stride * i][...], refs[stride * i + 1 + 2 * n + p][...], 1, 1)
+                total = term if total is None else total + term
+            if has_got:
+                total = total + refs[stride * count + n][:, p * width : (p + 1) * width].astype(f32)
+            out[:, p * width : (p + 1) * width] = total.astype(out.dtype)
+
+
+def piece_call(terms, block, js, gots, dtype):
+    rows = terms[0][0].shape[0]
+    me = jnp.stack([lax.axis_index("col") ^ j for j in js]).astype(jnp.int32)
+    arrays, specs = [], []
+    for left, pair in terms:
+        arrays.append(left)
+        specs.append(row_tile(left.shape[1]))
+        for n in range(len(js)):
+            arrays += pair
+            specs += [pl.BlockSpec((block, w.shape[1]), lambda i, m, n=n: (m[n], 0)) for w in pair]
+    has_got = gots[0] is not None
+    if has_got:
+        arrays += gots
+        specs += [row_tile(2 * block)] * len(js)
+    kernel = functools.partial(piece_kernel, len(terms), len(js), has_got)
+    outs = [jax.ShapeDtypeStruct((rows, 2 * block), dtype)] * len(js)
+    return tile_call(kernel, arrays, specs, outs, [row_tile(2 * block)] * len(js), (rows // TILE,), "piece", me)
+
+
+def rows_kernel(left_ref, right_ref, *refs):
+    total = dot(left_ref[...], right_ref[...], 0, 0)
+    if len(refs) > 1:
+        total = total + refs[0][...].astype(f32)
+    refs[-1][...] = total.astype(bf16)
+
+
+def rows_call(left, right, which, got=None):
+    rows, half, width = left.shape[0], left.shape[1] // 2, right.shape[1]
+    tile = 2 * TILE
+    steps = half // tile
+    arrays = [left, right] + ([] if got is None else [got])
+    specs = [pl.BlockSpec((rows, tile), lambda i: (0, which * steps + i)), whole(right.shape)]
+    out = pl.BlockSpec((tile, width), lambda i: (i, 0))
+    specs += [] if got is None else [out]
+    return tile_call(rows_kernel, arrays, specs, jax.ShapeDtypeStruct((half, width), bf16), out,
+                     (steps,), "rows")
+
+
+def parity_groups():
+    n = lax.axis_size("row")
+    return [list(range(p, n, 2)) for p in range(2)]
+
+
+def after(x, *earlier):
+    return lax.optimization_barrier((x,) + earlier)[0]
+
+
+def gather_parity(shard):
+    return lax.all_gather(shard, "row", axis=0, tiled=True, axis_index_groups=parity_groups())
+
+
+def scatter_parity(part):
+    return lax.psum_scatter(part, "row", scatter_dimension=0, tiled=True, axis_index_groups=parity_groups())
+
+
+def other_rows(left, right):
+    return rows_call(left, right, 1)
+
+
+def own_rows(left, right, got):
+    return rows_call(left, right, 0, got)
+
+
+def flip(first, second):
+    odd = (lax.axis_index("row") & 1) == 1
+    return jnp.where(odd, second, first), jnp.where(odd, first, second)
+
+
+def by_parity(x, chunk):
+    lead, width = x.shape
+    parts = x.reshape(lead, width // (2 * chunk), 2, chunk)
+    first, second = flip(parts[:, :, 0], parts[:, :, 1])
+    return jnp.concatenate([first.reshape(lead, width // 2), second.reshape(lead, width // 2)], 1)
+
+
+def by_place(x, chunk):
+    lead, width = x.shape
+    shape = (lead, width // (2 * chunk), chunk)
+    first, second = flip(x[:, : width // 2].reshape(shape), x[:, width // 2 :].reshape(shape))
+    return jnp.stack([first, second], 2).reshape(lead, width)
 
 
 def per_device(tokens, lengths, norm_in, q_weight, k_weight, v_weight, conv_q, conv_k, conv_v, beta_weight,
@@ -388,76 +595,127 @@
     live = live_column(lengths[0], rows)
     live_low = live.astype(bf16)
     beta_pad = jnp.pad(beta_weight, ((0, 0), (0, 128 - beta_weight.shape[1])))
-    w_in = gather_rows(jnp.concatenate([q_weight, k_weight, v_weight, beta_pad], 1))
-    w_out = gather_rows(out_weight.T)
-    w_ff = gather_rows(jnp.concatenate([gate_weight, up_weight], 1))
-    w_down = gather_rows(down_weight.T)
+    in_mine = gather_parity(jnp.concatenate([q_weight, k_weight, v_weight, beta_pad], 1))
+    out_mine = gather_parity(out_weight.T)
+    gate_mine = gather_parity(gate_weight)
+    up_mine = gather_parity(up_weight)
+    down_turned = down_weight.T
+    down_side = swap(down_turned, "row", 1)
+    down_mine = gather_parity(down_turned)
+    down_other = gather_parity(down_side)
     conv = jnp.concatenate([conv_q, conv_k, conv_v], 1)
     gain = head_gain.reshape(1, dh)
     gain_in = lax.dynamic_slice_in_dim(norm_in, col * width, width)
     gain_mid = lax.dynamic_slice_in_dim(norm_mid, col * width, width)
+    chunk = q_weight.shape[0]
+    tokens, cotangent = by_parity(tokens, chunk), by_parity(cotangent, chunk)
+    gain_in, gain_mid = by_parity(gain_in[None], chunk), by_parity(gain_mid[None], chunk)
+    norm_in, norm_mid = by_parity(norm_in[None], chunk), by_parity(norm_mid[None], chunk)
     tokens32 = tokens.astype(f32)
 
-    def block(w, j):
-        return lax.dynamic_slice_in_dim(w, (col ^ j) * width, width, 0)
-
+    block = width // 2
+
+    half = feat // 2
     normed, factor_in = join_norm(spread_cols(tokens), norm_in)
     ffn_cot = join(spread_cols(cotangent * live_low))
-    proj = dot(normed, w_in)
+    in_mine = after(in_mine, normed, ffn_cot, down_side)
+    in_other, out_other = swap(in_mine, "row", 1), swap(out_mine, "row", 1)
+    proj = halves(after(normed, out_mine), [(0, in_mine), (1, in_other)])
+    gate_mine = after(gate_mine, proj)
+    gate_other = swap(gate_mine, "row", 1)
+    proj = after(proj, gate_mine)
+    out_other = after(out_other, proj)
+    w_in, w_out = (in_mine, in_other), (out_mine, out_other)
     mixed, *kept = mixer_forward(proj, conv, gain, heads, dh)
-    branch = sum_cols(lambda j: dot(mixed, block(w_out, j), 1, 1))
-    middle = tokens32 + live * branch
+    branch = ColSum([(mixed, w_out)], block)
+    sent = branch.send(1)
+    sent = branch.send_last(*sent)
+    up_mine = after(up_mine, *sent)
+    up_other = swap(up_mine, "row", 1)
+    branch.set_base(*sent)
+    middle = tokens32 + live * after(branch.total(), gate_other)
     mid_low = middle.astype(bf16)
-    normed_mid, factor_mid = join_norm(spread_cols(mid_low), norm_mid)
-    gate = dot(normed_mid, w_ff[:, :ff])
-    up = dot(normed_mid, w_ff[:, ff:])
-    gate_sig = jax.nn.sigmoid(gate)
-    hidden = (gate * gate_sig * up).astype(bf16)
-    grad_down = scatter_rows(dot(ffn_cot, hidden, 0, 0))
-    hidden_cot = dot(ffn_cot, w_down)
-    gate_cot = (hidden_cot * up * gate_sig * (1.0 + gate * (1.0 - gate_sig))).astype(bf16)
-    up_cot = (hidden_cot * gate * gate_sig).astype(bf16)
-    grad_gate = scatter_rows(dot(normed_mid, gate_cot, 0, 0))
-    grad_up = scatter_rows(dot(normed_mid, up_cot, 0, 0))
-    inner_mid = jnp.sum(gate_cot.astype(f32) * gate + up_cot.astype(f32) * up, axis=1, keepdims=True)
+    normed_mid, factor_mid = join_norm(spread_cols(mid_low), after(norm_mid, up_mine))
+    w_gate, w_up = (gate_mine, gate_other), (up_mine, up_other)
+    gate = halves(normed_mid, [(0, gate_mine), (1, gate_other)], bf16)
+    up, hidden = hidden_call(after(normed_mid, gate), w_up, gate)
+    down_sent = other_rows(ffn_cot, hidden)
+    down_got = swap(down_sent, "row", 1)
+    w_down = after(down_mine, down_sent), after(down_other, down_sent)
+    gate_cot, up_cot, inner_mid = cots_call(ffn_cot, w_down, gate, up)
     inner_mid = sum_all(inner_mid.reshape(rows // 128, 128), "col").reshape(rows, 1) / factor_mid
-    both_cot = jnp.concatenate([gate_cot, up_cot], 1)
-    mid_cot = sum_cols(lambda j: dot(both_cot, block(w_ff, j), 1, 1))
-    result = sum_cols(lambda j: dot(hidden, block(w_down, j), 1, 1))
-    layer_out = (middle + live * result).astype(bf16)
+    mid_sum = ColSum([(gate_cot, w_gate), (up_cot, w_up)], block)
+    sent = mid_sum.send(1)
+    gate_sent = other_rows(after(normed_mid, *sent), gate_cot)
+    gate_got = swap(gate_sent, "row", 1)
+    sent = mid_sum.send_last(gate_sent)
+    up_sent = other_rows(after(normed_mid, *sent), up_cot)
+    up_got = swap(up_sent, "row", 1)
+    mid_sum.set_base(up_sent)
+    down_rows = own_rows(ffn_cot, hidden, after(down_got, mid_sum.base))
+    grad_down = scatter_parity(down_rows)
+    mid_cot = after(mid_sum.total(), down_rows)
 
     mid32 = mid_low.astype(f32)
     gmid_part = jnp.sum(mid_cot * mid32 * factor_mid, axis=0)
     middle_cot = cotangent.astype(f32) + factor_mid * gain_mid * mid_cot - mid32 * (factor_mid**3 * inner_mid / feat)
-    branch_cot = join(spread_cols((live * middle_cot).astype(bf16)))
-    mixed_cot = dot(branch_cot, w_out)
-    grad_out = scatter_rows(dot(branch_cot, mixed, 0, 0))
+    branch_low = (live * middle_cot).astype(bf16)
+    pieces = spread_cols(branch_low)
+    result = ColSum([(hidden, w_down)], block)
+    sent = result.send(1, branch_low)
+    pieces[0] = after(pieces[0], *sent)
+    branch_cot = join(pieces)
+    mixed_cot = halves(branch_cot, [(0, out_mine), (1, out_other)])
+    out_sent = other_rows(after(branch_cot, mixed_cot), mixed)
+    out_got = swap(out_sent, "row", 1)
+    gate_rows = own_rows(normed_mid, gate_cot, after(gate_got, out_sent, down_rows))
+    grad_gate = scatter_parity(gate_rows)
+    mixed_cot = after(mixed_cot, out_sent, gate_rows)
     low, gconv, ghead, inner_in = mixer_backward(proj, conv, gain, mixed_cot, kept, heads, dh)
-    grad_in = scatter_rows(dot(normed, low, 0, 0))
+    cut = 2 * hd
+    qk, vb = low[:, :cut], low[:, cut:]
+    qk_sent, vb_sent = other_rows(normed, qk), other_rows(normed, vb)
+    qk_got, vb_got = swap(qk_sent, "row", 1), swap(vb_sent, "row", 1)
+    up_rows = own_rows(normed_mid, up_cot, after(up_got, qk_sent, vb_sent, grad_down))
+    grad_up = scatter_parity(up_rows)
+    in_sum = ColSum([(low, w_in)], block)
+    sent = in_sum.send(1, up_rows)
+    sent = in_sum.send_last(*sent)
+    out_rows = own_rows(branch_cot, mixed, after(out_got, grad_gate, *sent))
+    grad_out = scatter_parity(out_rows)
+    in_sum.set_base(out_rows)
+    result.send_last(in_sum.base)
+    result.set_base(in_sum.base)
     inner_in = sum_all(inner_in.reshape(rows // 128, 128), "col").reshape(rows, 1) / factor_in
-    in_cot = sum_cols(lambda j: dot(low, block(w_in, j), 1, 1))
+    in_cot = in_sum.total()
     gin_part = jnp.sum(in_cot * tokens32 * factor_in, axis=0)
     grad_tokens = middle_cot + factor_in * gain_in * in_cot - tokens32 * (factor_in**3 * inner_in / feat)
+    qk_rows = own_rows(normed, qk, after(qk_got, out_rows, gin_part, grad_up))
+    grad_qk = scatter_parity(qk_rows)
+    layer_out = (middle + live * result.total()).astype(bf16)
 
     def own_cols(part):
+        part = by_place(part[None], chunk)[0]
         return lax.dynamic_update_slice_in_dim(jnp.zeros((feat,), f32), part, col * width, 0)
 
     sizes = [feat, feat, dh]
     wide = sum_all(jnp.concatenate([own_cols(gin_part), own_cols(gmid_part), ghead[0]]).reshape(-1, 128), "col")
     small = sum_all(jnp.concatenate([wide, gconv.reshape(-1, 128)], 0), "row")
     wide, gconv = small[: wide.shape[0]].reshape(-1), small[wide.shape[0] :].reshape(gconv.shape)
-    g_in = grad_in.astype(f32)
+    vb_rows = own_rows(normed, vb, after(vb_got, qk_rows, small, layer_out, grad_tokens, grad_out))
+    grad_vb = scatter_parity(vb_rows)
+    g_qk, g_vb = grad_qk.astype(f32), grad_vb.astype(f32)
     return (
-        layer_out,
-        grad_tokens,
+        by_place(layer_out, chunk),
+        by_place(grad_tokens, chunk),
         wide[:feat],
-        g_in[:, :hd],
-        g_in[:, hd : 2 * hd],
-        g_in[:, 2 * hd : 3 * hd],
+        g_qk[:, :hd],
+        g_qk[:, hd:],
+        g_vb[:, :hd],
         gconv[:, :hd],
         gconv[:, hd : 2 * hd],
         gconv[:, 2 * hd :],
-        g_in[:, 3 * hd : 3 * hd + beta_weight.shape[1]],
+        g_vb[:, hd : hd + beta_weight.shape[1]],
         wide[2 * feat :],
         grad_out.astype(f32).T,
         wide[feat : 2 * feat],

time: 1090 us -> 818 us (0.75)
  waiting for transfers between devices: 744 us -> 382 us
  Pallas kernels: 79.7 us -> 291 us
  matrix products: 170 us -> 0 us
  local copies, waits for them, and re-layouts: 31.3 us -> 61.4 us
  starting transfers between devices: 17.7 us -> 34.8 us
    reduce_scatter x5 -> x6, waiting for transfers between devices: 337 us -> 55.8 us  [scatter_parity(): lax.psum_scatter(part, 'row', scatter_dimension=0, tiled=True, axis_index...]
    pallas_call x0 -> x29, Pallas kernels: none -> 211 us  [the longest x17 130 us: tile_call(): pl.pallas_call(kernel, grid=grid, in_specs=specs, out_specs=out_specs, ou...]
    all_gather x4 -> x6, waiting for transfers between devices: 229 us -> 40.1 us  [gather_parity(): lax.all_gather(shard, 'row', axis=0, tiled=True, axis_index_groups=parity...]
    dot_general x26 -> x0, matrix products: 170 us -> none  [dot(): lax.dot_general(a, b, (((ca,), (cb,)), ((), ())), preferred_element_type=...]
    ppermute x33 -> x44, waiting for transfers between devices: 177 us -> 284 us  [swap(): return lax.ppermute(x, axis, [(i, i ^ bit) for i in range(n)])]
    unnamed x94 -> x130, local copies, waits for them, and re-layouts: 24.5 us -> 48.1 us
    ppermute x33 -> x44, starting transfers between devices: 17.1 us -> 33.9 us  [swap(): return lax.ppermute(x, axis, [(i, i ^ bit) for i in range(n)])]
  transfers between devices with their start and end apart: 42 -> 56, of which waited for: 21 -> 25; matrix products, arithmetic and copies ran while one was open for 14% -> 6% of each run, Pallas kernels for 7% -> 34%
where the time goes in v2:
time: 818 us; the launch traced here: 809 us
  waiting for transfers between devices  382 us (47%)
  Pallas kernels  291 us (36%)
  local copies, waits for them, and re-layouts  61.4 us (8%)
  starting transfers between devices  34.8 us (4%)
  other arithmetic  23.1 us (3%)
  between operations  16.2 us (2%)
    ppermute x44, waiting for transfers between devices, swap(): return lax.ppermute(x, axis, [(i, i ^ bit) for i in range(n)])  284 us
    pallas_call x17, Pallas kernels, tile_call(): pl.pallas_call(kernel, grid=grid, in_specs=specs, out_specs=out_specs, ou...  130 us
    pallas_call x12, Pallas kernels, tile_call(): pl.pallas_call(kernel, grid_spec=grid_spec, out_shape=outs, **params)  81.9 us
    reduce_scatter x6, waiting for transfers between devices, scatter_parity(): lax.psum_scatter(part, 'row', scatter_dimension=0, tiled=True, axis_index...  55.8 us
    unnamed x130, local copies, waits for them, and re-layouts  48.1 us
    all_gather x6, waiting for transfers between devices, gather_parity(): lax.all_gather(shard, 'row', axis=0, tiled=True, axis_index_groups=parity...  40.1 us
    pallas_call x1, Pallas kernels, mixer_backward(): pl.pallas_call(functools.partial(bwd_kernel, heads, dh), grid=(steps,), i...  36.9 us
    ppermute x44, starting transfers between devices, swap(): return lax.ppermute(x, axis, [(i, i ^ bit) for i in range(n)])  33.9 us
  transfers between devices with their start and end apart: 56, of which 25 were waited for; matrix products, arithmetic and copies ran while one was open for 6% of the time, Pallas kernels for 34%

profile of v2, /device:TPU:0, one launch (start us, length us, event | category | flops | bytes accessed | tf_op | source)
XLA Modules:
  0.0 808.5 jit_solution(1637636921258423267)
XLA Ops:
  20.1 23.8 %collective-permute-done.4.refs_2_ = bf16[1024,512]{1,0:T(8,128)(2,1)} collective-permute-done((bf16[1024,512]{1,0:T(8,128)(2,1)S(1)}, bf16[1024,512]{1,0:T(8,128)(2,1)}, u32[]{:S(2)}, u32[]{:S(2)}) %collective-permute-start.4) | collective-permute-done | bytes 1048608 | tf_op jit(solution)/shard_map/ppermute | solution.py:270
  44.5 21.0 %collective-permute-done.1.refs_2_ = bf16[1024,512]{1,0:T(8,128)(2,1)S(1)} collective-permute-done((bf16[1024,512]{1,0:T(8,128)(2,1)S(1)}, bf16[1024,512]{1,0:T(8,128)(2,1)S(1)}, u32[]{:S(2)}, u32[]{:S(2)}) %collective-permute-start.1) | collective-permute-done | bytes 1048608 | tf_op jit(solution)/shard_map/ppermute | solution.py:270
  88.4 21.3 %all-gather.7.cloned.1.call-done.refs_1_.refs_3_ = bf16[1024,512]{1,0:T(8,128)(2,1)} async-done(((bf16[256,512]{1,0:T(8,128)(2,1)}), bf16[1024,512]{1,0:T(8,128)(2,1)}) %all-gather.7.cloned.1.call-update) | async-done | bytes 1048592 | tf_op jit(solution)/shard_map/all_gather | solution.py:552
  111.2 52.3 %collective-permute-done.7.refs_3_.refs_2_.refs_4_ = bf16[1024,1664]{1,0:T(8,128)(2,1)S(1)} collective-permute-done((bf16[1024,1664]{1,0:T(8,128)(2,1)}, bf16[1024,1664]{1,0:T(8,128)(2,1)S(1)}, u32[]{:S(2)}, u32[]{:S(2)}) %collective-permute-start.7) | collective-permute-done | bytes 3407904 | tf_op jit(solution)/shard_map/ppermute | solution.py:270
  165.3 13.0 %halves.3.x_ref.prev_ref = f32[1024,1664]{1,0:T(8,128)} custom-call(bf16[1024,2048]{1,0:T(8,128)(2,1)} %copy-done.1, bf16[1024,1664]{1,0:T(8,128)(2,1)} %all-gather.9.cloned.1.call-done.refs_1_.refs_3_, bf16[1024,2048]{1,0:T(8,128)(2,1)} %copy-done.1, bf16[1024,1664]{1,0:T(8,128)(2,1)} %copy-done.22), custom_call_target="tpu_custom_call" | custom-call | tf_op jit(solution)/shard_map/halves/pallas_call | solution.py:405
  180.6 33.5 %mixer_forward.1 = (bf16[1024,512]{1,0:T(8,128)(2,1)S(1)}, f32[1024,512]{1,0:T(8,128)S(1)}, f32[1024,512]{1,0:T(8,128)S(1)}, f32[8,4,128,128]{3,2,1,0:T(8,128)S(1)}, f32[8,4,128,128]{3,2,1,0:T(8,128)S(1)}) custom-call(f32[1024,1664]{1,0:T(8,128)} %halves.3.x_ref.prev_ref, f32[4,1536]{1,0:T(4,128)S(1)} %constant_dynamic-update-slice_fusion.conv_ref, ...), custom_call_target="tpu_custom_call" | custom-call | tf_op jit(solution)/shard_map/mixer_forward/pallas_call | solution.py:201
  242.2 17.2 %collective-permute-done.11 = bf16[1024,512]{1,0:T(8,128)(2,1)S(1)} collective-permute-done((bf16[1024,512]{1,0:T(8,128)(2,1)}, bf16[1024,512]{1,0:T(8,128)(2,1)S(1)}, u32[]{:S(2)}, u32[]{:S(2)}) %collective-permute-start.11) | collective-permute-done | bytes 1048608 | tf_op jit(solution)/shard_map/ppermute | solution.py:270
  264.2 23.0 %collective-permute-done.14.refs_2_ = bf16[1024,512]{1,0:T(8,128)(2,1)S(1)} collective-permute-done((bf16[1024,512]{1,0:T(8,128)(2,1)S(1)}, bf16[1024,512]{1,0:T(8,128)(2,1)S(1)}, u32[]{:S(2)}, u32[]{:S(2)}) %collective-permute-start.14) | collective-permute-done | bytes 1048608 | tf_op jit(solution)/shard_map/ppermute | solution.py:270
  294.0 11.6 %halves.4.refs_4_ = bf16[1024,1408]{1,0:T(8,128)(2,1)} custom-call(bf16[1024,2048]{1,0:T(8,128)(2,1)} %copy-done, bf16[1024,1408]{1,0:T(8,128)(2,1)} %all-gather.11.cloned.1.call-done.refs_1_.refs_3_, bf16[1024,2048]{1,0:T(8,128)(2,1)} %copy-done, bf16[1024,1408]{1,0:T(8,128)(2,1)} %collective-permute-done.12.refs_3_.refs_2_.refs_4_), custom_call_target="tpu_custom_call" | custom-call | tf_op jit(solution)/shard_map/halves/pallas_call | solution.py:405
  308.3 12.1 %hidden.1 = (bf16[1024,1408]{1,0:T(8,128)(2,1)}, bf16[1024,1408]{1,0:T(8,128)(2,1)}) custom-call(bf16[1024,2048]{1,0:T(8,128)(2,1)} %copy-done, bf16[1024,2048]{1,0:T(8,128)(2,1)} %copy-done, bf16[1024,1408]{1,0:T(8,128)(2,1)} %all-gather.13.cloned.1.call-done.refs_2_.refs_6_.refs_8_.refs_4_, ...), custom_call_target="tpu_custom_call" | custom-call | tf_op jit(solution)/shard_map/hidden/pallas_call | solution.py:405
  320.4 6.9 rows.12
  329.1 18.8 %all-gather.17.cloned.1.call-done.refs_3_.refs_2_.refs_4_ = bf16[1024,1408]{1,0:T(8,128)(2,1)} async-done(((bf16[256,1408]{1,0:T(8,128)(2,1)}), bf16[1024,1408]{1,0:T(8,128)(2,1)}) %all-gather.17.cloned.1.call-update) | async-done | bytes 2883600 | tf_op jit(solution)/shard_map/all_gather | solution.py:552
  347.9 14.3 %cots.1 = (bf16[1024,1408]{1,0:T(8,128)(2,1)}, bf16[1024,1408]{1,0:T(8,128)(2,1)}, f32[1024,1]{1,0:T(8,128)}) custom-call(bf16[1024,2048]{1,0:T(8,128)(2,1)} %copy-done.2, bf16[1024,2048]{1,0:T(8,128)(2,1)} %copy-done.2, bf16[1024,1408]{1,0:T(8,128)(2,1)} %all-gather.15.cloned.1.call-done.refs_2_.refs_1_.refs_3_, ...), custom_call_target="tpu_custom_call" | custom-call | tf_op jit(solution)/shard_map/cots/pallas_call | solution.py:405
  362.2 11.9 %piece.15 = (bf16[1024,512]{1,0:T(8,128)(2,1)}, bf16[1024,512]{1,0:T(8,128)(2,1)}) custom-call(s32[2]{0:T(128)} %pad_add_fusion.me_ref, bf16[1024,1408]{1,0:T(8,128)(2,1)} %get-tuple-element.102.refs_0_.right_ref, bf16[1024,1408]{1,0:T(8,128)(2,1)} %all-gather.11.cloned.1.call-done.refs_1_.refs_3_, ...), custom_call_target="tpu_custom_call" | custom-call | tf_op jit(solution)/shard_map/piece/pallas_call | solution.py:409
  374.6 6.9 rows.13
  382.5 7.9 piece.16
  390.4 7.1 rows.14
  398.5 8.1 piece.17
  406.6 7.5 rows.15
  417.8 22.8 %collective-permute-done.21 = f32[8,128]{1,0:T(8,128)S(1)} collective-permute-done((f32[8,128]{1,0:T(8,128)S(1)}, f32[8,128]{1,0:T(8,128)S(1)}, u32[]{:S(2)}, u32[]{:S(2)}) %collective-permute-start.21) | collective-permute-done | bytes 4128 | tf_op jit(solution)/shard_map/ppermute | solution.py:270
  447.6 23.7 %collective-permute-done.24.refs_2_ = bf16[1024,512]{1,0:T(8,128)(2,1)S(1)} collective-permute-done((bf16[1024,512]{1,0:T(8,128)(2,1)S(1)}, bf16[1024,512]{1,0:T(8,128)(2,1)S(1)}, u32[]{:S(2)}, u32[]{:S(2)}) %collective-permute-start.24) | collective-permute-done | bytes 1048608 | tf_op jit(solution)/shard_map/ppermute | solution.py:270
  471.3 7.7 piece.18
  491.7 14.1 %collective-permute-done.26.refs_0_ = bf16[1024,1408]{1,0:T(8,128)(2,1)} collective-permute-done((bf16[1024,1408]{1,0:T(8,128)(2,1)}, bf16[1024,1408]{1,0:T(8,128)(2,1)}, u32[]{:S(2)}, u32[]{:S(2)}) %collective-permute-start.26) | collective-permute-done | bytes 2883616 | tf_op jit(solution)/shard_map/ppermute | solution.py:270
  505.8 7.4 rows.17
  522.9 36.9 %mixer_backward.1 = (bf16[1024,1664]{1,0:T(8,128)(2,1)S(1)}, f32[4,1536]{1,0:T(4,128)S(1)}, f32[1,128]{1,0:T(1,128)S(1)}, f32[1024,1]{1,0:T(8,128)S(1)}) custom-call(f32[1024,1664]{1,0:T(8,128)} %halves.3.x_ref.prev_ref, f32[1024,1664]{1,0:T(8,128)} %halves.3.x_ref.prev_ref, f32[4,1536]{1,0:T(4,128)S(1)} %constant_dynamic-update-slice_fusion.conv_ref, ...), custom_call_target="tpu_custom_call" | custom-call | tf_op jit(solution)/shard_map/mixer_backward/pallas_call | solution.py:233
  577.7 7.4 rows.20
  585.1 8.5 %piece.19 = (bf16[1024,512]{1,0:T(8,128)(2,1)}, bf16[1024,512]{1,0:T(8,128)(2,1)}) custom-call(s32[2]{0:T(128)} %pad_add_fusion.me_ref, bf16[1024,1664]{1,0:T(8,128)(2,1)} %copy-done.4, bf16[1024,1664]{1,0:T(8,128)(2,1)} %all-gather.9.cloned.1.call-done.refs_1_.refs_3_, bf16[1024,1664]{1,0:T(8,128)(2,1)} %copy-done.22, ...), custom_call_target="tpu_custom_call" | custom-call | tf_op jit(solution)/shard_map/piece/pallas_call | solution.py:409
  605.7 23.2 %collective-permute-done.35 = f32[8,128]{1,0:T(8,128)S(1)} collective-permute-done((f32[8,128]{1,0:T(8,128)S(1)}, f32[8,128]{1,0:T(8,128)S(1)}, u32[]{:S(2)}, u32[]{:S(2)}) %collective-permute-start.35) | collective-permute-done | bytes 4128 | tf_op jit(solution)/shard_map/ppermute | solution.py:270
  656.7 17.6 %collective-permute-done.37 = f32[33,128]{1,0:T(8,128)S(1)} collective-permute-done((f32[33,128]{1,0:T(8,128)S(1)}, f32[33,128]{1,0:T(8,128)S(1)}, u32[]{:S(2)}, u32[]{:S(2)}) %collective-permute-start.37) | collective-permute-done | bytes 16928 | tf_op jit(solution)/shard_map/ppermute | solution.py:270
  691.3 16.9 %collective-permute-done.41 = f32[81,128]{1,0:T(8,128)S(1)} collective-permute-done((f32[81,128]{1,0:T(8,128)S(1)}, f32[81,128]{1,0:T(8,128)S(1)}, u32[]{:S(2)}, u32[]{:S(2)}) %collective-permute-start.41) | collective-permute-done | bytes 41504 | tf_op jit(solution)/shard_map/ppermute | solution.py:270
  740.0 14.2 %reduce-scatter.17.cloned.1.call-done = bf16[256,640]{1,0:T(8,128)(2,1)} async-done(((bf16[1024,640]{1,0:T(8,128)(2,1)}), bf16[256,640]{1,0:T(8,128)(2,1)}) %reduce-scatter.17.cloned.1.call-update) | async-done | bytes 327696 | tf_op jit(solution)/shard_map/reduce_scatter | solution.py:556
  757.5 41.6 %reduce-scatter.13.cloned.1.call-done = bf16[256,1024]{1,0:T(8,128)(2,1)} async-done(((bf16[1024,1024]{1,0:T(8,128)(2,1)}), bf16[256,1024]{1,0:T(8,128)(2,1)}) %reduce-scatter.13.cloned.1.call-update) | async-done | bytes 524304 | tf_op jit(solution)/shard_map/reduce_scatter | solution.py:556
  (331 shorter events, 232.3 us)
Async XLA Ops:
  7.2 79.4 %all-gather.9.cloned.1.call-start = ((), (), s32[]{:S(2)}) async-start(), calls=%async_computation.7 | async-start | bytes 4259840 | tf_op jit(solution)/shard_map/all_gather | solution.py:552
  10.3 99.4 %all-gather.7.cloned.1.call-start = ((), (), s32[]{:S(2)}) async-start(), calls=%async_computation.6 | async-start | bytes 1310720 | tf_op jit(solution)/shard_map/all_gather | solution.py:552
  11.2 167.0 %all-gather.11.cloned.1.call-start = ((), (), s32[]{:S(2)}) async-start(), calls=%async_computation.8 | async-start | bytes 3604480 | tf_op jit(solution)/shard_map/all_gather | solution.py:552
  11.9 223.5 %all-gather.13.cloned.1.call-start = ((), (), s32[]{:S(2)}) async-start(), calls=%async_computation.9 | async-start | bytes 3604480 | tf_op jit(solution)/shard_map/all_gather | solution.py:552
  12.5 316.6 %all-gather.15.cloned.1.call-start = ((), (), s32[]{:S(2)}) async-start(), calls=%async_computation.10 | async-start | bytes 3604480 | tf_op jit(solution)/shard_map/all_gather | solution.py:552
  20.0 45.5 %collective-permute-start.1 = (bf16[1024,512]{1,0:T(8,128)(2,1)S(1)}, bf16[1024,512]{1,0:T(8,128)(2,1)S(1)}, u32[]{:S(2)}, u32[]{:S(2)}) collective-permute-start(bf16[1024,512]{1,0:T(8,128)(2,1)S(1)} %pad_maximum_fusion.1.refs_0_), channel_id=1, source_target_pairs={{0,2},{1,3},{2,0},{3,1},{4,6},{5,7},{6,4},{7,5},{8,10},{9,11},{10,... | collective-permute-start | bytes 3145736 | tf_op jit(solution)/shard_map/ppermute | solution.py:270
  20.1 49.5 %collective-permute-start.3 = (bf16[1024,512]{1,0:T(8,128)(2,1)S(1)}, bf16[1024,512]{1,0:T(8,128)(2,1)}, u32[]{:S(2)}, u32[]{:S(2)}) collective-permute-start(bf16[1024,512]{1,0:T(8,128)(2,1)S(1)} %fusion.9.refs_0_), channel_id=1, source_target_pairs={{0,1},{1,0},{2,3},{3,2},{4,5},{5,4},{6,7},{7,6},{8,9},{9,8},{10,11... | collective-permute-start | bytes 3145736 | tf_op jit(solution)/shard_map/ppermute | solution.py:270
  43.9 30.4 %collective-permute-start = (bf16[1024,512]{1,0:T(8,128)(2,1)S(1)}, bf16[1024,512]{1,0:T(8,128)(2,1)}, u32[]{:S(2)}, u32[]{:S(2)}) collective-permute-start(bf16[1024,512]{1,0:T(8,128)(2,1)S(1)} %pad_maximum_fusion.1.refs_0_), channel_id=1, source_target_pairs={{0,1},{1,0},{2,3},{3,2},{4,5},{5,4},{6,7},{7,6},{8,9},{9,8},{10,11... | collective-permute-start | bytes 3145736 | tf_op jit(solution)/shard_map/ppermute | solution.py:270
  86.6 76.8 %collective-permute-start.7 = (bf16[1024,1664]{1,0:T(8,128)(2,1)}, bf16[1024,1664]{1,0:T(8,128)(2,1)S(1)}, u32[]{:S(2)}, u32[]{:S(2)}) collective-permute-start(bf16[1024,1664]{1,0:T(8,128)(2,1)} %all-gather.9.cloned.1.call-done.refs_1_.refs_3_), channel_id=1, source_target_pairs={{0,4},{4,0},{8,12},{12,8},{16,20},{20,16},{24,28},{28,24},{1,5},{5... | collective-permute-start | bytes 10223624 | tf_op jit(solution)/shard_map/ppermute | solution.py:270
  88.3 259.6 %all-gather.17.cloned.1.call-start = ((), (), s32[]{:S(2)}) async-start(), calls=%async_computation.11 | async-start | bytes 3604480 | tf_op jit(solution)/shard_map/all_gather | solution.py:552
  109.7 110.9 %collective-permute-start.8 = (bf16[1024,512]{1,0:T(8,128)(2,1)}, bf16[1024,512]{1,0:T(8,128)(2,1)}, u32[]{:S(2)}, u32[]{:S(2)}) collective-permute-start(bf16[1024,512]{1,0:T(8,128)(2,1)} %all-gather.7.cloned.1.call-done.refs_1_.refs_3_), channel_id=1, source_target_pairs={{0,4},{4,0},{8,12},{12,8},{16,20},{20,16},{24,28},{28,24},{1,5},{5... | collective-permute-start | bytes 3145736 | tf_op jit(solution)/shard_map/ppermute | solution.py:270
  178.2 83.1 %collective-permute-start.12 = (bf16[1024,1408]{1,0:T(8,128)(2,1)}, bf16[1024,1408]{1,0:T(8,128)(2,1)}, u32[]{:S(2)}, u32[]{:S(2)}) collective-permute-start(bf16[1024,1408]{1,0:T(8,128)(2,1)} %all-gather.11.cloned.1.call-done.refs_1_.refs_3_), channel_id=1, source_target_pairs={{0,4},{4,0},{8,12},{12,8},{16,20},{20,16},{24,28},{28,24},{1,5},{5... | collective-permute-start | bytes 8650760 | tf_op jit(solution)/shard_map/ppermute | solution.py:270
  235.5 72.8 %collective-permute-start.16 = (bf16[1024,1408]{1,0:T(8,128)(2,1)}, bf16[1024,1408]{1,0:T(8,128)(2,1)}, u32[]{:S(2)}, u32[]{:S(2)}) collective-permute-start(bf16[1024,1408]{1,0:T(8,128)(2,1)} %all-gather.13.cloned.1.call-done.refs_2_.refs_6_.refs_8_.refs_4_), channel_id=1, source_target_pairs={{0,4},{4,0},{8,12},{12,8},{16,20},{20,16},{24,28},{28,24},{1,5},{5... | collective-permute-start | bytes 8650760 | tf_op jit(solution)/shard_map/ppermute | solution.py:270
  236.1 341.6 %reduce-scatter.9.cloned.1.call-start = ((), (), s32[]{:S(2)}) async-start(), calls=%async_computation.13 | async-start | bytes 3604480 | tf_op jit(solution)/shard_map/reduce_scatter | solution.py:556
  327.3 79.3 %collective-permute-start.20 = (bf16[1024,1408]{1,0:T(8,128)(2,1)}, bf16[1024,1408]{1,0:T(8,128)(2,1)}, u32[]{:S(2)}, u32[]{:S(2)}) collective-permute-start(bf16[1024,1408]{1,0:T(8,128)(2,1)} %rows.12), channel_id=1, source_target_pairs={{0,4},{4,0},{8,12},{12,8},{16,20},{20,16},{24,28},{28,24},{1,5},{5... | collective-permute-start | bytes 8650760 | tf_op jit(solution)/shard_map/ppermute | solution.py:270
  414.1 218.3 %reduce-scatter.7.cloned.1.call-start = ((), (), s32[]{:S(2)}) async-start(), calls=%async_computation.12 | async-start | bytes 3604480 | tf_op jit(solution)/shard_map/reduce_scatter | solution.py:556
  415.3 27.5 %collective-permute-start.19 = (bf16[1024,512]{1,0:T(8,128)(2,1)S(1)}, bf16[1024,512]{1,0:T(8,128)(2,1)}, u32[]{:S(2)}, u32[]{:S(2)}) collective-permute-start(bf16[1024,512]{1,0:T(8,128)(2,1)S(1)} %copy-done.38), channel_id=1, source_target_pairs={{0,2},{1,3},{2,0},{3,1},{4,6},{5,7},{6,4},{7,5},{8,10},{9,11},{10,... | collective-permute-start | bytes 3145736 | tf_op jit(solution)/shard_map/ppermute | solution.py:270
  440.6 65.2 %collective-permute-start.26 = (bf16[1024,1408]{1,0:T(8,128)(2,1)}, bf16[1024,1408]{1,0:T(8,128)(2,1)}, u32[]{:S(2)}, u32[]{:S(2)}) collective-permute-start(bf16[1024,1408]{1,0:T(8,128)(2,1)} %rows.13), channel_id=1, source_target_pairs={{0,4},{4,0},{8,12},{12,8},{16,20},{20,16},{24,28},{28,24},{1,5},{5... | collective-permute-start | bytes 8650760 | tf_op jit(solution)/shard_map/ppermute | solution.py:270
  447.6 31.4 %collective-permute-start.23 = (bf16[1024,512]{1,0:T(8,128)(2,1)S(1)}, bf16[1024,512]{1,0:T(8,128)(2,1)S(1)}, u32[]{:S(2)}, u32[]{:S(2)}) collective-permute-start(bf16[1024,512]{1,0:T(8,128)(2,1)S(1)} %multiply_convert_fusion.refs_0_), channel_id=1, source_target_pairs={{0,1},{1,0},{2,3},{3,2},{4,5},{5,4},{6,7},{7,6},{8,9},{9,8},{10,11... | collective-permute-start | bytes 3145736 | tf_op jit(solution)/shard_map/ppermute | solution.py:270
  513.2 199.0 %reduce-scatter.11.cloned.1.call-start = ((), (), s32[]{:S(2)}) async-start(), calls=%async_computation.14 | async-start | bytes 3604480 | tf_op jit(solution)/shard_map/reduce_scatter | solution.py:556
  513.2 64.4 %collective-permute-start.28 = (bf16[1024,1408]{1,0:T(8,128)(2,1)}, bf16[1024,1408]{1,0:T(8,128)(2,1)}, u32[]{:S(2)}, u32[]{:S(2)}) collective-permute-start(bf16[1024,1408]{1,0:T(8,128)(2,1)} %rows.14), channel_id=1, source_target_pairs={{0,4},{4,0},{8,12},{12,8},{16,20},{20,16},{24,28},{28,24},{1,5},{5... | collective-permute-start | bytes 8650760 | tf_op jit(solution)/shard_map/ppermute | solution.py:270
  585.0 133.3 %reduce-scatter.15.cloned.1.call-start = ((), (), s32[]{:S(2)}) async-start(), calls=%async_computation.16 | async-start | bytes 1310720 | tf_op jit(solution)/shard_map/reduce_scatter | solution.py:556
  593.6 37.3 %collective-permute-start.27 = (bf16[1024,512]{1,0:T(8,128)(2,1)}, bf16[1024,512]{1,0:T(8,128)(2,1)}, u32[]{:S(2)}, u32[]{:S(2)}) collective-permute-start(bf16[1024,512]{1,0:T(8,128)(2,1)} %rows.16), channel_id=1, source_target_pairs={{0,4},{4,0},{8,12},{12,8},{16,20},{20,16},{24,28},{28,24},{1,5},{5... | collective-permute-start | bytes 3145736 | tf_op jit(solution)/shard_map/ppermute | solution.py:270
  595.0 41.7 %collective-permute-start.30 = (bf16[1024,512]{1,0:T(8,128)(2,1)}, bf16[1024,512]{1,0:T(8,128)(2,1)}, u32[]{:S(2)}, u32[]{:S(2)}) collective-permute-start(bf16[1024,512]{1,0:T(8,128)(2,1)} %get-tuple-element.120), channel_id=1, source_target_pairs={{0,1},{1,0},{2,3},{3,2},{4,5},{5,4},{6,7},{7,6},{8,9},{9,8},{10,11... | collective-permute-start | bytes 3145736 | tf_op jit(solution)/shard_map/ppermute | solution.py:270
  595.3 47.6 %collective-permute-start.32 = (bf16[1024,512]{1,0:T(8,128)(2,1)}, bf16[1024,512]{1,0:T(8,128)(2,1)}, u32[]{:S(2)}, u32[]{:S(2)}) collective-permute-start(bf16[1024,512]{1,0:T(8,128)(2,1)} %get-tuple-element.108), channel_id=1, source_target_pairs={{0,1},{1,0},{2,3},{3,2},{4,5},{5,4},{6,7},{7,6},{8,9},{9,8},{10,11... | collective-permute-start | bytes 3145736 | tf_op jit(solution)/shard_map/ppermute | solution.py:270
  603.4 46.6 %collective-permute-start.34 = (bf16[1024,512]{1,0:T(8,128)(2,1)}, bf16[1024,512]{1,0:T(8,128)(2,1)}, u32[]{:S(2)}, u32[]{:S(2)}) collective-permute-start(bf16[1024,512]{1,0:T(8,128)(2,1)} %piece.20), channel_id=1, source_target_pairs={{0,2},{1,3},{2,0},{3,1},{4,6},{5,7},{6,4},{7,5},{8,10},{9,11},{10,... | collective-permute-start | bytes 3145736 | tf_op jit(solution)/shard_map/ppermute | solution.py:270
  630.1 55.2 %collective-permute-start.31 = (bf16[1024,512]{1,0:T(8,128)(2,1)}, bf16[1024,512]{1,0:T(8,128)(2,1)}, u32[]{:S(2)}, u32[]{:S(2)}) collective-permute-start(bf16[1024,512]{1,0:T(8,128)(2,1)} %get-tuple-element.107), channel_id=1, source_target_pairs={{0,1},{1,0},{2,3},{3,2},{4,5},{5,4},{6,7},{7,6},{8,9},{9,8},{10,11... | collective-permute-start | bytes 3145736 | tf_op jit(solution)/shard_map/ppermute | solution.py:270
  630.9 81.2 %collective-permute-start.42 = (bf16[1024,1024]{1,0:T(8,128)(2,1)}, bf16[1024,1024]{1,0:T(8,128)(2,1)}, u32[]{:S(2)}, u32[]{:S(2)}) collective-permute-start(bf16[1024,1024]{1,0:T(8,128)(2,1)} %rows.18), channel_id=1, source_target_pairs={{0,4},{4,0},{8,12},{12,8},{16,20},{20,16},{24,28},{28,24},{1,5},{5... | collective-permute-start | bytes 6291464 | tf_op jit(solution)/shard_map/ppermute | solution.py:270
  648.5 60.3 %collective-permute-start.33 = (bf16[1024,512]{1,0:T(8,128)(2,1)}, bf16[1024,512]{1,0:T(8,128)(2,1)}, u32[]{:S(2)}, u32[]{:S(2)}) collective-permute-start(bf16[1024,512]{1,0:T(8,128)(2,1)} %piece.23), channel_id=1, source_target_pairs={{0,2},{1,3},{2,0},{3,1},{4,6},{5,7},{6,4},{7,5},{8,10},{9,11},{10,... | collective-permute-start | bytes 3145736 | tf_op jit(solution)/shard_map/ppermute | solution.py:270
  650.0 104.2 %reduce-scatter.17.cloned.1.call-start = ((), (), s32[]{:S(2)}) async-start(), calls=%async_computation.17 | async-start | bytes 1638400 | tf_op jit(solution)/shard_map/reduce_scatter | solution.py:556
  656.0 62.3 %collective-permute-start.43 = (bf16[1024,640]{1,0:T(8,128)(2,1)}, bf16[1024,640]{1,0:T(8,128)(2,1)S(1)}, u32[]{:S(2)}, u32[]{:S(2)}) collective-permute-start(bf16[1024,640]{1,0:T(8,128)(2,1)} %rows.19), channel_id=1, source_target_pairs={{0,4},{4,0},{8,12},{12,8},{16,20},{20,16},{24,28},{28,24},{1,5},{5... | collective-permute-start | bytes 3932168 | tf_op jit(solution)/shard_map/ppermute | solution.py:270
  724.1 74.9 %reduce-scatter.13.cloned.1.call-start = ((), (), s32[]{:S(2)}) async-start(), calls=%async_computation.15 | async-start | bytes 2621440 | tf_op jit(solution)/shard_map/reduce_scatter | solution.py:556
  (80 other events, 1152.4 us)
Sparse Core Ops, SparseCore 0:
  10.4 70.5 all-gather.8
  83.1 26.5 all-gather.6
  111.2 58.6 all-gather.10
  171.4 57.8 all-gather.12
  230.7 57.8 all-gather.14
  290.0 57.8 all-gather.16
  414.2 54.8 reduce-scatter.8
  513.3 54.8 reduce-scatter.6
  585.2 54.8 reduce-scatter.10
  650.1 24.1 reduce-scatter.14
  724.3 29.8 reduce-scatter.16
  756.4 42.6 reduce-scatter.12

commit v3 on v2

--- a/solution.py
+++ b/solution.py
@@ -8,7 +8,7 @@
 
 CHUNK = 128
 EPS = 1e-6
-FREE = pl.CostEstimate(flops=0, bytes_accessed=0, transcendentals=0)
+FREE = pl.CostEstimate(flops=2**20, bytes_accessed=2**18, transcendentals=0)
 bf16 = jnp.bfloat16
 f32 = jnp.float32
 
@@ -26,7 +26,7 @@
 
 
 def sigmoid(x):
-    return 1.0 / (1.0 + jnp.exp(-x))
+    return 0.5 * jnp.tanh(0.5 * x) + 0.5
 
 
 def masks(n):
@@ -215,7 +215,7 @@
             jax.ShapeDtypeStruct((steps, heads, dh, dh), f32),
         ],
         scratch_shapes=[pltpu.VMEM((heads, dh, dh), f32), pltpu.VMEM((8, 3 * hd), f32)],
-        compiler_params=pltpu.CompilerParams(vmem_limit_bytes=40 * 2**20),
+        compiler_params=pltpu.CompilerParams(vmem_limit_bytes=60 * 2**20),
         cost_estimate=FREE,
         name="mixer_forward",
     )(proj, conv, gain)
@@ -255,7 +255,7 @@
             jax.ShapeDtypeStruct((rows, 1), f32),
         ],
         scratch_shapes=[pltpu.VMEM((heads, dh, dh), f32), pltpu.VMEM((8, 3 * hd), f32)],
-        compiler_params=pltpu.CompilerParams(vmem_limit_bytes=40 * 2**20),
+        compiler_params=pltpu.CompilerParams(vmem_limit_bytes=60 * 2**20),
         cost_estimate=FREE,
         name="mixer_backward",
     )(proj, proj, conv, gain, mixed_cot, o, fresh, inv, states)
@@ -298,14 +298,17 @@
         self.terms, self.block = terms, block
         self.kept, self.got = list(range(lax.axis_size("col"))), {}
 
-    def pieces(self, js, dtype, earlier):
+    def pieces(self, js, dtypes, earlier):
         (left, pair), rest = self.terms[0], self.terms[1:]
-        gots = [self.got.get(j) for j in js]
-        return piece_call([(after(left, *earlier), pair)] + rest, self.block, js, gots, dtype)
+        gots = [self.got.pop(j, None) for j in js]
+        return piece_call([(after(left, *earlier), pair)] + rest, self.block, js, gots, dtypes)
 
     def send(self, bit, *earlier):
         js = [j for j in self.kept if j & bit]
-        sent = self.pieces(js, bf16, earlier)
+        last = bit > 1 and 2 * bit == lax.axis_size("col")
+        sent = list(self.pieces(js + [0] * last, [bf16] * len(js) + [f32] * last, earlier))
+        if last:
+            self.base = sent.pop()
         for j, low in zip(js, sent):
             got, base = swap(low, "col", bit), j ^ bit
             self.got[base] = got if base not in self.got else self.got[base].astype(f32) + got.astype(f32)
@@ -314,21 +317,13 @@
 
     def send_last(self, *earlier):
         bit = 2
-        while 2 * bit < lax.axis_size("col"):
+        while bit < lax.axis_size("col"):
             earlier = self.send(bit, *earlier)
             bit *= 2
-        first = self.got.pop(0)
-        sent = self.send(bit, *earlier)
-        self.last = self.got[0]
-        self.got[0] = first
-        return sent
-
-    def set_base(self, *earlier):
-        self.base = self.pieces([0], f32, earlier)[0]
-        return self.base
+        return earlier
 
     def total(self):
-        return self.base + self.last.astype(f32)
+        return self.base + self.got[0].astype(f32)
 
 
 def norm_kernel(width, me_ref, *refs):
@@ -373,7 +368,7 @@
             out_specs=[pl.BlockSpec((TILE, o.shape[1]), lambda i, m: (i, 0)) for o in outs],
         ),
         out_shape=outs,
-        compiler_params=pltpu.CompilerParams(vmem_limit_bytes=24 * 2**20),
+        compiler_params=pltpu.CompilerParams(vmem_limit_bytes=60 * 2**20),
         cost_estimate=FREE,
         name=name,
     )(me, *pieces, *extra)
@@ -394,12 +389,12 @@
     return lax.dot_general(a, b, (((ca,), (cb,)), ((), ())), preferred_element_type=f32)
 
 
-FREE = pl.CostEstimate(flops=0, bytes_accessed=0, transcendentals=0)
+FREE = pl.CostEstimate(flops=2**20, bytes_accessed=2**18, transcendentals=0)
 
 
 def tile_call(kernel, arrays, specs, outs, out_specs, grid, name, me=None):
     params = dict(
-        compiler_params=pltpu.CompilerParams(vmem_limit_bytes=56 * 2**20), cost_estimate=FREE, name=name
+        compiler_params=pltpu.CompilerParams(vmem_limit_bytes=48 * 2**20), cost_estimate=FREE, name=name
     )
     if me is None:
         return pl.pallas_call(kernel, grid=grid, in_specs=specs, out_specs=out_specs, out_shape=outs, **params)(*arrays)
@@ -501,7 +496,7 @@
             out[:, p * width : (p + 1) * width] = total.astype(out.dtype)
 
 
-def piece_call(terms, block, js, gots, dtype):
+def piece_call(terms, block, js, gots, dtypes):
     rows = terms[0][0].shape[0]
     me = jnp.stack([lax.axis_index("col") ^ j for j in js]).astype(jnp.int32)
     arrays, specs = [], []
@@ -516,27 +511,30 @@
         arrays += gots
         specs += [row_tile(2 * block)] * len(js)
     kernel = functools.partial(piece_kernel, len(terms), len(js), has_got)
-    outs = [jax.ShapeDtypeStruct((rows, 2 * block), dtype)] * len(js)
+    outs = [jax.ShapeDtypeStruct((rows, 2 * block), dtype) for dtype in dtypes]
     return tile_call(kernel, arrays, specs, outs, [row_tile(2 * block)] * len(js), (rows // TILE,), "piece", me)
 
 
 def rows_kernel(left_ref, right_ref, *refs):
     total = dot(left_ref[...], right_ref[...], 0, 0)
-    if len(refs) > 1:
-        total = total + refs[0][...].astype(f32)
-    refs[-1][...] = total.astype(bf16)
-
-
-def rows_call(left, right, which, got=None):
-    rows, half, width = left.shape[0], left.shape[1] // 2, right.shape[1]
-    tile = 2 * TILE
-    steps = half // tile
-    arrays = [left, right] + ([] if got is None else [got])
-    specs = [pl.BlockSpec((rows, tile), lambda i: (0, which * steps + i)), whole(right.shape)]
+    gots, out = refs[:-1], refs[-1]
+    if len(gots) < 2:
+        out[...] = (total + gots[0][...].astype(f32) if gots else total).astype(bf16)
+        return
+    for n, got in enumerate(gots):
+
+        @pl.when(pl.program_id(0) == n)
+        def _(got=got):
+            out[...] = (total + got[...].astype(f32)).astype(bf16)
+
+
+def rows_call(left, right, first, count, gots=()):
+    rows, tile, width = left.shape[0], left.shape[1] // 4, right.shape[1]
+    specs = [pl.BlockSpec((rows, tile), lambda i: (0, first + i)), whole(right.shape)]
     out = pl.BlockSpec((tile, width), lambda i: (i, 0))
-    specs += [] if got is None else [out]
-    return tile_call(rows_kernel, arrays, specs, jax.ShapeDtypeStruct((half, width), bf16), out,
-                     (steps,), "rows")
+    specs += [out] if len(gots) == 1 else [whole((tile, width))] * len(gots)
+    return tile_call(rows_kernel, [left, right, *gots], specs, jax.ShapeDtypeStruct((count * tile, width), bf16), out,
+                     (count,), "rows")
 
 
 def parity_groups():
@@ -556,12 +554,15 @@
     return lax.psum_scatter(part, "row", scatter_dimension=0, tiled=True, axis_index_groups=parity_groups())
 
 
-def other_rows(left, right):
-    return rows_call(left, right, 1)
-
-
-def own_rows(left, right, got):
-    return rows_call(left, right, 0, got)
+def trade_rows(left, right, parts=1):
+    count = 2 // parts
+    sent = [rows_call(left, right, 2 + part * count, count) for part in range(parts)]
+    return sent, [swap(part, "row", 1) for part in sent]
+
+
+def own_rows(left, right, gots, *earlier):
+    first = after(gots[0], *gots[1:], *earlier)
+    return rows_call(left, right, 0, 2, [first, *gots[1:]])
 
 
 def flip(first, second):
@@ -617,8 +618,8 @@
 
     half = feat // 2
     normed, factor_in = join_norm(spread_cols(tokens), norm_in)
-    ffn_cot = join(spread_cols(cotangent * live_low))
-    in_mine = after(in_mine, normed, ffn_cot, down_side)
+    ffn_cot = join(spread_cols(after(cotangent * live_low, down_side)))
+    in_mine = after(in_mine, normed, ffn_cot)
     in_other, out_other = swap(in_mine, "row", 1), swap(out_mine, "row", 1)
     proj = halves(after(normed, out_mine), [(0, in_mine), (1, in_other)])
     gate_mine = after(gate_mine, proj)
@@ -632,67 +633,51 @@
     sent = branch.send_last(*sent)
     up_mine = after(up_mine, *sent)
     up_other = swap(up_mine, "row", 1)
-    branch.set_base(*sent)
     middle = tokens32 + live * after(branch.total(), gate_other)
     mid_low = middle.astype(bf16)
     normed_mid, factor_mid = join_norm(spread_cols(mid_low), after(norm_mid, up_mine))
     w_gate, w_up = (gate_mine, gate_other), (up_mine, up_other)
     gate = halves(normed_mid, [(0, gate_mine), (1, gate_other)], bf16)
     up, hidden = hidden_call(after(normed_mid, gate), w_up, gate)
-    down_sent = other_rows(ffn_cot, hidden)
-    down_got = swap(down_sent, "row", 1)
+    down_sent, down_got = trade_rows(ffn_cot, hidden)
+    down_sent = down_sent[0]
     w_down = after(down_mine, down_sent), after(down_other, down_sent)
     gate_cot, up_cot, inner_mid = cots_call(ffn_cot, w_down, gate, up)
     inner_mid = sum_all(inner_mid.reshape(rows // 128, 128), "col").reshape(rows, 1) / factor_mid
     mid_sum = ColSum([(gate_cot, w_gate), (up_cot, w_up)], block)
     sent = mid_sum.send(1)
-    gate_sent = other_rows(after(normed_mid, *sent), gate_cot)
-    gate_got = swap(gate_sent, "row", 1)
-    sent = mid_sum.send_last(gate_sent)
-    up_sent = other_rows(after(normed_mid, *sent), up_cot)
-    up_got = swap(up_sent, "row", 1)
-    mid_sum.set_base(up_sent)
-    down_rows = own_rows(ffn_cot, hidden, after(down_got, mid_sum.base))
+    gate_sent, gate_got = trade_rows(after(normed_mid, *sent), gate_cot, 2)
+    mid_sum.send_last(inner_mid, gate_sent[0])
+    up_sent, up_got = trade_rows(after(normed_mid, gate_got[0]), up_cot)
+    mid_sum.got[0] = after(mid_sum.got[0], *up_sent)
+    down_rows = own_rows(ffn_cot, hidden, down_got, mid_sum.got[0])
     grad_down = scatter_parity(down_rows)
-    mid_cot = after(mid_sum.total(), down_rows)
+    mid_cot = mid_sum.total()
 
     mid32 = mid_low.astype(f32)
     gmid_part = jnp.sum(mid_cot * mid32 * factor_mid, axis=0)
     middle_cot = cotangent.astype(f32) + factor_mid * gain_mid * mid_cot - mid32 * (factor_mid**3 * inner_mid / feat)
     branch_low = (live * middle_cot).astype(bf16)
     pieces = spread_cols(branch_low)
-    result = ColSum([(hidden, w_down)], block)
-    sent = result.send(1, branch_low)
-    pieces[0] = after(pieces[0], *sent)
+    gate_rows = own_rows(normed_mid, gate_cot, gate_got, pieces[2])
+    grad_gate = scatter_parity(gate_rows)
     branch_cot = join(pieces)
     mixed_cot = halves(branch_cot, [(0, out_mine), (1, out_other)])
-    out_sent = other_rows(after(branch_cot, mixed_cot), mixed)
-    out_got = swap(out_sent, "row", 1)
-    gate_rows = own_rows(normed_mid, gate_cot, after(gate_got, out_sent, down_rows))
-    grad_gate = scatter_parity(gate_rows)
-    mixed_cot = after(mixed_cot, out_sent, gate_rows)
+    out_sent, out_got = trade_rows(after(branch_cot, mixed_cot), mixed)
+    mixed_cot = after(mixed_cot, *out_sent)
     low, gconv, ghead, inner_in = mixer_backward(proj, conv, gain, mixed_cot, kept, heads, dh)
-    cut = 2 * hd
-    qk, vb = low[:, :cut], low[:, cut:]
-    qk_sent, vb_sent = other_rows(normed, qk), other_rows(normed, vb)
-    qk_got, vb_got = swap(qk_sent, "row", 1), swap(vb_sent, "row", 1)
-    up_rows = own_rows(normed_mid, up_cot, after(up_got, qk_sent, vb_sent, grad_down))
+    low_sent, low_got = trade_rows(normed, low, 2)
+    inner_in = sum_all(inner_in.reshape(rows // 128, 128), "col").reshape(rows, 1) / factor_in
+    in_sum = ColSum([(low, w_in)], block)
+    sent = in_sum.send(1, *low_sent)
+    in_sum.send_last(inner_in, *sent)
+    up_rows = own_rows(normed_mid, up_cot, up_got, *out_got, in_sum.base, grad_down)
     grad_up = scatter_parity(up_rows)
-    in_sum = ColSum([(low, w_in)], block)
-    sent = in_sum.send(1, up_rows)
-    sent = in_sum.send_last(*sent)
-    out_rows = own_rows(branch_cot, mixed, after(out_got, grad_gate, *sent))
+    out_rows = own_rows(branch_cot, mixed, out_got, grad_gate, up_rows, low_got[0], in_sum.got[0])
     grad_out = scatter_parity(out_rows)
-    in_sum.set_base(out_rows)
-    result.send_last(in_sum.base)
-    result.set_base(in_sum.base)
-    inner_in = sum_all(inner_in.reshape(rows // 128, 128), "col").reshape(rows, 1) / factor_in
     in_cot = in_sum.total()
     gin_part = jnp.sum(in_cot * tokens32 * factor_in, axis=0)
     grad_tokens = middle_cot + factor_in * gain_in * in_cot - tokens32 * (factor_in**3 * inner_in / feat)
-    qk_rows = own_rows(normed, qk, after(qk_got, out_rows, gin_part, grad_up))
-    grad_qk = scatter_parity(qk_rows)
-    layer_out = (middle + live * result.total()).astype(bf16)
 
     def own_cols(part):
         part = by_place(part[None], chunk)[0]
@@ -700,22 +685,46 @@
 
     sizes = [feat, feat, dh]
     wide = sum_all(jnp.concatenate([own_cols(gin_part), own_cols(gmid_part), ghead[0]]).reshape(-1, 128), "col")
-    small = sum_all(jnp.concatenate([wide, gconv.reshape(-1, 128)], 0), "row")
+    small = jnp.concatenate([wide, gconv.reshape(-1, 128)], 0)
+    bits = bits_down(lax.axis_size("row"))
+    for bit in bits[:-1]:
+        small = small + swap(small, "row", bit)
+    low_rows = own_rows(normed, low, low_got, out_rows, grad_up, small, grad_tokens)
+    grad_low = scatter_parity(low_rows)
+    in_cot = in_sum.total()
+    gin_part = jnp.sum(in_cot * tokens32 * factor_in, axis=0)
+    grad_tokens = middle_cot + factor_in * gain_in * in_cot - tokens32 * (factor_in**3 * inner_in / feat)
+
+    def own_cols(part):
+        part = by_place(part[None], chunk)[0]
+        return lax.dynamic_update_slice_in_dim(jnp.zeros((feat,), f32), part, col * width, 0)
+
+    sizes = [feat, feat, dh]
+    wide = sum_all(jnp.concatenate([own_cols(gin_part), own_cols(gmid_part), ghead[0]]).reshape(-1, 128), "col")
+    small = jnp.concatenate([wide, gconv.reshape(-1, 128)], 0)
+    bits = bits_down(lax.axis_size("row"))
+    for bit in bits[:-1]:
+        small = small + swap(small, "row", bit)
+    low_rows = own_rows(normed, low, low_got, out_rows, grad_up, small, grad_tokens)
+    grad_low = scatter_parity(low_rows)
+    result = ColSum([(hidden, w_down)], block)
+    sent = result.send(1, low_rows)
+    result.send_last(*sent)
+    layer_out = (middle + live * result.total()).astype(bf16)
+    small = small + swap(small, "row", bits[-1])
     wide, gconv = small[: wide.shape[0]].reshape(-1), small[wide.shape[0] :].reshape(gconv.shape)
-    vb_rows = own_rows(normed, vb, after(vb_got, qk_rows, small, layer_out, grad_tokens, grad_out))
-    grad_vb = scatter_parity(vb_rows)
-    g_qk, g_vb = grad_qk.astype(f32), grad_vb.astype(f32)
+    g_low = grad_low.astype(f32)
     return (
         by_place(layer_out, chunk),
         by_place(grad_tokens, chunk),
         wide[:feat],
-        g_qk[:, :hd],
-        g_qk[:, hd:],
-        g_vb[:, :hd],
+        g_low[:, :hd],
+        g_low[:, hd : 2 * hd],
+        g_low[:, 2 * hd : 3 * hd],
         gconv[:, :hd],
         gconv[:, hd : 2 * hd],
         gconv[:, 2 * hd :],
-        g_vb[:, hd : hd + beta_weight.shape[1]],
+        g_low[:, 3 * hd : 3 * hd + beta_weight.shape[1]],
         wide[2 * feat :],
         grad_out.astype(f32).T,
         wide[feat : 2 * feat],

time: 818 us -> 777 us (0.950)
  waiting for transfers between devices: 382 us -> 347 us
  Pallas kernels: 291 us -> 279 us
    reduce_scatter x6 -> x5, waiting for transfers between devices: 55.8 us -> 6.9 us  [scatter_parity(): lax.psum_scatter(part, 'row', scatter_dimension=0, tiled=True, axis_index...]
    pallas_call x12 -> x8, Pallas kernels: 81.9 us -> 63 us  [tile_call(): pl.pallas_call(kernel, grid_spec=grid_spec, out_shape=outs, **params)]
    all_gather x6, waiting for transfers between devices: 40.1 us -> 58.2 us  [gather_parity(): lax.all_gather(shard, 'row', axis=0, tiled=True, axis_index_groups=parity...]
    pallas_call x4, Pallas kernels: 9.25 us -> 21.4 us  [join_call(): pl.pallas_call(functools.partial(kernel, width), grid_spec=pltpu.Prefetch...]
    ppermute x44 -> x45, starting transfers between devices: 33.9 us -> 40.8 us  [swap(): return lax.ppermute(x, axis, [(i, i ^ bit) for i in range(n)])]
    ppermute x44 -> x45, waiting for transfers between devices: 284 us -> 280 us  [swap(): return lax.ppermute(x, axis, [(i, i ^ bit) for i in range(n)])]
    unnamed x130 -> x176, local copies, waits for them, and re-layouts: 48.1 us -> 48.2 us
  transfers between devices with their start and end apart: 56 -> 56, of which waited for: 25 -> 29; matrix products, arithmetic and copies ran while one was open for 6% -> 6% of each run, Pallas kernels for 34% -> 36%
where the time goes in v3:
time: 777 us; the launch traced here: 767 us
  waiting for transfers between devices  347 us (45%)
  Pallas kernels  279 us (36%)
  local copies, waits for them, and re-layouts  58.7 us (8%)
  starting transfers between devices  41.2 us (5%)
  other arithmetic  25.2 us (3%)
  between operations  15.9 us (2%)
    ppermute x45, waiting for transfers between devices, swap(): return lax.ppermute(x, axis, [(i, i ^ bit) for i in range(n)])  280 us
    pallas_call x17, Pallas kernels, tile_call(): pl.pallas_call(kernel, grid=grid, in_specs=specs, out_specs=out_specs, ou...  123 us
    pallas_call x8, Pallas kernels, tile_call(): pl.pallas_call(kernel, grid_spec=grid_spec, out_shape=outs, **params)  63 us
    all_gather x6, waiting for transfers between devices, gather_parity(): lax.all_gather(shard, 'row', axis=0, tiled=True, axis_index_groups=parity...  58.2 us
    unnamed x176, local copies, waits for them, and re-layouts  48.2 us
    ppermute x45, starting transfers between devices, swap(): return lax.ppermute(x, axis, [(i, i ^ bit) for i in range(n)])  40.8 us
    pallas_call x1, Pallas kernels, mixer_backward(): pl.pallas_call(functools.partial(bwd_kernel, heads, dh), grid=(steps,), i...  37.5 us
    pallas_call x1, Pallas kernels, mixer_forward(): pl.pallas_call(functools.partial(fwd_kernel, heads, dh), grid=(steps,), i...  34.2 us
  transfers between devices with their start and end apart: 56, of which 29 were waited for; matrix products, arithmetic and copies ran while one was open for 6% of the time, Pallas kernels for 36%

profile of v3, /device:TPU:0, one launch (start us, length us, event | category | flops | bytes accessed | tf_op | source)
XLA Modules:
  0.0 767.1 jit_solution(10875325428605347646)
XLA Ops:
  23.7 8.4 %collective-permute-done.3 = bf16[256,1408]{1,0:T(8,128)(2,1)} collective-permute-done((bf16[256,1408]{1,0:T(8,128)(2,1)S(1)}, bf16[256,1408]{1,0:T(8,128)(2,1)}, u32[]{:S(2)}, u32[]{:S(2)}) %collective-permute-start.3) | collective-permute-done | bytes 720928 | tf_op jit(solution)/shard_map/ppermute | solution.py:270
  33.9 13.4 %collective-permute-done.1.refs_2_ = bf16[1024,512]{1,0:T(8,128)(2,1)} collective-permute-done((bf16[1024,512]{1,0:T(8,128)(2,1)S(1)}, bf16[1024,512]{1,0:T(8,128)(2,1)}, u32[]{:S(2)}, u32[]{:S(2)}) %collective-permute-start.1) | collective-permute-done | bytes 1048608 | tf_op jit(solution)/shard_map/ppermute | solution.py:270
  47.9 20.4 %collective-permute-done.5.refs_2_ = bf16[1024,512]{1,0:T(8,128)(2,1)S(1)} collective-permute-done((bf16[1024,512]{1,0:T(8,128)(2,1)S(1)}, bf16[1024,512]{1,0:T(8,128)(2,1)S(1)}, u32[]{:S(2)}, u32[]{:S(2)}) %collective-permute-start.5) | collective-permute-done | bytes 1048608 | tf_op jit(solution)/shard_map/ppermute | solution.py:270
  82.5 27.2 %all-gather.7.cloned.1.call-done.refs_1_.refs_3_ = bf16[1024,512]{1,0:T(8,128)(2,1)} async-done(((bf16[256,512]{1,0:T(8,128)(2,1)}), bf16[1024,512]{1,0:T(8,128)(2,1)}) %all-gather.7.cloned.1.call-update) | async-done | bytes 1048592 | tf_op jit(solution)/shard_map/all_gather | solution.py:550
  111.1 46.7 %collective-permute-done.7.refs_3_.refs_2_.refs_4_ = bf16[1024,1664]{1,0:T(8,128)(2,1)} collective-permute-done((bf16[1024,1664]{1,0:T(8,128)(2,1)}, bf16[1024,1664]{1,0:T(8,128)(2,1)}, u32[]{:S(2)}, u32[]{:S(2)}) %collective-permute-start.7) | collective-permute-done | bytes 3407904 | tf_op jit(solution)/shard_map/ppermute | solution.py:270
  159.8 11.8 %halves.3.x_ref.prev_ref = f32[1024,1664]{1,0:T(8,128)} custom-call(bf16[1024,2048]{1,0:T(8,128)(2,1)} %get-tuple-element.79.refs_0_.refs_2_.left_ref, bf16[1024,1664]{1,0:T(8,128)(2,1)S(1)} %copy-done, bf16[1024,2048]{1,0:T(8,128)(2,1)} %get-tuple-element.79.refs_0_.refs_2_.left_ref, bf16[1024,1664]{1,0:T(8,128)(2,1)} %collective-permute-done.7.refs_3_.refs_2_.refs_4_), custom_call_target="tpu_custom_call" | custom-call | flops 1048576 | bytes 262144 | tf_op jit(solution)/shard_map/halves/pallas_call | solution.py:400
  173.9 34.2 %mixer_forward.1 = (bf16[1024,512]{1,0:T(8,128)(2,1)}, f32[1024,512]{1,0:T(8,128)}, f32[1024,512]{1,0:T(8,128)}, f32[8,4,128,128]{3,2,1,0:T(8,128)}, f32[8,4,128,128]{3,2,1,0:T(8,128)}) custom-call(f32[1024,1664]{1,0:T(8,128)} %halves.3.x_ref.prev_ref, f32[4,1536]{1,0:T(4,128)} %copy-done.71, f32[1,128]{1,0:T(1,128)} %bitcast.111), custom_call_target="tpu_custom_call" | custom-call | flops 1048576 | bytes 262144 | tf_op jit(solution)/shard_map/mixer_forward/pallas_call | solution.py:201
  230.7 17.1 %collective-permute-done.11 = bf16[1024,512]{1,0:T(8,128)(2,1)S(1)} collective-permute-done((bf16[1024,512]{1,0:T(8,128)(2,1)}, bf16[1024,512]{1,0:T(8,128)(2,1)S(1)}, u32[]{:S(2)}, u32[]{:S(2)}) %collective-permute-start.11) | collective-permute-done | bytes 1048608 | tf_op jit(solution)/shard_map/ppermute | solution.py:270
  252.7 23.0 %collective-permute-done.14.refs_2_ = bf16[1024,512]{1,0:T(8,128)(2,1)S(1)} collective-permute-done((bf16[1024,512]{1,0:T(8,128)(2,1)S(1)}, bf16[1024,512]{1,0:T(8,128)(2,1)S(1)}, u32[]{:S(2)}, u32[]{:S(2)}) %collective-permute-start.14) | collective-permute-done | bytes 1048608 | tf_op jit(solution)/shard_map/ppermute | solution.py:270
  284.5 9.4 %halves.4.refs_4_ = bf16[1024,1408]{1,0:T(8,128)(2,1)S(1)} custom-call(bf16[1024,2048]{1,0:T(8,128)(2,1)} %get-tuple-element.110.refs_0_.refs_2_.refs_1_.left_ref, bf16[1024,1408]{1,0:T(8,128)(2,1)S(1)} %copy-done.5, bf16[1024,2048]{1,0:T(8,128)(2,1)} %get-tuple-element.110.refs_0_.refs_2_.refs_1_.left_ref, ...), custom_call_target="tpu_custom_call" | custom-call | flops 1048576 | bytes 262144 | tf_op jit(solution)/shard_map/halves/pallas_call | solution.py:400
  295.5 7.3 collective-permute-done.16.refs_3_.refs_7_.refs_9_
  302.7 10.9 %hidden.1 = (bf16[1024,1408]{1,0:T(8,128)(2,1)S(1)}, bf16[1024,1408]{1,0:T(8,128)(2,1)S(1)}) custom-call(bf16[1024,2048]{1,0:T(8,128)(2,1)} %get-tuple-element.110.refs_0_.refs_2_.refs_1_.left_ref, bf16[1024,2048]{1,0:T(8,128)(2,1)} %get-tuple-element.110.refs_0_.refs_2_.refs_1_.left_ref, ...), custom_call_target="tpu_custom_call" | custom-call | flops 1048576 | bytes 262144 | tf_op jit(solution)/shard_map/hidden/pallas_call | solution.py:400
  315.1 6.8 rows.12
  323.4 24.5 %all-gather.17.cloned.1.call-done.refs_3_.refs_2_.refs_4_ = bf16[1024,1408]{1,0:T(8,128)(2,1)} async-done(((bf16[256,1408]{1,0:T(8,128)(2,1)}), bf16[1024,1408]{1,0:T(8,128)(2,1)}) %all-gather.17.cloned.1.call-update) | async-done | bytes 2883600 | tf_op jit(solution)/shard_map/all_gather | solution.py:550
  347.9 13.8 %cots.1 = (bf16[1024,1408]{1,0:T(8,128)(2,1)S(1)}, bf16[1024,1408]{1,0:T(8,128)(2,1)}, f32[1024,1]{1,0:T(8,128)S(1)}) custom-call(bf16[1024,2048]{1,0:T(8,128)(2,1)} %join.2.left_ref.refs_0_.refs_1_, bf16[1024,2048]{1,0:T(8,128)(2,1)} %join.2.left_ref.refs_0_.refs_1_, bf16[1024,1408]{1,0:T(8,128)(2,1)} %all-gather.15.cloned.1.call-done.refs_2_.refs_1_.refs_3_, ...), custom_call_target="tpu_custom_call" | custom-call | flops 1048576 | bytes 262144 | tf_op jit(solution)/shard_map/cots/pallas_call | solution.py:400
  361.7 12.0 %piece.10 = (bf16[1024,512]{1,0:T(8,128)(2,1)}, bf16[1024,512]{1,0:T(8,128)(2,1)}) custom-call(s32[2]{0:T(128)S(1)} %pad_add_fusion.1.me_ref, bf16[1024,1408]{1,0:T(8,128)(2,1)S(1)} %get-tuple-element.107.refs_0_.right_ref, bf16[1024,1408]{1,0:T(8,128)(2,1)} %all-gather.11.cloned.1.call-done.refs_1_.refs_3_, ...), custom_call_target="tpu_custom_call" | custom-call | flops 1048576 | bytes 262144 | tf_op jit(solution)/shard_map/piece/pallas_call | solution.py:404
  384.4 11.8 %piece.11 = (bf16[1024,512]{1,0:T(8,128)(2,1)S(1)}, f32[1024,512]{1,0:T(8,128)S(1)}) custom-call(s32[2]{0:T(128)S(1)} %pad_add_fusion.me_ref, bf16[1024,1408]{1,0:T(8,128)(2,1)} %copy-done.3, bf16[1024,1408]{1,0:T(8,128)(2,1)} %all-gather.11.cloned.1.call-done.refs_1_.refs_3_, bf16[1024,1408]{1,0:T(8,128)(2,1)} %collective-permute-done.12.refs_3_.refs_2_.refs_4_, ...), custom_call_target="tpu_custom_call" | custom-call | flops 1048576 | bytes 262144 | tf_op jit(solution)/shard_map/piece/pallas_call | solution.py:404
  399.0 17.5 %collective-permute-done.22.refs_0_ = bf16[512,1408]{1,0:T(8,128)(2,1)S(1)} collective-permute-done((bf16[512,1408]{1,0:T(8,128)(2,1)}, bf16[512,1408]{1,0:T(8,128)(2,1)S(1)}, u32[]{:S(2)}, u32[]{:S(2)}) %collective-permute-start.22) | collective-permute-done | bytes 1441824 | tf_op jit(solution)/shard_map/ppermute | solution.py:270
  416.5 16.9 %rows.14 = bf16[1024,1408]{1,0:T(8,128)(2,1)S(1)} custom-call(bf16[1024,2048]{1,0:T(8,128)(2,1)} %get-tuple-element.110.refs_0_.refs_2_.refs_1_.left_ref, bf16[1024,1408]{1,0:T(8,128)(2,1)S(1)} %copy-done.9), custom_call_target="tpu_custom_call" | custom-call | flops 1048576 | bytes 262144 | tf_op jit(solution)/shard_map/rows/pallas_call | solution.py:400
  453.4 27.9 %collective-permute-done.29.refs_1_ = bf16[512,1408]{1,0:T(8,128)(2,1)S(1)} collective-permute-done((bf16[512,1408]{1,0:T(8,128)(2,1)S(1)}, bf16[512,1408]{1,0:T(8,128)(2,1)S(1)}, u32[]{:S(2)}, u32[]{:S(2)}) %collective-permute-start.29) | collective-permute-done | bytes 1441824 | tf_op jit(solution)/shard_map/ppermute | solution.py:270
  481.3 7.5 rows.19
  509.9 37.5 %mixer_backward.1 = (bf16[1024,1664]{1,0:T(8,128)(2,1)}, f32[4,1536]{1,0:T(4,128)}, f32[1,128]{1,0:T(1,128)}, f32[1024,1]{1,0:T(8,128)}) custom-call(f32[1024,1664]{1,0:T(8,128)} %halves.3.x_ref.prev_ref, f32[1024,1664]{1,0:T(8,128)} %halves.3.x_ref.prev_ref, f32[4,1536]{1,0:T(4,128)} %copy-done.71, f32[1,128]{1,0:T(1,128)} %bitcast.112, ...), custom_call_target="tpu_custom_call" | custom-call | flops 1048576 | bytes 262144 | tf_op jit(solution)/shard_map/mixer_backward/pallas_call | solution.py:233
  557.5 8.2 %piece.12 = (bf16[1024,512]{1,0:T(8,128)(2,1)}, bf16[1024,512]{1,0:T(8,128)(2,1)}) custom-call(s32[2]{0:T(128)S(1)} %pad_add_fusion.1.me_ref, bf16[1024,1664]{1,0:T(8,128)(2,1)S(1)} %copy-done.2, bf16[1024,1664]{1,0:T(8,128)(2,1)} %all-gather.9.cloned.1.call-done.refs_1_.refs_3_, bf16[1024,1664]{1,0:T(8,128)(2,1)} %collective-permute-done.7.refs_3_.refs_2_.refs_4_, ...), custom_call_target="tpu_custom_call" | custom-call | flops 1048576 | bytes 262144 | tf_op jit(solution)/shard_map/piece/pallas_call | solution.py:404
  573.0 8.1 %piece.13 = (bf16[1024,512]{1,0:T(8,128)(2,1)S(1)}, f32[1024,512]{1,0:T(8,128)S(1)}) custom-call(s32[2]{0:T(128)S(1)} %pad_add_fusion.me_ref, bf16[1024,1664]{1,0:T(8,128)(2,1)} %get-tuple-element.125.right_ref.refs_0_, bf16[1024,1664]{1,0:T(8,128)(2,1)} %all-gather.9.cloned.1.call-done.refs_1_.refs_3_, ...), custom_call_target="tpu_custom_call" | custom-call | flops 1048576 | bytes 262144 | tf_op jit(solution)/shard_map/piece/pallas_call | solution.py:404
  583.4 8.3 %collective-permute-done.28.refs_0_ = bf16[1024,512]{1,0:T(8,128)(2,1)} collective-permute-done((bf16[1024,512]{1,0:T(8,128)(2,1)}, bf16[1024,512]{1,0:T(8,128)(2,1)}, u32[]{:S(2)}, u32[]{:S(2)}) %collective-permute-start.28) | collective-permute-done | bytes 1048608 | tf_op jit(solution)/shard_map/ppermute | solution.py:270
  602.9 35.8 %collective-permute-done.26.refs_0_ = bf16[512,1664]{1,0:T(8,128)(2,1)S(1)} collective-permute-done((bf16[512,1664]{1,0:T(8,128)(2,1)S(1)}, bf16[512,1664]{1,0:T(8,128)(2,1)S(1)}, u32[]{:S(2)}, u32[]{:S(2)}) %collective-permute-start.26) | collective-permute-done | bytes 1703968 | tf_op jit(solution)/shard_map/ppermute | solution.py:270
  663.9 18.1 %collective-permute-done.27.refs_1_ = bf16[512,1664]{1,0:T(8,128)(2,1)} collective-permute-done((bf16[512,1664]{1,0:T(8,128)(2,1)}, bf16[512,1664]{1,0:T(8,128)(2,1)}, u32[]{:S(2)}, u32[]{:S(2)}) %collective-permute-start.27) | collective-permute-done | bytes 1703968 | tf_op jit(solution)/shard_map/ppermute | solution.py:270
  683.5 8.9 %rows.23 = bf16[1024,1664]{1,0:T(8,128)(2,1)} custom-call(bf16[1024,2048]{1,0:T(8,128)(2,1)} %get-tuple-element.79.refs_0_.refs_2_.left_ref, bf16[1024,1664]{1,0:T(8,128)(2,1)} %get-tuple-element.125.right_ref.refs_0_, bf16[512,1664]{1,0:T(8,128)(2,1)S(1)} %copy-done.31, bf16[512,1664]{1,0:T(8,128)(2,1)} %collective-permute-done.27.refs_1_), custom_call_target="tpu_custom_call" | custom-call | flops 1048576 | bytes 262144 | tf_op jit(solution)/shard_map/rows/pallas_call | solution.py:400
  694.3 7.2 piece.14
  713.4 7.1 piece.15
  734.4 11.2 %collective-permute-done.43 = bf16[1024,512]{1,0:T(8,128)(2,1)} collective-permute-done((bf16[1024,512]{1,0:T(8,128)(2,1)}, bf16[1024,512]{1,0:T(8,128)(2,1)}, u32[]{:S(2)}, u32[]{:S(2)}) %collective-permute-start.43) | collective-permute-done | bytes 1048608 | tf_op jit(solution)/shard_map/ppermute | solution.py:270
  749.5 6.9 reduce-scatter.12.cloned.1.call-done
  (369 shorter events, 225.2 us)
Async XLA Ops:
  7.2 73.8 %all-gather.9.cloned.1.call-start = ((), (), s32[]{:S(2)}) async-start(), calls=%async_computation.6 | async-start | bytes 4259840 | tf_op jit(solution)/shard_map/all_gather | solution.py:550
  10.3 99.4 %all-gather.7.cloned.1.call-start = ((), (), s32[]{:S(2)}) async-start(), calls=%async_computation.5 | async-start | bytes 1310720 | tf_op jit(solution)/shard_map/all_gather | solution.py:550
  11.2 160.5 %all-gather.11.cloned.1.call-start = ((), (), s32[]{:S(2)}) async-start(), calls=%async_computation.7 | async-start | bytes 3604480 | tf_op jit(solution)/shard_map/all_gather | solution.py:550
  11.9 217.3 %all-gather.13.cloned.1.call-start = ((), (), s32[]{:S(2)}) async-start(), calls=%async_computation.8 | async-start | bytes 3604480 | tf_op jit(solution)/shard_map/all_gather | solution.py:550
  12.5 310.9 %all-gather.15.cloned.1.call-start = ((), (), s32[]{:S(2)}) async-start(), calls=%async_computation.9 | async-start | bytes 3604480 | tf_op jit(solution)/shard_map/all_gather | solution.py:550
  21.1 26.3 %collective-permute-start.1 = (bf16[1024,512]{1,0:T(8,128)(2,1)S(1)}, bf16[1024,512]{1,0:T(8,128)(2,1)}, u32[]{:S(2)}, u32[]{:S(2)}) collective-permute-start(bf16[1024,512]{1,0:T(8,128)(2,1)S(1)} %pad_maximum_fusion.1.refs_0_), channel_id=1, source_target_pairs={{0,2},{1,3},{2,0},{3,1},{4,6},{5,7},{6,4},{7,5},{8,10},{9,11},{10,... | collective-permute-start | bytes 3145736 | tf_op jit(solution)/shard_map/ppermute | solution.py:270
  32.2 36.1 %collective-permute-start.5 = (bf16[1024,512]{1,0:T(8,128)(2,1)S(1)}, bf16[1024,512]{1,0:T(8,128)(2,1)S(1)}, u32[]{:S(2)}, u32[]{:S(2)}) collective-permute-start(bf16[1024,512]{1,0:T(8,128)(2,1)S(1)} %fusion.9.refs_0_), channel_id=1, source_target_pairs={{0,2},{1,3},{2,0},{3,1},{4,6},{5,7},{6,4},{7,5},{8,10},{9,11},{10,... | collective-permute-start | bytes 3145736 | tf_op jit(solution)/shard_map/ppermute | solution.py:270
  33.9 35.1 %collective-permute-start = (bf16[1024,512]{1,0:T(8,128)(2,1)S(1)}, bf16[1024,512]{1,0:T(8,128)(2,1)}, u32[]{:S(2)}, u32[]{:S(2)}) collective-permute-start(bf16[1024,512]{1,0:T(8,128)(2,1)S(1)} %pad_maximum_fusion.1.refs_0_), channel_id=1, source_target_pairs={{0,1},{1,0},{2,3},{3,2},{4,5},{5,4},{6,7},{7,6},{8,9},{9,8},{10,11... | collective-permute-start | bytes 3145736 | tf_op jit(solution)/shard_map/ppermute | solution.py:270
  47.4 27.5 %collective-permute-start.4 = (bf16[1024,512]{1,0:T(8,128)(2,1)S(1)}, bf16[1024,512]{1,0:T(8,128)(2,1)}, u32[]{:S(2)}, u32[]{:S(2)}) collective-permute-start(bf16[1024,512]{1,0:T(8,128)(2,1)S(1)} %fusion.9.refs_0_), channel_id=1, source_target_pairs={{0,1},{1,0},{2,3},{3,2},{4,5},{5,4},{6,7},{7,6},{8,9},{9,8},{10,11... | collective-permute-start | bytes 3145736 | tf_op jit(solution)/shard_map/ppermute | solution.py:270
  80.9 76.9 %collective-permute-start.7 = (bf16[1024,1664]{1,0:T(8,128)(2,1)}, bf16[1024,1664]{1,0:T(8,128)(2,1)}, u32[]{:S(2)}, u32[]{:S(2)}) collective-permute-start(bf16[1024,1664]{1,0:T(8,128)(2,1)} %all-gather.9.cloned.1.call-done.refs_1_.refs_3_), channel_id=1, source_target_pairs={{0,4},{4,0},{8,12},{12,8},{16,20},{20,16},{24,28},{28,24},{1,5},{5... | collective-permute-start | bytes 10223624 | tf_op jit(solution)/shard_map/ppermute | solution.py:270
  82.4 265.5 %all-gather.17.cloned.1.call-start = ((), (), s32[]{:S(2)}) async-start(), calls=%async_computation.10 | async-start | bytes 3604480 | tf_op jit(solution)/shard_map/all_gather | solution.py:550
  109.7 98.5 %collective-permute-start.8 = (bf16[1024,512]{1,0:T(8,128)(2,1)}, bf16[1024,512]{1,0:T(8,128)(2,1)S(1)}, u32[]{:S(2)}, u32[]{:S(2)}) collective-permute-start(bf16[1024,512]{1,0:T(8,128)(2,1)} %all-gather.7.cloned.1.call-done.refs_1_.refs_3_), channel_id=1, source_target_pairs={{0,4},{4,0},{8,12},{12,8},{16,20},{20,16},{24,28},{28,24},{1,5},{5... | collective-permute-start | bytes 3145736 | tf_op jit(solution)/shard_map/ppermute | solution.py:270
  171.7 78.2 %collective-permute-start.12 = (bf16[1024,1408]{1,0:T(8,128)(2,1)}, bf16[1024,1408]{1,0:T(8,128)(2,1)}, u32[]{:S(2)}, u32[]{:S(2)}) collective-permute-start(bf16[1024,1408]{1,0:T(8,128)(2,1)} %all-gather.11.cloned.1.call-done.refs_1_.refs_3_), channel_id=1, source_target_pairs={{0,4},{4,0},{8,12},{12,8},{16,20},{20,16},{24,28},{28,24},{1,5},{5... | collective-permute-start | bytes 8650760 | tf_op jit(solution)/shard_map/ppermute | solution.py:270
  222.5 25.4 %collective-permute-start.11 = (bf16[1024,512]{1,0:T(8,128)(2,1)}, bf16[1024,512]{1,0:T(8,128)(2,1)S(1)}, u32[]{:S(2)}, u32[]{:S(2)}) collective-permute-start(bf16[1024,512]{1,0:T(8,128)(2,1)} %get-tuple-element.90), channel_id=1, source_target_pairs={{0,2},{1,3},{2,0},{3,1},{4,6},{5,7},{6,4},{7,5},{8,10},{9,11},{10,... | collective-permute-start | bytes 3145736 | tf_op jit(solution)/shard_map/ppermute | solution.py:270
  224.0 367.7 %reduce-scatter.8.cloned.1.call-start = ((), (), s32[]{:S(2)}) async-start(), calls=%async_computation.12 | async-start | bytes 3604480 | tf_op jit(solution)/shard_map/reduce_scatter | solution.py:554
  229.3 73.5 %collective-permute-start.16 = (bf16[1024,1408]{1,0:T(8,128)(2,1)}, bf16[1024,1408]{1,0:T(8,128)(2,1)}, u32[]{:S(2)}, u32[]{:S(2)}) collective-permute-start(bf16[1024,1408]{1,0:T(8,128)(2,1)} %all-gather.13.cloned.1.call-done.refs_2_.refs_6_.refs_8_), channel_id=1, source_target_pairs={{0,4},{4,0},{8,12},{12,8},{16,20},{20,16},{24,28},{28,24},{1,5},{5... | collective-permute-start | bytes 8650760 | tf_op jit(solution)/shard_map/ppermute | solution.py:270
  251.2 24.5 %collective-permute-start.14 = (bf16[1024,512]{1,0:T(8,128)(2,1)S(1)}, bf16[1024,512]{1,0:T(8,128)(2,1)S(1)}, u32[]{:S(2)}, u32[]{:S(2)}) collective-permute-start(bf16[1024,512]{1,0:T(8,128)(2,1)S(1)} %fusion.7.refs_0_), channel_id=1, source_target_pairs={{0,2},{1,3},{2,0},{3,1},{4,6},{5,7},{6,4},{7,5},{8,10},{9,11},{10,... | collective-permute-start | bytes 3145736 | tf_op jit(solution)/shard_map/ppermute | solution.py:270
  321.9 113.2 %collective-permute-start.35 = (bf16[1024,1408]{1,0:T(8,128)(2,1)}, bf16[1024,1408]{1,0:T(8,128)(2,1)}, u32[]{:S(2)}, u32[]{:S(2)}) collective-permute-start(bf16[1024,1408]{1,0:T(8,128)(2,1)} %rows.12), channel_id=1, source_target_pairs={{0,4},{4,0},{8,12},{12,8},{16,20},{20,16},{24,28},{28,24},{1,5},{5... | collective-permute-start | bytes 8650760 | tf_op jit(solution)/shard_map/ppermute | solution.py:270
  382.3 34.1 %collective-permute-start.22 = (bf16[512,1408]{1,0:T(8,128)(2,1)}, bf16[512,1408]{1,0:T(8,128)(2,1)S(1)}, u32[]{:S(2)}, u32[]{:S(2)}) collective-permute-start(bf16[512,1408]{1,0:T(8,128)(2,1)} %rows.13), channel_id=1, source_target_pairs={{0,4},{4,0},{8,12},{12,8},{16,20},{20,16},{24,28},{28,24},{1,5},{5... | collective-permute-start | bytes 4325384 | tf_op jit(solution)/shard_map/ppermute | solution.py:270
  397.5 37.6 %collective-permute-start.21 = (bf16[1024,512]{1,0:T(8,128)(2,1)S(1)}, bf16[1024,512]{1,0:T(8,128)(2,1)S(1)}, u32[]{:S(2)}, u32[]{:S(2)}) collective-permute-start(bf16[1024,512]{1,0:T(8,128)(2,1)S(1)} %get-tuple-element.109), channel_id=1, source_target_pairs={{0,2},{1,3},{2,0},{3,1},{4,6},{5,7},{6,4},{7,5},{8,10},{9,11},{10,... | collective-permute-start | bytes 3145736 | tf_op jit(solution)/shard_map/ppermute | solution.py:270
  443.1 196.8 %reduce-scatter.6.cloned.1.call-start = ((), (), s32[]{:S(2)}) async-start(), calls=%async_computation.11 | async-start | bytes 3604480 | tf_op jit(solution)/shard_map/reduce_scatter | solution.py:554
  448.1 33.2 %collective-permute-start.29 = (bf16[512,1408]{1,0:T(8,128)(2,1)S(1)}, bf16[512,1408]{1,0:T(8,128)(2,1)S(1)}, u32[]{:S(2)}, u32[]{:S(2)}) collective-permute-start(bf16[512,1408]{1,0:T(8,128)(2,1)S(1)} %rows.18), channel_id=1, source_target_pairs={{0,4},{4,0},{8,12},{12,8},{16,20},{20,16},{24,28},{28,24},{1,5},{5... | collective-permute-start | bytes 4325384 | tf_op jit(solution)/shard_map/ppermute | solution.py:270
  451.9 29.4 %collective-permute-start.24 = (bf16[1024,512]{1,0:T(8,128)(2,1)S(1)}, bf16[1024,512]{1,0:T(8,128)(2,1)}, u32[]{:S(2)}, u32[]{:S(2)}) collective-permute-start(bf16[1024,512]{1,0:T(8,128)(2,1)S(1)} %get-tuple-element.177.refs_0_), channel_id=1, source_target_pairs={{0,2},{1,3},{2,0},{3,1},{4,6},{5,7},{6,4},{7,5},{8,10},{9,11},{10,... | collective-permute-start | bytes 3145736 | tf_op jit(solution)/shard_map/ppermute | solution.py:270
  488.8 193.3 %reduce-scatter.10.cloned.1.call-start = ((), (), s32[]{:S(2)}) async-start(), calls=%async_computation.13 | async-start | bytes 3604480 | tf_op jit(solution)/shard_map/reduce_scatter | solution.py:554
  488.9 94.5 %collective-permute-start.30 = (bf16[1024,1408]{1,0:T(8,128)(2,1)}, bf16[1024,1408]{1,0:T(8,128)(2,1)}, u32[]{:S(2)}, u32[]{:S(2)}) collective-permute-start(bf16[1024,1408]{1,0:T(8,128)(2,1)} %copy-done.24), channel_id=1, source_target_pairs={{0,4},{4,0},{8,12},{12,8},{16,20},{20,16},{24,28},{28,24},{1,5},{5... | collective-permute-start | bytes 8650760 | tf_op jit(solution)/shard_map/ppermute | solution.py:270
  566.2 25.5 %collective-permute-start.28 = (bf16[1024,512]{1,0:T(8,128)(2,1)}, bf16[1024,512]{1,0:T(8,128)(2,1)}, u32[]{:S(2)}, u32[]{:S(2)}) collective-permute-start(bf16[1024,512]{1,0:T(8,128)(2,1)} %rows.15), channel_id=1, source_target_pairs={{0,4},{4,0},{8,12},{12,8},{16,20},{20,16},{24,28},{28,24},{1,5},{5... | collective-permute-start | bytes 3145736 | tf_op jit(solution)/shard_map/ppermute | solution.py:270
  598.9 129.2 %reduce-scatter.14.cloned.1.call-start = ((), (), s32[]{:S(2)}) async-start(), calls=%async_computation.15 | async-start | bytes 1310720 | tf_op jit(solution)/shard_map/reduce_scatter | solution.py:554
  600.3 38.4 %collective-permute-start.26 = (bf16[512,1664]{1,0:T(8,128)(2,1)S(1)}, bf16[512,1664]{1,0:T(8,128)(2,1)S(1)}, u32[]{:S(2)}, u32[]{:S(2)}) collective-permute-start(bf16[512,1664]{1,0:T(8,128)(2,1)S(1)} %copy-done.33), channel_id=1, source_target_pairs={{0,4},{4,0},{8,12},{12,8},{16,20},{20,16},{24,28},{28,24},{1,5},{5... | collective-permute-start | bytes 5111816 | tf_op jit(solution)/shard_map/ppermute | solution.py:270
  601.4 38.5 %collective-permute-start.36 = (bf16[1024,512]{1,0:T(8,128)(2,1)}, bf16[1024,512]{1,0:T(8,128)(2,1)}, u32[]{:S(2)}, u32[]{:S(2)}) collective-permute-start(bf16[1024,512]{1,0:T(8,128)(2,1)} %copy-done.38), channel_id=1, source_target_pairs={{0,2},{1,3},{2,0},{3,1},{4,6},{5,7},{6,4},{7,5},{8,10},{9,11},{10,... | collective-permute-start | bytes 3145736 | tf_op jit(solution)/shard_map/ppermute | solution.py:270
  643.8 112.6 %reduce-scatter.12.cloned.1.call-start = ((), (), s32[]{:S(2)}) async-start(), calls=%async_computation.14 | async-start | bytes 4259840 | tf_op jit(solution)/shard_map/reduce_scatter | solution.py:554
  644.1 37.9 %collective-permute-start.27 = (bf16[512,1664]{1,0:T(8,128)(2,1)}, bf16[512,1664]{1,0:T(8,128)(2,1)}, u32[]{:S(2)}, u32[]{:S(2)}) collective-permute-start(bf16[512,1664]{1,0:T(8,128)(2,1)} %copy-done.29), channel_id=1, source_target_pairs={{0,4},{4,0},{8,12},{12,8},{16,20},{20,16},{24,28},{28,24},{1,5},{5... | collective-permute-start | bytes 5111816 | tf_op jit(solution)/shard_map/ppermute | solution.py:270
  720.5 25.1 %collective-permute-start.43 = (bf16[1024,512]{1,0:T(8,128)(2,1)}, bf16[1024,512]{1,0:T(8,128)(2,1)}, u32[]{:S(2)}, u32[]{:S(2)}) collective-permute-start(bf16[1024,512]{1,0:T(8,128)(2,1)} %get-tuple-element.139), channel_id=1, source_target_pairs={{0,2},{1,3},{2,0},{3,1},{4,6},{5,7},{6,4},{7,5},{8,10},{9,11},{10,... | collective-permute-start | bytes 3145736 | tf_op jit(solution)/shard_map/ppermute | solution.py:270
  (103 other events, 978.6 us)
Sparse Core Ops, SparseCore 0:
  10.4 70.5 all-gather.8
  83.1 26.5 all-gather.6
  111.2 58.6 all-gather.10
  171.4 57.8 all-gather.12
  230.7 57.8 all-gather.14
  290.0 57.8 all-gather.16
  443.2 56.4 reduce-scatter.7
  502.0 56.0 reduce-scatter.5
  599.0 55.6 reduce-scatter.9
  657.4 26.9 reduce-scatter.13
  692.6 63.7 reduce-scatter.11

commit v4 on v3

--- a/solution.py
+++ b/solution.py
@@ -352,7 +352,7 @@
             out_ref[:, pl.ds(pl.multiple_of(start, half), half)] = piece[:, p * half : (p + 1) * half]
 
 
-TILE = 256
+TILE = 512
 
 
 def join_call(kernel, pieces, extra, outs, name):
@@ -515,26 +515,31 @@
     return tile_call(kernel, arrays, specs, outs, [row_tile(2 * block)] * len(js), (rows // TILE,), "piece", me)
 
 
-def rows_kernel(left_ref, right_ref, *refs):
+def rows_kernel(parts, left_ref, right_ref, *refs):
     total = dot(left_ref[...], right_ref[...], 0, 0)
     gots, out = refs[:-1], refs[-1]
-    if len(gots) < 2:
-        out[...] = (total + gots[0][...].astype(f32) if gots else total).astype(bf16)
-        return
-    for n, got in enumerate(gots):
-
-        @pl.when(pl.program_id(0) == n)
+    if not gots:
+        out[...] = total.astype(bf16)
+    start = 0
+    for got, part in zip(gots, parts):
+
+        @pl.when((pl.program_id(0) >= start) & (pl.program_id(0) < start + part))
         def _(got=got):
             out[...] = (total + got[...].astype(f32)).astype(bf16)
 
-
-def rows_call(left, right, first, count, gots=()):
-    rows, tile, width = left.shape[0], left.shape[1] // 4, right.shape[1]
+        start += part
+
+
+def rows_call(left, right, first, parts, tile, gots=()):
+    rows, width, count = left.shape[0], right.shape[1], sum(parts)
     specs = [pl.BlockSpec((rows, tile), lambda i: (0, first + i)), whole(right.shape)]
+    start = 0
+    for _, part in zip(gots, parts):
+        specs.append(pl.BlockSpec((tile, width), lambda i, s=start, p=part: (jnp.clip(i - s, 0, p - 1), 0)))
+        start += part
     out = pl.BlockSpec((tile, width), lambda i: (i, 0))
-    specs += [out] if len(gots) == 1 else [whole((tile, width))] * len(gots)
-    return tile_call(rows_kernel, [left, right, *gots], specs, jax.ShapeDtypeStruct((count * tile, width), bf16), out,
-                     (count,), "rows")
+    return tile_call(functools.partial(rows_kernel, parts), [left, right, *gots], specs,
+                     jax.ShapeDtypeStruct((count * tile, width), bf16), out, (count,), "rows")
 
 
 def parity_groups():
@@ -554,15 +559,36 @@
     return lax.psum_scatter(part, "row", scatter_dimension=0, tiled=True, axis_index_groups=parity_groups())
 
 
-def trade_rows(left, right, parts=1):
-    count = 2 // parts
-    sent = [rows_call(left, right, 2 + part * count, count) for part in range(parts)]
+def all_rows(left, right):
+    rows, tile, width = left.shape[0], left.shape[1] // 4, right.shape[1]
+    odd = (lax.axis_index("row") & 1).astype(jnp.int32).reshape(1)
+
+    def kernel(odd_ref, left_ref, right_ref, out_ref):
+        out_ref[...] = dot(left_ref[...], right_ref[...], 0, 0).astype(bf16)
+
+    return tile_call(kernel, [left, right], [pl.BlockSpec((rows, tile), lambda i, m: (0, i)), whole(right.shape)],
+                     jax.ShapeDtypeStruct((4 * tile, width), bf16),
+                     pl.BlockSpec((tile, width), lambda i, m: (2 * ((i // 2) ^ m[0]) + i % 2, 0)), (4,), "all_rows", odd)
+
+
+def scatter_rows(part):
+    even, odd = parity_groups()
+    return lax.psum_scatter(part, "row", scatter_dimension=0, tiled=True, axis_index_groups=[even + odd])
+
+
+def trade_rows(left, right, parts=(2,)):
+    tile = left.shape[1] // 2 // sum(parts)
+    sent, first = [], sum(parts)
+    for part in parts:
+        sent.append(rows_call(left, right, first, (part,), tile))
+        first += part
     return sent, [swap(part, "row", 1) for part in sent]
 
 
 def own_rows(left, right, gots, *earlier):
     first = after(gots[0], *gots[1:], *earlier)
-    return rows_call(left, right, 0, 2, [first, *gots[1:]])
+    tile = 512 if len(gots) == 1 else min(got.shape[0] for got in gots)
+    return rows_call(left, right, 0, tuple(got.shape[0] // tile for got in gots), tile, [first, *gots[1:]])
 
 
 def flip(first, second):
@@ -639,19 +665,17 @@
     w_gate, w_up = (gate_mine, gate_other), (up_mine, up_other)
     gate = halves(normed_mid, [(0, gate_mine), (1, gate_other)], bf16)
     up, hidden = hidden_call(after(normed_mid, gate), w_up, gate)
-    down_sent, down_got = trade_rows(ffn_cot, hidden)
-    down_sent = down_sent[0]
+    down_sent = all_rows(ffn_cot, hidden)
+    grad_down = scatter_rows(down_sent)
     w_down = after(down_mine, down_sent), after(down_other, down_sent)
     gate_cot, up_cot, inner_mid = cots_call(ffn_cot, w_down, gate, up)
     inner_mid = sum_all(inner_mid.reshape(rows // 128, 128), "col").reshape(rows, 1) / factor_mid
     mid_sum = ColSum([(gate_cot, w_gate), (up_cot, w_up)], block)
     sent = mid_sum.send(1)
-    gate_sent, gate_got = trade_rows(after(normed_mid, *sent), gate_cot, 2)
+    gate_sent, gate_got = trade_rows(after(normed_mid, *sent), gate_cot)
     mid_sum.send_last(inner_mid, gate_sent[0])
-    up_sent, up_got = trade_rows(after(normed_mid, gate_got[0]), up_cot)
+    up_sent, up_got = trade_rows(after(normed_mid, mid_sum.base), up_cot)
     mid_sum.got[0] = after(mid_sum.got[0], *up_sent)
-    down_rows = own_rows(ffn_cot, hidden, down_got, mid_sum.got[0])
-    grad_down = scatter_parity(down_rows)
     mid_cot = mid_sum.total()
 
     mid32 = mid_low.astype(f32)
@@ -666,14 +690,14 @@
     out_sent, out_got = trade_rows(after(branch_cot, mixed_cot), mixed)
     mixed_cot = after(mixed_cot, *out_sent)
     low, gconv, ghead, inner_in = mixer_backward(proj, conv, gain, mixed_cot, kept, heads, dh)
-    low_sent, low_got = trade_rows(normed, low, 2)
+    in_sum = ColSum([(low, w_in)], block)
+    sent = in_sum.send(1)
+    low_sent, low_got = trade_rows(after(normed, *sent), low)
     inner_in = sum_all(inner_in.reshape(rows // 128, 128), "col").reshape(rows, 1) / factor_in
-    in_sum = ColSum([(low, w_in)], block)
-    sent = in_sum.send(1, *low_sent)
-    in_sum.send_last(inner_in, *sent)
+    in_sum.send_last(inner_in, *low_sent)
     up_rows = own_rows(normed_mid, up_cot, up_got, *out_got, in_sum.base, grad_down)
     grad_up = scatter_parity(up_rows)
-    out_rows = own_rows(branch_cot, mixed, out_got, grad_gate, up_rows, low_got[0], in_sum.got[0])
+    out_rows = own_rows(branch_cot, mixed, out_got, grad_gate, up_rows)
     grad_out = scatter_parity(out_rows)
     in_cot = in_sum.total()
     gin_part = jnp.sum(in_cot * tokens32 * factor_in, axis=0)

time: 777 us -> 755 us (0.972)
  Pallas kernels: 279 us -> 257 us
    pallas_call x17 -> x13, Pallas kernels: 123 us -> 97.3 us  [tile_call(): pl.pallas_call(kernel, grid=grid, in_specs=specs, out_specs=out_specs, ou...]
    pallas_call x8 -> x9, Pallas kernels: 63 us -> 70 us  [tile_call(): pl.pallas_call(kernel, grid_spec=grid_spec, out_shape=outs, **params)]
    ppermute x45 -> x42, starting transfers between devices: 40.8 us -> 34.6 us  [swap(): return lax.ppermute(x, axis, [(i, i ^ bit) for i in range(n)])]
    ppermute x45 -> x42, waiting for transfers between devices: 280 us -> 284 us  [swap(): return lax.ppermute(x, axis, [(i, i ^ bit) for i in range(n)])]
    unnamed x176 -> x148, local copies, waits for them, and re-layouts: 48.2 us -> 45.8 us
  transfers between devices with their start and end apart: 56 -> 53, of which waited for: 29 -> 29; matrix products, arithmetic and copies ran while one was open for 6% -> 6% of each run, Pallas kernels for 36% -> 35%
where the time goes in v4:
time: 755 us; the launch traced here: 746 us
  waiting for transfers between devices  353 us (47%)
  Pallas kernels  257 us (34%)
  local copies, waits for them, and re-layouts  56.3 us (7%)
  starting transfers between devices  35.6 us (5%)
  other arithmetic  27.4 us (4%)
  between operations  15.9 us (2%)
    ppermute x42, waiting for transfers between devices, swap(): return lax.ppermute(x, axis, [(i, i ^ bit) for i in range(n)])  284 us
    pallas_call x13, Pallas kernels, tile_call(): pl.pallas_call(kernel, grid=grid, in_specs=specs, out_specs=out_specs, ou...  97.3 us
    pallas_call x9, Pallas kernels, tile_call(): pl.pallas_call(kernel, grid_spec=grid_spec, out_shape=outs, **params)  70 us
    all_gather x6, waiting for transfers between devices, gather_parity(): lax.all_gather(shard, 'row', axis=0, tiled=True, axis_index_groups=parity...  56.5 us
    unnamed x148, local copies, waits for them, and re-layouts  45.8 us
    pallas_call x1, Pallas kernels, mixer_backward(): pl.pallas_call(functools.partial(bwd_kernel, heads, dh), grid=(steps,), i...  37.5 us
    ppermute x42, starting transfers between devices, swap(): return lax.ppermute(x, axis, [(i, i ^ bit) for i in range(n)])  34.6 us
    pallas_call x1, Pallas kernels, mixer_forward(): pl.pallas_call(functools.partial(fwd_kernel, heads, dh), grid=(steps,), i...  34.2 us
  transfers between devices with their start and end apart: 53, of which 29 were waited for; matrix products, arithmetic and copies ran while one was open for 6% of the time, Pallas kernels for 35%

profile of v4, /device:TPU:0, one launch (start us, length us, event | category | flops | bytes accessed | tf_op | source)
XLA Modules:
  0.0 746.0 jit_solution(13142557277163324726)
XLA Ops:
  23.7 8.4 %collective-permute-done.3 = bf16[256,1408]{1,0:T(8,128)(2,1)} collective-permute-done((bf16[256,1408]{1,0:T(8,128)(2,1)S(1)}, bf16[256,1408]{1,0:T(8,128)(2,1)}, u32[]{:S(2)}, u32[]{:S(2)}) %collective-permute-start.3) | collective-permute-done | bytes 720928 | tf_op jit(solution)/shard_map/ppermute | solution.py:270
  33.9 13.4 %collective-permute-done.1.refs_2_ = bf16[1024,512]{1,0:T(8,128)(2,1)} collective-permute-done((bf16[1024,512]{1,0:T(8,128)(2,1)S(1)}, bf16[1024,512]{1,0:T(8,128)(2,1)}, u32[]{:S(2)}, u32[]{:S(2)}) %collective-permute-start.1) | collective-permute-done | bytes 1048608 | tf_op jit(solution)/shard_map/ppermute | solution.py:270
  47.9 20.4 %collective-permute-done.5.refs_2_ = bf16[1024,512]{1,0:T(8,128)(2,1)S(1)} collective-permute-done((bf16[1024,512]{1,0:T(8,128)(2,1)S(1)}, bf16[1024,512]{1,0:T(8,128)(2,1)S(1)}, u32[]{:S(2)}, u32[]{:S(2)}) %collective-permute-start.5) | collective-permute-done | bytes 1048608 | tf_op jit(solution)/shard_map/ppermute | solution.py:270
  82.5 27.2 %all-gather.7.cloned.1.call-done.refs_1_.refs_3_ = bf16[1024,512]{1,0:T(8,128)(2,1)} async-done(((bf16[256,512]{1,0:T(8,128)(2,1)}), bf16[1024,512]{1,0:T(8,128)(2,1)}) %all-gather.7.cloned.1.call-update) | async-done | bytes 1048592 | tf_op jit(solution)/shard_map/all_gather | solution.py:555
  111.1 46.7 %collective-permute-done.7.refs_3_.refs_2_.refs_4_ = bf16[1024,1664]{1,0:T(8,128)(2,1)} collective-permute-done((bf16[1024,1664]{1,0:T(8,128)(2,1)}, bf16[1024,1664]{1,0:T(8,128)(2,1)}, u32[]{:S(2)}, u32[]{:S(2)}) %collective-permute-start.7) | collective-permute-done | bytes 3407904 | tf_op jit(solution)/shard_map/ppermute | solution.py:270
  159.8 12.7 %halves.3.x_ref.prev_ref = f32[1024,1664]{1,0:T(8,128)} custom-call(bf16[1024,2048]{1,0:T(8,128)(2,1)} %get-tuple-element.120.refs_0_.refs_2_.left_ref, bf16[1024,1664]{1,0:T(8,128)(2,1)S(1)} %copy-done, bf16[1024,2048]{1,0:T(8,128)(2,1)} %get-tuple-element.120.refs_0_.refs_2_.left_ref, bf16[1024,1664]{1,0:T(8,128)(2,1)} %collective-permute-done.7.refs_3_.refs_2_.refs_4_), custom_call_target="tpu_custom_call" | custom-call | flops 1048576 | bytes 262144 | tf_op jit(solution)/shard_map/halves/pallas_call | solution.py:400
  174.7 34.2 %mixer_forward.1 = (bf16[1024,512]{1,0:T(8,128)(2,1)}, f32[1024,512]{1,0:T(8,128)}, f32[1024,512]{1,0:T(8,128)}, f32[8,4,128,128]{3,2,1,0:T(8,128)}, f32[8,4,128,128]{3,2,1,0:T(8,128)}) custom-call(f32[1024,1664]{1,0:T(8,128)} %halves.3.x_ref.prev_ref, f32[4,1536]{1,0:T(4,128)} %copy-done.57, f32[1,128]{1,0:T(1,128)} %bitcast.112), custom_call_target="tpu_custom_call" | custom-call | flops 1048576 | bytes 262144 | tf_op jit(solution)/shard_map/mixer_forward/pallas_call | solution.py:201
  230.7 16.5 %collective-permute-done.11 = bf16[1024,512]{1,0:T(8,128)(2,1)S(1)} collective-permute-done((bf16[1024,512]{1,0:T(8,128)(2,1)}, bf16[1024,512]{1,0:T(8,128)(2,1)S(1)}, u32[]{:S(2)}, u32[]{:S(2)}) %collective-permute-start.11) | collective-permute-done | bytes 1048608 | tf_op jit(solution)/shard_map/ppermute | solution.py:270
  252.1 23.0 %collective-permute-done.14.refs_2_ = bf16[1024,512]{1,0:T(8,128)(2,1)S(1)} collective-permute-done((bf16[1024,512]{1,0:T(8,128)(2,1)S(1)}, bf16[1024,512]{1,0:T(8,128)(2,1)S(1)}, u32[]{:S(2)}, u32[]{:S(2)}) %collective-permute-start.14) | collective-permute-done | bytes 1048608 | tf_op jit(solution)/shard_map/ppermute | solution.py:270
  283.1 9.3 %halves.4.refs_4_ = bf16[1024,1408]{1,0:T(8,128)(2,1)S(1)} custom-call(bf16[1024,2048]{1,0:T(8,128)(2,1)} %get-tuple-element.109.refs_0_.refs_2_.refs_1_.left_ref, bf16[1024,1408]{1,0:T(8,128)(2,1)S(1)} %copy-done.1, bf16[1024,2048]{1,0:T(8,128)(2,1)} %get-tuple-element.109.refs_0_.refs_2_.refs_1_.left_ref, ...), custom_call_target="tpu_custom_call" | custom-call | flops 1048576 | bytes 262144 | tf_op jit(solution)/shard_map/halves/pallas_call | solution.py:400
  294.0 8.8 %collective-permute-done.16.refs_3_.refs_7_.refs_9_ = bf16[1024,1408]{1,0:T(8,128)(2,1)} collective-permute-done((bf16[1024,1408]{1,0:T(8,128)(2,1)}, bf16[1024,1408]{1,0:T(8,128)(2,1)}, u32[]{:S(2)}, u32[]{:S(2)}) %collective-permute-start.16) | collective-permute-done | bytes 2883616 | tf_op jit(solution)/shard_map/ppermute | solution.py:270
  302.7 11.3 %hidden.1 = (bf16[1024,1408]{1,0:T(8,128)(2,1)S(1)}, bf16[1024,1408]{1,0:T(8,128)(2,1)S(1)}) custom-call(bf16[1024,2048]{1,0:T(8,128)(2,1)} %get-tuple-element.109.refs_0_.refs_2_.refs_1_.left_ref, bf16[1024,2048]{1,0:T(8,128)(2,1)} %get-tuple-element.109.refs_0_.refs_2_.refs_1_.left_ref, ...), custom_call_target="tpu_custom_call" | custom-call | flops 1048576 | bytes 262144 | tf_op jit(solution)/shard_map/hidden/pallas_call | solution.py:400
  315.6 9.7 %all_rows.1 = bf16[2048,1408]{1,0:T(8,128)(2,1)} custom-call(s32[1]{0:T(128)} %bitcast.21.odd_ref, bf16[1024,2048]{1,0:T(8,128)(2,1)} %join.2.left_ref.refs_0_.refs_1_, bf16[1024,1408]{1,0:T(8,128)(2,1)S(1)} %get-tuple-element.135.right_ref.refs_0_), custom_call_target="tpu_custom_call" | custom-call | flops 1048576 | bytes 262144 | tf_op jit(solution)/shard_map/all_rows/pallas_call | solution.py:404
  327.3 20.6 %all-gather.17.cloned.1.call-done.refs_3_.refs_2_.refs_4_ = bf16[1024,1408]{1,0:T(8,128)(2,1)} async-done(((bf16[256,1408]{1,0:T(8,128)(2,1)}), bf16[1024,1408]{1,0:T(8,128)(2,1)}) %all-gather.17.cloned.1.call-update) | async-done | bytes 2883600 | tf_op jit(solution)/shard_map/all_gather | solution.py:555
  347.9 14.5 %cots.1 = (bf16[1024,1408]{1,0:T(8,128)(2,1)S(1)}, bf16[1024,1408]{1,0:T(8,128)(2,1)}, f32[1024,1]{1,0:T(8,128)S(1)}) custom-call(bf16[1024,2048]{1,0:T(8,128)(2,1)} %join.2.left_ref.refs_0_.refs_1_, bf16[1024,2048]{1,0:T(8,128)(2,1)} %join.2.left_ref.refs_0_.refs_1_, bf16[1024,1408]{1,0:T(8,128)(2,1)} %all-gather.15.cloned.1.call-done.refs_2_.refs_1_.refs_3_, ...), custom_call_target="tpu_custom_call" | custom-call | flops 1048576 | bytes 262144 | tf_op jit(solution)/shard_map/cots/pallas_call | solution.py:400
  362.4 11.8 %piece.10 = (bf16[1024,512]{1,0:T(8,128)(2,1)}, bf16[1024,512]{1,0:T(8,128)(2,1)}) custom-call(s32[2]{0:T(128)S(1)} %pad_add_fusion.1.me_ref, bf16[1024,1408]{1,0:T(8,128)(2,1)S(1)} %get-tuple-element.106.refs_0_.right_ref, bf16[1024,1408]{1,0:T(8,128)(2,1)} %all-gather.11.cloned.1.call-done.refs_1_.refs_3_, ...), custom_call_target="tpu_custom_call" | custom-call | flops 1048576 | bytes 262144 | tf_op jit(solution)/shard_map/piece/pallas_call | solution.py:404
  378.7 6.2 rows.8
  386.9 12.7 %piece.11 = (bf16[1024,512]{1,0:T(8,128)(2,1)}, f32[1024,512]{1,0:T(8,128)S(1)}) custom-call(s32[2]{0:T(128)S(1)} %pad_add_fusion.me_ref, bf16[1024,1408]{1,0:T(8,128)(2,1)} %copy-done.4, bf16[1024,1408]{1,0:T(8,128)(2,1)} %all-gather.11.cloned.1.call-done.refs_1_.refs_3_, bf16[1024,1408]{1,0:T(8,128)(2,1)} %collective-permute-done.12.refs_3_.refs_2_.refs_4_, ...), custom_call_target="tpu_custom_call" | custom-call | flops 1048576 | bytes 262144 | tf_op jit(solution)/shard_map/piece/pallas_call | solution.py:404
  409.3 17.2 %collective-permute-done.21 = bf16[1024,512]{1,0:T(8,128)(2,1)} collective-permute-done((bf16[1024,512]{1,0:T(8,128)(2,1)}, bf16[1024,512]{1,0:T(8,128)(2,1)}, u32[]{:S(2)}, u32[]{:S(2)}) %collective-permute-start.21) | collective-permute-done | bytes 1048608 | tf_op jit(solution)/shard_map/ppermute | solution.py:270
  431.5 42.0 %collective-permute-done.27.refs_0_ = bf16[1024,1408]{1,0:T(8,128)(2,1)} collective-permute-done((bf16[1024,1408]{1,0:T(8,128)(2,1)}, bf16[1024,1408]{1,0:T(8,128)(2,1)}, u32[]{:S(2)}, u32[]{:S(2)}) %collective-permute-start.27) | collective-permute-done | bytes 2883616 | tf_op jit(solution)/shard_map/ppermute | solution.py:270
  502.7 37.5 %mixer_backward.1 = (bf16[1024,1664]{1,0:T(8,128)(2,1)}, f32[4,1536]{1,0:T(4,128)}, f32[1,128]{1,0:T(1,128)}, f32[1024,1]{1,0:T(8,128)}) custom-call(f32[1024,1664]{1,0:T(8,128)} %halves.3.x_ref.prev_ref, f32[1024,1664]{1,0:T(8,128)} %halves.3.x_ref.prev_ref, f32[4,1536]{1,0:T(4,128)} %copy-done.57, f32[1,128]{1,0:T(1,128)} %bitcast.113, ...), custom_call_target="tpu_custom_call" | custom-call | flops 1048576 | bytes 262144 | tf_op jit(solution)/shard_map/mixer_backward/pallas_call | solution.py:233
  542.2 7.5 %piece.12 = (bf16[1024,512]{1,0:T(8,128)(2,1)}, bf16[1024,512]{1,0:T(8,128)(2,1)}) custom-call(s32[2]{0:T(128)S(1)} %pad_add_fusion.1.me_ref, bf16[1024,1664]{1,0:T(8,128)(2,1)S(1)} %copy-done.2, bf16[1024,1664]{1,0:T(8,128)(2,1)} %all-gather.9.cloned.1.call-done.refs_1_.refs_3_, bf16[1024,1664]{1,0:T(8,128)(2,1)} %collective-permute-done.7.refs_3_.refs_2_.refs_4_, ...), custom_call_target="tpu_custom_call" | custom-call | flops 1048576 | bytes 262144 | tf_op jit(solution)/shard_map/piece/pallas_call | solution.py:404
  554.5 6.5 rows.11
  564.5 7.8 %piece.13 = (bf16[1024,512]{1,0:T(8,128)(2,1)}, f32[1024,512]{1,0:T(8,128)S(1)}) custom-call(s32[2]{0:T(128)S(1)} %pad_add_fusion.me_ref, bf16[1024,1664]{1,0:T(8,128)(2,1)} %get-tuple-element.124.refs_0_.right_ref, bf16[1024,1664]{1,0:T(8,128)(2,1)} %all-gather.9.cloned.1.call-done.refs_1_.refs_3_, ...), custom_call_target="tpu_custom_call" | custom-call | flops 1048576 | bytes 262144 | tf_op jit(solution)/shard_map/piece/pallas_call | solution.py:404
  590.0 18.7 %collective-permute-done.33 = bf16[1024,512]{1,0:T(8,128)(2,1)} collective-permute-done((bf16[1024,512]{1,0:T(8,128)(2,1)}, bf16[1024,512]{1,0:T(8,128)(2,1)}, u32[]{:S(2)}, u32[]{:S(2)}) %collective-permute-start.33) | collective-permute-done | bytes 1048608 | tf_op jit(solution)/shard_map/ppermute | solution.py:270
  619.1 7.6 %collective-permute-done.36 = f32[81,128]{1,0:T(8,128)S(1)} collective-permute-done((f32[81,128]{1,0:T(8,128)S(1)}, f32[81,128]{1,0:T(8,128)S(1)}, u32[]{:S(2)}, u32[]{:S(2)}) %collective-permute-start.36) | collective-permute-done | bytes 41504 | tf_op jit(solution)/shard_map/ppermute | solution.py:270
  632.2 26.5 %collective-permute-done.25.refs_0_ = bf16[1024,1664]{1,0:T(8,128)(2,1)} collective-permute-done((bf16[1024,1664]{1,0:T(8,128)(2,1)}, bf16[1024,1664]{1,0:T(8,128)(2,1)}, u32[]{:S(2)}, u32[]{:S(2)}) %collective-permute-start.25) | collective-permute-done | bytes 3407904 | tf_op jit(solution)/shard_map/ppermute | solution.py:270
  658.7 7.7 %rows.15 = bf16[1024,1664]{1,0:T(8,128)(2,1)S(1)} custom-call(bf16[1024,2048]{1,0:T(8,128)(2,1)} %get-tuple-element.120.refs_0_.refs_2_.left_ref, bf16[1024,1664]{1,0:T(8,128)(2,1)} %get-tuple-element.124.refs_0_.right_ref, bf16[1024,1664]{1,0:T(8,128)(2,1)} %collective-permute-done.25.refs_0_), custom_call_target="tpu_custom_call" | custom-call | flops 1048576 | bytes 262144 | tf_op jit(solution)/shard_map/rows/pallas_call | solution.py:400
  670.0 6.9 piece.14
  688.5 6.5 piece.15
  709.2 11.0 %collective-permute-done.40 = bf16[1024,512]{1,0:T(8,128)(2,1)} collective-permute-done((bf16[1024,512]{1,0:T(8,128)(2,1)}, bf16[1024,512]{1,0:T(8,128)(2,1)}, u32[]{:S(2)}, u32[]{:S(2)}) %collective-permute-start.40) | collective-permute-done | bytes 1048608 | tf_op jit(solution)/shard_map/ppermute | solution.py:270
  724.0 11.2 %reduce-scatter.12.cloned.1.call-done = bf16[256,1664]{1,0:T(8,128)(2,1)} async-done(((bf16[1024,1664]{1,0:T(8,128)(2,1)}), bf16[256,1664]{1,0:T(8,128)(2,1)}) %reduce-scatter.12.cloned.1.call-update) | async-done | bytes 851984 | tf_op jit(solution)/shard_map/reduce_scatter | solution.py:559
  (332 shorter events, 207.9 us)
Async XLA Ops:
  7.2 73.8 %all-gather.9.cloned.1.call-start = ((), (), s32[]{:S(2)}) async-start(), calls=%async_computation.6 | async-start | bytes 4259840 | tf_op jit(solution)/shard_map/all_gather | solution.py:555
  10.3 99.4 %all-gather.7.cloned.1.call-start = ((), (), s32[]{:S(2)}) async-start(), calls=%async_computation.5 | async-start | bytes 1310720 | tf_op jit(solution)/shard_map/all_gather | solution.py:555
  11.2 161.3 %all-gather.11.cloned.1.call-start = ((), (), s32[]{:S(2)}) async-start(), calls=%async_computation.7 | async-start | bytes 3604480 | tf_op jit(solution)/shard_map/all_gather | solution.py:555
  11.9 217.3 %all-gather.13.cloned.1.call-start = ((), (), s32[]{:S(2)}) async-start(), calls=%async_computation.8 | async-start | bytes 3604480 | tf_op jit(solution)/shard_map/all_gather | solution.py:555
  12.5 314.8 %all-gather.15.cloned.1.call-start = ((), (), s32[]{:S(2)}) async-start(), calls=%async_computation.9 | async-start | bytes 3604480 | tf_op jit(solution)/shard_map/all_gather | solution.py:555
  12.9 19.2 %collective-permute-start.3 = (bf16[256,1408]{1,0:T(8,128)(2,1)S(1)}, bf16[256,1408]{1,0:T(8,128)(2,1)}, u32[]{:S(2)}, u32[]{:S(2)}) collective-permute-start(bf16[256,1408]{1,0:T(8,128)(2,1)S(1)} %bitcast.92), channel_id=1, source_target_pairs={{0,4},{4,0},{8,12},{12,8},{16,20},{20,16},{24,28},{28,24},{1,5},{5... | collective-permute-start | bytes 2162696 | tf_op jit(solution)/shard_map/ppermute | solution.py:270
  21.1 26.3 %collective-permute-start.1 = (bf16[1024,512]{1,0:T(8,128)(2,1)S(1)}, bf16[1024,512]{1,0:T(8,128)(2,1)}, u32[]{:S(2)}, u32[]{:S(2)}) collective-permute-start(bf16[1024,512]{1,0:T(8,128)(2,1)S(1)} %pad_maximum_fusion.1.refs_0_), channel_id=1, source_target_pairs={{0,2},{1,3},{2,0},{3,1},{4,6},{5,7},{6,4},{7,5},{8,10},{9,11},{10,... | collective-permute-start | bytes 3145736 | tf_op jit(solution)/shard_map/ppermute | solution.py:270
  32.2 36.1 %collective-permute-start.5 = (bf16[1024,512]{1,0:T(8,128)(2,1)S(1)}, bf16[1024,512]{1,0:T(8,128)(2,1)S(1)}, u32[]{:S(2)}, u32[]{:S(2)}) collective-permute-start(bf16[1024,512]{1,0:T(8,128)(2,1)S(1)} %fusion.9.refs_0_), channel_id=1, source_target_pairs={{0,2},{1,3},{2,0},{3,1},{4,6},{5,7},{6,4},{7,5},{8,10},{9,11},{10,... | collective-permute-start | bytes 3145736 | tf_op jit(solution)/shard_map/ppermute | solution.py:270
  33.9 35.1 %collective-permute-start = (bf16[1024,512]{1,0:T(8,128)(2,1)S(1)}, bf16[1024,512]{1,0:T(8,128)(2,1)}, u32[]{:S(2)}, u32[]{:S(2)}) collective-permute-start(bf16[1024,512]{1,0:T(8,128)(2,1)S(1)} %pad_maximum_fusion.1.refs_0_), channel_id=1, source_target_pairs={{0,1},{1,0},{2,3},{3,2},{4,5},{5,4},{6,7},{7,6},{8,9},{9,8},{10,11... | collective-permute-start | bytes 3145736 | tf_op jit(solution)/shard_map/ppermute | solution.py:270
  47.4 21.7 %collective-permute-start.2 = (bf16[1024,512]{1,0:T(8,128)(2,1)}, bf16[1024,512]{1,0:T(8,128)(2,1)}, u32[]{:S(2)}, u32[]{:S(2)}) collective-permute-start(bf16[1024,512]{1,0:T(8,128)(2,1)} %collective-permute-done.1.refs_2_), channel_id=1, source_target_pairs={{0,1},{1,0},{2,3},{3,2},{4,5},{5,4},{6,7},{7,6},{8,9},{9,8},{10,11... | collective-permute-start | bytes 3145736 | tf_op jit(solution)/shard_map/ppermute | solution.py:270
  47.4 26.9 %collective-permute-start.4 = (bf16[1024,512]{1,0:T(8,128)(2,1)S(1)}, bf16[1024,512]{1,0:T(8,128)(2,1)}, u32[]{:S(2)}, u32[]{:S(2)}) collective-permute-start(bf16[1024,512]{1,0:T(8,128)(2,1)S(1)} %fusion.9.refs_0_), channel_id=1, source_target_pairs={{0,1},{1,0},{2,3},{3,2},{4,5},{5,4},{6,7},{7,6},{8,9},{9,8},{10,11... | collective-permute-start | bytes 3145736 | tf_op jit(solution)/shard_map/ppermute | solution.py:270
  80.9 76.9 %collective-permute-start.7 = (bf16[1024,1664]{1,0:T(8,128)(2,1)}, bf16[1024,1664]{1,0:T(8,128)(2,1)}, u32[]{:S(2)}, u32[]{:S(2)}) collective-permute-start(bf16[1024,1664]{1,0:T(8,128)(2,1)} %all-gather.9.cloned.1.call-done.refs_1_.refs_3_), channel_id=1, source_target_pairs={{0,4},{4,0},{8,12},{12,8},{16,20},{20,16},{24,28},{28,24},{1,5},{5... | collective-permute-start | bytes 10223624 | tf_op jit(solution)/shard_map/ppermute | solution.py:270
  82.4 265.5 %all-gather.17.cloned.1.call-start = ((), (), s32[]{:S(2)}) async-start(), calls=%async_computation.10 | async-start | bytes 3604480 | tf_op jit(solution)/shard_map/all_gather | solution.py:555
  109.7 99.3 %collective-permute-start.8 = (bf16[1024,512]{1,0:T(8,128)(2,1)}, bf16[1024,512]{1,0:T(8,128)(2,1)S(1)}, u32[]{:S(2)}, u32[]{:S(2)}) collective-permute-start(bf16[1024,512]{1,0:T(8,128)(2,1)} %all-gather.7.cloned.1.call-done.refs_1_.refs_3_), channel_id=1, source_target_pairs={{0,4},{4,0},{8,12},{12,8},{16,20},{20,16},{24,28},{28,24},{1,5},{5... | collective-permute-start | bytes 3145736 | tf_op jit(solution)/shard_map/ppermute | solution.py:270
  172.5 76.8 %collective-permute-start.12 = (bf16[1024,1408]{1,0:T(8,128)(2,1)}, bf16[1024,1408]{1,0:T(8,128)(2,1)}, u32[]{:S(2)}, u32[]{:S(2)}) collective-permute-start(bf16[1024,1408]{1,0:T(8,128)(2,1)} %all-gather.11.cloned.1.call-done.refs_1_.refs_3_), channel_id=1, source_target_pairs={{0,4},{4,0},{8,12},{12,8},{16,20},{20,16},{24,28},{28,24},{1,5},{5... | collective-permute-start | bytes 8650760 | tf_op jit(solution)/shard_map/ppermute | solution.py:270
  213.7 362.0 %reduce-scatter.8.cloned.1.call-start = ((), (), s32[]{:S(2)}) async-start(), calls=%async_computation.12 | async-start | bytes 6488064 | tf_op jit(solution)/shard_map/reduce_scatter | solution.py:576
  221.9 25.4 %collective-permute-start.11 = (bf16[1024,512]{1,0:T(8,128)(2,1)}, bf16[1024,512]{1,0:T(8,128)(2,1)S(1)}, u32[]{:S(2)}, u32[]{:S(2)}) collective-permute-start(bf16[1024,512]{1,0:T(8,128)(2,1)} %get-tuple-element.89), channel_id=1, source_target_pairs={{0,2},{1,3},{2,0},{3,1},{4,6},{5,7},{6,4},{7,5},{8,10},{9,11},{10,... | collective-permute-start | bytes 3145736 | tf_op jit(solution)/shard_map/ppermute | solution.py:270
  229.3 73.5 %collective-permute-start.16 = (bf16[1024,1408]{1,0:T(8,128)(2,1)}, bf16[1024,1408]{1,0:T(8,128)(2,1)}, u32[]{:S(2)}, u32[]{:S(2)}) collective-permute-start(bf16[1024,1408]{1,0:T(8,128)(2,1)} %all-gather.13.cloned.1.call-done.refs_2_.refs_6_.refs_8_), channel_id=1, source_target_pairs={{0,4},{4,0},{8,12},{12,8},{16,20},{20,16},{24,28},{28,24},{1,5},{5... | collective-permute-start | bytes 8650760 | tf_op jit(solution)/shard_map/ppermute | solution.py:270
  250.7 24.5 %collective-permute-start.14 = (bf16[1024,512]{1,0:T(8,128)(2,1)S(1)}, bf16[1024,512]{1,0:T(8,128)(2,1)S(1)}, u32[]{:S(2)}, u32[]{:S(2)}) collective-permute-start(bf16[1024,512]{1,0:T(8,128)(2,1)S(1)} %fusion.7.refs_0_), channel_id=1, source_target_pairs={{0,2},{1,3},{2,0},{3,1},{4,6},{5,7},{6,4},{7,5},{8,10},{9,11},{10,... | collective-permute-start | bytes 3145736 | tf_op jit(solution)/shard_map/ppermute | solution.py:270
  252.1 23.7 %collective-permute-start.13 = (bf16[1024,512]{1,0:T(8,128)(2,1)S(1)}, bf16[1024,512]{1,0:T(8,128)(2,1)S(1)}, u32[]{:S(2)}, u32[]{:S(2)}) collective-permute-start(bf16[1024,512]{1,0:T(8,128)(2,1)S(1)} %fusion.7.refs_0_), channel_id=1, source_target_pairs={{0,1},{1,0},{2,3},{3,2},{4,5},{5,4},{6,7},{7,6},{8,9},{9,8},{10,11... | collective-permute-start | bytes 3145736 | tf_op jit(solution)/shard_map/ppermute | solution.py:270
  326.9 258.7 %reduce-scatter.6.cloned.1.call-start = ((), (), s32[]{:S(2)}) async-start(), calls=%async_computation.11 | async-start | bytes 3604480 | tf_op jit(solution)/shard_map/reduce_scatter | solution.py:559
  384.8 88.7 %collective-permute-start.27 = (bf16[1024,1408]{1,0:T(8,128)(2,1)}, bf16[1024,1408]{1,0:T(8,128)(2,1)}, u32[]{:S(2)}, u32[]{:S(2)}) collective-permute-start(bf16[1024,1408]{1,0:T(8,128)(2,1)} %rows.8), channel_id=1, source_target_pairs={{0,4},{4,0},{8,12},{12,8},{16,20},{20,16},{24,28},{28,24},{1,5},{5... | collective-permute-start | bytes 8650760 | tf_op jit(solution)/shard_map/ppermute | solution.py:270
  401.0 25.5 %collective-permute-start.21 = (bf16[1024,512]{1,0:T(8,128)(2,1)}, bf16[1024,512]{1,0:T(8,128)(2,1)}, u32[]{:S(2)}, u32[]{:S(2)}) collective-permute-start(bf16[1024,512]{1,0:T(8,128)(2,1)} %get-tuple-element.108), channel_id=1, source_target_pairs={{0,2},{1,3},{2,0},{3,1},{4,6},{5,7},{6,4},{7,5},{8,10},{9,11},{10,... | collective-permute-start | bytes 3145736 | tf_op jit(solution)/shard_map/ppermute | solution.py:270
  430.0 43.5 %collective-permute-start.23 = (bf16[1024,512]{1,0:T(8,128)(2,1)S(1)}, bf16[1024,512]{1,0:T(8,128)(2,1)}, u32[]{:S(2)}, u32[]{:S(2)}) collective-permute-start(bf16[1024,512]{1,0:T(8,128)(2,1)S(1)} %get-tuple-element.175.refs_0_), channel_id=1, source_target_pairs={{0,2},{1,3},{2,0},{3,1},{4,6},{5,7},{6,4},{7,5},{8,10},{9,11},{10,... | collective-permute-start | bytes 3145736 | tf_op jit(solution)/shard_map/ppermute | solution.py:270
  481.2 177.5 %reduce-scatter.10.cloned.1.call-start = ((), (), s32[]{:S(2)}) async-start(), calls=%async_computation.13 | async-start | bytes 3604480 | tf_op jit(solution)/shard_map/reduce_scatter | solution.py:559
  481.3 92.3 %collective-permute-start.28 = (bf16[1024,1408]{1,0:T(8,128)(2,1)}, bf16[1024,1408]{1,0:T(8,128)(2,1)}, u32[]{:S(2)}, u32[]{:S(2)}) collective-permute-start(bf16[1024,1408]{1,0:T(8,128)(2,1)} %copy-done.23), channel_id=1, source_target_pairs={{0,4},{4,0},{8,12},{12,8},{16,20},{20,16},{24,28},{28,24},{1,5},{5... | collective-permute-start | bytes 8650760 | tf_op jit(solution)/shard_map/ppermute | solution.py:270
  550.2 25.5 %collective-permute-start.26 = (bf16[1024,512]{1,0:T(8,128)(2,1)}, bf16[1024,512]{1,0:T(8,128)(2,1)}, u32[]{:S(2)}, u32[]{:S(2)}) collective-permute-start(bf16[1024,512]{1,0:T(8,128)(2,1)} %rows.10), channel_id=1, source_target_pairs={{0,4},{4,0},{8,12},{12,8},{16,20},{20,16},{24,28},{28,24},{1,5},{5... | collective-permute-start | bytes 3145736 | tf_op jit(solution)/shard_map/ppermute | solution.py:270
  583.4 119.3 %reduce-scatter.14.cloned.1.call-start = ((), (), s32[]{:S(2)}) async-start(), calls=%async_computation.15 | async-start | bytes 1310720 | tf_op jit(solution)/shard_map/reduce_scatter | solution.py:559
  583.5 75.3 %collective-permute-start.25 = (bf16[1024,1664]{1,0:T(8,128)(2,1)}, bf16[1024,1664]{1,0:T(8,128)(2,1)}, u32[]{:S(2)}, u32[]{:S(2)}) collective-permute-start(bf16[1024,1664]{1,0:T(8,128)(2,1)} %copy-done.21), channel_id=1, source_target_pairs={{0,4},{4,0},{8,12},{12,8},{16,20},{20,16},{24,28},{28,24},{1,5},{5... | collective-permute-start | bytes 10223624 | tf_op jit(solution)/shard_map/ppermute | solution.py:270
  584.0 24.6 %collective-permute-start.33 = (bf16[1024,512]{1,0:T(8,128)(2,1)}, bf16[1024,512]{1,0:T(8,128)(2,1)}, u32[]{:S(2)}, u32[]{:S(2)}) collective-permute-start(bf16[1024,512]{1,0:T(8,128)(2,1)} %get-tuple-element.128), channel_id=1, source_target_pairs={{0,2},{1,3},{2,0},{3,1},{4,6},{5,7},{6,4},{7,5},{8,10},{9,11},{10,... | collective-permute-start | bytes 3145736 | tf_op jit(solution)/shard_map/ppermute | solution.py:270
  589.6 145.6 %reduce-scatter.12.cloned.1.call-start = ((), (), s32[]{:S(2)}) async-start(), calls=%async_computation.14 | async-start | bytes 4259840 | tf_op jit(solution)/shard_map/reduce_scatter | solution.py:559
  695.1 25.1 %collective-permute-start.40 = (bf16[1024,512]{1,0:T(8,128)(2,1)}, bf16[1024,512]{1,0:T(8,128)(2,1)}, u32[]{:S(2)}, u32[]{:S(2)}) collective-permute-start(bf16[1024,512]{1,0:T(8,128)(2,1)} %get-tuple-element.137), channel_id=1, source_target_pairs={{0,2},{1,3},{2,0},{3,1},{4,6},{5,7},{6,4},{7,5},{8,10},{9,11},{10,... | collective-permute-start | bytes 3145736 | tf_op jit(solution)/shard_map/ppermute | solution.py:270
  (86 other events, 870.7 us)
Sparse Core Ops, SparseCore 0:
  10.4 70.5 all-gather.8
  83.1 26.5 all-gather.6
  111.2 58.6 all-gather.10
  171.4 57.8 all-gather.12
  230.7 57.8 all-gather.14
  290.0 57.8 all-gather.16
  351.5 129.6 reduce-scatter.7
  483.6 54.7 reduce-scatter.5
  583.5 56.4 reduce-scatter.9
  642.8 27.0 reduce-scatter.13
  672.2 62.9 reduce-scatter.11

commit v5 on v4

--- a/solution.py
+++ b/solution.py
@@ -5,6 +5,7 @@
 from jax.experimental import pallas as pl
 from jax.experimental.pallas import tpu as pltpu
 from jax.sharding import PartitionSpec as P
+from jax.experimental.layout import Layout, with_layout_constraint
 
 CHUNK = 128
 EPS = 1e-6
@@ -434,8 +435,25 @@
                      jax.ShapeDtypeStruct((rows, width), dtype), row_tile(width), (rows // TILE,), "halves")
 
 
+def flat(ref):
+    value = ref[...]
+    return value.reshape(-1, value.shape[-1])
+
+
+def weight_spec(w, p):
+    if w.ndim == 2:
+        return whole(w.shape)
+    return pl.BlockSpec((w.shape[0], 1) + w.shape[2:], lambda i, *_: (0, p, 0, 0))
+
+
+def block_spec(w, p, n, block):
+    if w.ndim == 2:
+        return pl.BlockSpec((block, w.shape[1]), lambda i, m: (m[n], 0))
+    return pl.BlockSpec((block // w.shape[2], 1) + w.shape[2:], lambda i, m: (m[n], p, 0, 0))
+
+
 def both(refs):
-    return dot(refs[0][...], refs[2][...]) + dot(refs[1][...], refs[3][...])
+    return dot(refs[0][...], flat(refs[2])) + dot(refs[1][...], flat(refs[3]))
 
 
 def hidden_kernel(*refs):
@@ -448,7 +466,7 @@
 
 def both_specs(left, pair):
     half = left.shape[1] // 2
-    return [left, left, *pair], [half_tile(half, 0), half_tile(half, 1), whole(pair[0].shape), whole(pair[1].shape)]
+    return [left, left, *pair], [half_tile(half, 0), half_tile(half, 1), weight_spec(pair[0], 0), weight_spec(pair[1], 1)]
 
 
 def hidden_call(left, pair, gate):
@@ -489,7 +507,7 @@
         for p in range(2):
             total = None
             for i in range(count):
-                term = dot(refs[stride * i][...], refs[stride * i + 1 + 2 * n + p][...], 1, 1)
+                term = dot(refs[stride * i][...], flat(refs[stride * i + 1 + 2 * n + p]), 1, 1)
                 total = term if total is None else total + term
             if has_got:
                 total = total + refs[stride * count + n][:, p * width : (p + 1) * width].astype(f32)
@@ -505,7 +523,7 @@
         specs.append(row_tile(left.shape[1]))
         for n in range(len(js)):
             arrays += pair
-            specs += [pl.BlockSpec((block, w.shape[1]), lambda i, m, n=n: (m[n], 0)) for w in pair]
+            specs += [block_spec(w, p, n, block) for p, w in enumerate(pair)]
     has_got = gots[0] is not None
     if has_got:
         arrays += gots
@@ -628,8 +646,8 @@
     up_mine = gather_parity(up_weight)
     down_turned = down_weight.T
     down_side = swap(down_turned, "row", 1)
-    down_mine = gather_parity(down_turned)
-    down_other = gather_parity(down_side)
+    down_both = with_layout_constraint(jnp.concatenate([down_turned, down_side], 0), Layout((0, 1)))
+    down_rows = with_layout_constraint(gather_parity(down_both), Layout((0, 1))).reshape(-1, 2, *down_turned.shape)
     conv = jnp.concatenate([conv_q, conv_k, conv_v], 1)
     gain = head_gain.reshape(1, dh)
     gain_in = lax.dynamic_slice_in_dim(norm_in, col * width, width)
@@ -667,7 +685,7 @@
     up, hidden = hidden_call(after(normed_mid, gate), w_up, gate)
     down_sent = all_rows(ffn_cot, hidden)
     grad_down = scatter_rows(down_sent)
-    w_down = after(down_mine, down_sent), after(down_other, down_sent)
+    w_down = (after(down_rows, down_sent),) * 2
     gate_cot, up_cot, inner_mid = cots_call(ffn_cot, w_down, gate, up)
     inner_mid = sum_all(inner_mid.reshape(rows // 128, 128), "col").reshape(rows, 1) / factor_mid
     mid_sum = ColSum([(gate_cot, w_gate), (up_cot, w_up)], block)

time: 755 us -> 739 us (0.979)
  waiting for transfers between devices: 353 us -> 341 us
    all_gather x6 -> x5, waiting for transfers between devices: 56.5 us -> 43.9 us  [gather_parity(): lax.all_gather(shard, 'row', axis=0, tiled=True, axis_index_groups=parity...]
    unnamed x148 -> x144, local copies, waits for them, and re-layouts: 45.8 us -> 42.8 us
  transfers between devices with their start and end apart: 53 -> 52, of which waited for: 29 -> 29; matrix products, arithmetic and copies ran while one was open for 6% -> 7% of each run, Pallas kernels for 35% -> 35%
where the time goes in v5:
time: 739 us; the launch traced here: 734 us
  waiting for transfers between devices  341 us (46%)
  Pallas kernels  259 us (35%)
  local copies, waits for them, and re-layouts  53.3 us (7%)
  starting transfers between devices  34.7 us (5%)
  other arithmetic  30 us (4%)
  between operations  16 us (2%)
    ppermute x42, waiting for transfers between devices, swap(): return lax.ppermute(x, axis, [(i, i ^ bit) for i in range(n)])  285 us
    pallas_call x13, Pallas kernels, tile_call(): pl.pallas_call(kernel, grid=grid, in_specs=specs, out_specs=out_specs, ou...  97.6 us
    pallas_call x9, Pallas kernels, tile_call(): pl.pallas_call(kernel, grid_spec=grid_spec, out_shape=outs, **params)  71.2 us
    all_gather x5, waiting for transfers between devices, gather_parity(): lax.all_gather(shard, 'row', axis=0, tiled=True, axis_index_groups=parity...  43.9 us
    unnamed x144, local copies, waits for them, and re-layouts  42.8 us
    pallas_call x1, Pallas kernels, mixer_backward(): pl.pallas_call(functools.partial(bwd_kernel, heads, dh), grid=(steps,), i...  37.5 us
    pallas_call x1, Pallas kernels, mixer_forward(): pl.pallas_call(functools.partial(fwd_kernel, heads, dh), grid=(steps,), i...  34.2 us
    ppermute x42, starting transfers between devices, swap(): return lax.ppermute(x, axis, [(i, i ^ bit) for i in range(n)])  34.1 us
  transfers between devices with their start and end apart: 52, of which 29 were waited for; matrix products, arithmetic and copies ran while one was open for 7% of the time, Pallas kernels for 35%

profile of v5, /device:TPU:0, one launch (start us, length us, event | category | flops | bytes accessed | tf_op | source)
XLA Modules:
  0.0 733.5 jit_solution(12299425420480780676)
XLA Ops:
  23.7 8.4 %collective-permute-done.3 = bf16[256,1408]{1,0:T(8,128)(2,1)} collective-permute-done((bf16[256,1408]{1,0:T(8,128)(2,1)S(1)}, bf16[256,1408]{1,0:T(8,128)(2,1)}, u32[]{:S(2)}, u32[]{:S(2)}) %collective-permute-start.3) | collective-permute-done | bytes 720928 | tf_op jit(solution)/shard_map/ppermute | solution.py:271
  33.9 13.4 %collective-permute-done.1.refs_2_ = bf16[1024,512]{1,0:T(8,128)(2,1)} collective-permute-done((bf16[1024,512]{1,0:T(8,128)(2,1)S(1)}, bf16[1024,512]{1,0:T(8,128)(2,1)}, u32[]{:S(2)}, u32[]{:S(2)}) %collective-permute-start.1) | collective-permute-done | bytes 1048608 | tf_op jit(solution)/shard_map/ppermute | solution.py:271
  47.9 20.4 %collective-permute-done.5.refs_2_ = bf16[1024,512]{1,0:T(8,128)(2,1)S(1)} collective-permute-done((bf16[1024,512]{1,0:T(8,128)(2,1)S(1)}, bf16[1024,512]{1,0:T(8,128)(2,1)S(1)}, u32[]{:S(2)}, u32[]{:S(2)}) %collective-permute-start.5) | collective-permute-done | bytes 1048608 | tf_op jit(solution)/shard_map/ppermute | solution.py:271
  85.2 24.5 %all-gather.6.cloned.1.call-done.refs_1_.refs_3_ = bf16[1024,512]{1,0:T(8,128)(2,1)} async-done(((bf16[256,512]{1,0:T(8,128)(2,1)}), bf16[1024,512]{1,0:T(8,128)(2,1)}) %all-gather.6.cloned.1.call-update) | async-done | bytes 1048592 | tf_op jit(solution)/shard_map/all_gather | solution.py:573
  111.1 46.7 %collective-permute-done.7.refs_3_.refs_2_.refs_4_ = bf16[1024,1664]{1,0:T(8,128)(2,1)} collective-permute-done((bf16[1024,1664]{1,0:T(8,128)(2,1)}, bf16[1024,1664]{1,0:T(8,128)(2,1)}, u32[]{:S(2)}, u32[]{:S(2)}) %collective-permute-start.7) | collective-permute-done | bytes 3407904 | tf_op jit(solution)/shard_map/ppermute | solution.py:271
  157.9 12.6 %halves.3.x_ref.prev_ref = f32[1024,1664]{1,0:T(8,128)} custom-call(bf16[1024,2048]{1,0:T(8,128)(2,1)} %get-tuple-element.118.refs_0_.refs_2_.left_ref, bf16[1024,1664]{1,0:T(8,128)(2,1)S(1)} %copy-done, bf16[1024,2048]{1,0:T(8,128)(2,1)} %get-tuple-element.118.refs_0_.refs_2_.left_ref, bf16[1024,1664]{1,0:T(8,128)(2,1)} %collective-permute-done.7.refs_3_.refs_2_.refs_4_), custom_call_target="tpu_custom_call" | custom-call | flops 1048576 | bytes 262144 | tf_op jit(solution)/shard_map/halves/pallas_call | solution.py:401
  172.7 34.2 %mixer_forward.1 = (bf16[1024,512]{1,0:T(8,128)(2,1)}, f32[1024,512]{1,0:T(8,128)}, f32[1024,512]{1,0:T(8,128)}, f32[8,4,128,128]{3,2,1,0:T(8,128)}, f32[8,4,128,128]{3,2,1,0:T(8,128)}) custom-call(f32[1024,1664]{1,0:T(8,128)} %halves.3.x_ref.prev_ref, f32[4,1536]{1,0:T(4,128)} %copy-done.55, f32[1,128]{1,0:T(1,128)} %bitcast.123), custom_call_target="tpu_custom_call" | custom-call | flops 1048576 | bytes 262144 | tf_op jit(solution)/shard_map/mixer_forward/pallas_call | solution.py:202
  222.5 6.8 all-gather.12.cloned.1.call-done.refs_2_.refs_6_.refs_8_
  230.7 15.7 %collective-permute-done.11 = bf16[1024,512]{1,0:T(8,128)(2,1)S(1)} collective-permute-done((bf16[1024,512]{1,0:T(8,128)(2,1)}, bf16[1024,512]{1,0:T(8,128)(2,1)S(1)}, u32[]{:S(2)}, u32[]{:S(2)}) %collective-permute-start.11) | collective-permute-done | bytes 1048608 | tf_op jit(solution)/shard_map/ppermute | solution.py:271
  251.3 23.0 %collective-permute-done.14.refs_2_ = bf16[1024,512]{1,0:T(8,128)(2,1)S(1)} collective-permute-done((bf16[1024,512]{1,0:T(8,128)(2,1)S(1)}, bf16[1024,512]{1,0:T(8,128)(2,1)S(1)}, u32[]{:S(2)}, u32[]{:S(2)}) %collective-permute-start.14) | collective-permute-done | bytes 1048608 | tf_op jit(solution)/shard_map/ppermute | solution.py:271
  282.3 9.4 %halves.4.refs_4_ = bf16[1024,1408]{1,0:T(8,128)(2,1)S(1)} custom-call(bf16[1024,2048]{1,0:T(8,128)(2,1)} %get-tuple-element.107.refs_0_.refs_2_.refs_1_.left_ref, bf16[1024,1408]{1,0:T(8,128)(2,1)S(1)} %copy-done.1, bf16[1024,2048]{1,0:T(8,128)(2,1)} %get-tuple-element.107.refs_0_.refs_2_.refs_1_.left_ref, ...), custom_call_target="tpu_custom_call" | custom-call | flops 1048576 | bytes 262144 | tf_op jit(solution)/shard_map/halves/pallas_call | solution.py:401
  293.3 9.5 %collective-permute-done.16.refs_3_.refs_7_.refs_9_ = bf16[1024,1408]{1,0:T(8,128)(2,1)} collective-permute-done((bf16[1024,1408]{1,0:T(8,128)(2,1)}, bf16[1024,1408]{1,0:T(8,128)(2,1)}, u32[]{:S(2)}, u32[]{:S(2)}) %collective-permute-start.16) | collective-permute-done | bytes 2883616 | tf_op jit(solution)/shard_map/ppermute | solution.py:271
  302.7 11.3 %hidden.1 = (bf16[1024,1408]{1,0:T(8,128)(2,1)S(1)}, bf16[1024,1408]{1,0:T(8,128)(2,1)S(1)}) custom-call(bf16[1024,2048]{1,0:T(8,128)(2,1)} %get-tuple-element.107.refs_0_.refs_2_.refs_1_.left_ref, bf16[1024,2048]{1,0:T(8,128)(2,1)} %get-tuple-element.107.refs_0_.refs_2_.refs_1_.left_ref, ...), custom_call_target="tpu_custom_call" | custom-call | flops 1048576 | bytes 262144 | tf_op jit(solution)/shard_map/hidden/pallas_call | solution.py:401
  315.6 9.7 %all_rows.1 = bf16[2048,1408]{1,0:T(8,128)(2,1)} custom-call(s32[1]{0:T(128)} %bitcast.22.odd_ref, bf16[1024,2048]{1,0:T(8,128)(2,1)} %join.2.left_ref.refs_0_.refs_1_, bf16[1024,1408]{1,0:T(8,128)(2,1)S(1)} %get-tuple-element.133.right_ref.refs_0_), custom_call_target="tpu_custom_call" | custom-call | flops 1048576 | bytes 262144 | tf_op jit(solution)/shard_map/all_rows/pallas_call | solution.py:405
  326.9 9.7 %all-gather.14.cloned.1.call-done = bf16[2048,1408]{1,0:T(8,128)(2,1)} async-done(((bf16[512,1408]{1,0:T(8,128)(2,1)}), bf16[2048,1408]{1,0:T(8,128)(2,1)}) %all-gather.14.cloned.1.call-update) | async-done | bytes 5767184 | tf_op jit(solution)/shard_map/all_gather | solution.py:573
  336.7 14.7 %cots.1 = (bf16[1024,1408]{1,0:T(8,128)(2,1)S(1)}, bf16[1024,1408]{1,0:T(8,128)(2,1)}, f32[1024,1]{1,0:T(8,128)S(1)}) custom-call(bf16[1024,2048]{1,0:T(8,128)(2,1)} %join.2.left_ref.refs_0_.refs_1_, bf16[1024,2048]{1,0:T(8,128)(2,1)} %join.2.left_ref.refs_0_.refs_1_, bf16[4,2,256,1408]{3,2,1,0:T(8,128)(2,1)} %bitcast.89, ...), custom_call_target="tpu_custom_call" | custom-call | flops 1048576 | bytes 262144 | tf_op jit(solution)/shard_map/cots/pallas_call | solution.py:401
  351.4 11.8 %piece.10 = (bf16[1024,512]{1,0:T(8,128)(2,1)}, bf16[1024,512]{1,0:T(8,128)(2,1)}) custom-call(s32[2]{0:T(128)S(1)} %pad_add_fusion.1.me_ref, bf16[1024,1408]{1,0:T(8,128)(2,1)S(1)} %get-tuple-element.104.refs_0_.right_ref, bf16[1024,1408]{1,0:T(8,128)(2,1)} %all-gather.10.cloned.1.call-done.refs_1_.refs_3_, ...), custom_call_target="tpu_custom_call" | custom-call | flops 1048576 | bytes 262144 | tf_op jit(solution)/shard_map/piece/pallas_call | solution.py:405
  375.8 12.7 %piece.11 = (bf16[1024,512]{1,0:T(8,128)(2,1)}, f32[1024,512]{1,0:T(8,128)S(1)}) custom-call(s32[2]{0:T(128)S(1)} %pad_add_fusion.me_ref, bf16[1024,1408]{1,0:T(8,128)(2,1)} %copy-done.4, bf16[1024,1408]{1,0:T(8,128)(2,1)} %all-gather.10.cloned.1.call-done.refs_1_.refs_3_, bf16[1024,1408]{1,0:T(8,128)(2,1)} %collective-permute-done.12.refs_3_.refs_2_.refs_4_, ...), custom_call_target="tpu_custom_call" | custom-call | flops 1048576 | bytes 262144 | tf_op jit(solution)/shard_map/piece/pallas_call | solution.py:405
  398.2 17.1 %collective-permute-done.21 = bf16[1024,512]{1,0:T(8,128)(2,1)} collective-permute-done((bf16[1024,512]{1,0:T(8,128)(2,1)}, bf16[1024,512]{1,0:T(8,128)(2,1)}, u32[]{:S(2)}, u32[]{:S(2)}) %collective-permute-start.21) | collective-permute-done | bytes 1048608 | tf_op jit(solution)/shard_map/ppermute | solution.py:271
  420.3 41.7 %collective-permute-done.27.refs_0_ = bf16[1024,1408]{1,0:T(8,128)(2,1)} collective-permute-done((bf16[1024,1408]{1,0:T(8,128)(2,1)}, bf16[1024,1408]{1,0:T(8,128)(2,1)}, u32[]{:S(2)}, u32[]{:S(2)}) %collective-permute-start.27) | collective-permute-done | bytes 2883616 | tf_op jit(solution)/shard_map/ppermute | solution.py:271
  490.6 37.5 %mixer_backward.1 = (bf16[1024,1664]{1,0:T(8,128)(2,1)}, f32[4,1536]{1,0:T(4,128)}, f32[1,128]{1,0:T(1,128)}, f32[1024,1]{1,0:T(8,128)}) custom-call(f32[1024,1664]{1,0:T(8,128)} %halves.3.x_ref.prev_ref, f32[1024,1664]{1,0:T(8,128)} %halves.3.x_ref.prev_ref, f32[4,1536]{1,0:T(4,128)} %copy-done.55, f32[1,128]{1,0:T(1,128)} %bitcast.124, ...), custom_call_target="tpu_custom_call" | custom-call | flops 1048576 | bytes 262144 | tf_op jit(solution)/shard_map/mixer_backward/pallas_call | solution.py:234
  530.1 7.5 %piece.12 = (bf16[1024,512]{1,0:T(8,128)(2,1)}, bf16[1024,512]{1,0:T(8,128)(2,1)}) custom-call(s32[2]{0:T(128)S(1)} %pad_add_fusion.1.me_ref, bf16[1024,1664]{1,0:T(8,128)(2,1)S(1)} %copy-done.2, bf16[1024,1664]{1,0:T(8,128)(2,1)} %all-gather.8.cloned.1.call-done.refs_1_.refs_3_, bf16[1024,1664]{1,0:T(8,128)(2,1)} %collective-permute-done.7.refs_3_.refs_2_.refs_4_, ...), custom_call_target="tpu_custom_call" | custom-call | flops 1048576 | bytes 262144 | tf_op jit(solution)/shard_map/piece/pallas_call | solution.py:405
  542.3 6.5 rows.11
  552.2 7.8 %piece.13 = (bf16[1024,512]{1,0:T(8,128)(2,1)}, f32[1024,512]{1,0:T(8,128)S(1)}) custom-call(s32[2]{0:T(128)S(1)} %pad_add_fusion.me_ref, bf16[1024,1664]{1,0:T(8,128)(2,1)} %get-tuple-element.122.refs_0_.right_ref, bf16[1024,1664]{1,0:T(8,128)(2,1)} %all-gather.8.cloned.1.call-done.refs_1_.refs_3_, ...), custom_call_target="tpu_custom_call" | custom-call | flops 1048576 | bytes 262144 | tf_op jit(solution)/shard_map/piece/pallas_call | solution.py:405
  577.7 18.7 %collective-permute-done.33 = bf16[1024,512]{1,0:T(8,128)(2,1)} collective-permute-done((bf16[1024,512]{1,0:T(8,128)(2,1)}, bf16[1024,512]{1,0:T(8,128)(2,1)}, u32[]{:S(2)}, u32[]{:S(2)}) %collective-permute-start.33) | collective-permute-done | bytes 1048608 | tf_op jit(solution)/shard_map/ppermute | solution.py:271
  606.5 7.7 %collective-permute-done.36 = f32[81,128]{1,0:T(8,128)S(1)} collective-permute-done((f32[81,128]{1,0:T(8,128)S(1)}, f32[81,128]{1,0:T(8,128)S(1)}, u32[]{:S(2)}, u32[]{:S(2)}) %collective-permute-start.36) | collective-permute-done | bytes 41504 | tf_op jit(solution)/shard_map/ppermute | solution.py:271
  619.7 27.1 %collective-permute-done.25.refs_0_ = bf16[1024,1664]{1,0:T(8,128)(2,1)} collective-permute-done((bf16[1024,1664]{1,0:T(8,128)(2,1)}, bf16[1024,1664]{1,0:T(8,128)(2,1)}, u32[]{:S(2)}, u32[]{:S(2)}) %collective-permute-start.25) | collective-permute-done | bytes 3407904 | tf_op jit(solution)/shard_map/ppermute | solution.py:271
  646.8 7.7 %rows.15 = bf16[1024,1664]{1,0:T(8,128)(2,1)S(1)} custom-call(bf16[1024,2048]{1,0:T(8,128)(2,1)} %get-tuple-element.118.refs_0_.refs_2_.left_ref, bf16[1024,1664]{1,0:T(8,128)(2,1)} %get-tuple-element.122.refs_0_.right_ref, bf16[1024,1664]{1,0:T(8,128)(2,1)} %collective-permute-done.25.refs_0_), custom_call_target="tpu_custom_call" | custom-call | flops 1048576 | bytes 262144 | tf_op jit(solution)/shard_map/rows/pallas_call | solution.py:401
  658.1 6.8 piece.14
  676.3 6.5 piece.15
  697.0 10.9 %collective-permute-done.40 = bf16[1024,512]{1,0:T(8,128)(2,1)} collective-permute-done((bf16[1024,512]{1,0:T(8,128)(2,1)}, bf16[1024,512]{1,0:T(8,128)(2,1)}, u32[]{:S(2)}, u32[]{:S(2)}) %collective-permute-start.40) | collective-permute-done | bytes 1048608 | tf_op jit(solution)/shard_map/ppermute | solution.py:271
  711.9 10.8 %reduce-scatter.12.cloned.1.call-done = bf16[256,1664]{1,0:T(8,128)(2,1)} async-done(((bf16[1024,1664]{1,0:T(8,128)(2,1)}), bf16[256,1664]{1,0:T(8,128)(2,1)}) %reduce-scatter.12.cloned.1.call-update) | async-done | bytes 851984 | tf_op jit(solution)/shard_map/reduce_scatter | solution.py:577
  (326 shorter events, 208.5 us)
Async XLA Ops:
  7.2 73.8 %all-gather.8.cloned.1.call-start = ((), (), s32[]{:S(2)}) async-start(), calls=%async_computation.6 | async-start | bytes 4259840 | tf_op jit(solution)/shard_map/all_gather | solution.py:573
  10.3 99.4 %all-gather.6.cloned.1.call-start = ((), (), s32[]{:S(2)}) async-start(), calls=%async_computation.5 | async-start | bytes 1310720 | tf_op jit(solution)/shard_map/all_gather | solution.py:573
  11.2 159.3 %all-gather.10.cloned.1.call-start = ((), (), s32[]{:S(2)}) async-start(), calls=%async_computation.7 | async-start | bytes 3604480 | tf_op jit(solution)/shard_map/all_gather | solution.py:573
  11.9 217.3 %all-gather.12.cloned.1.call-start = ((), (), s32[]{:S(2)}) async-start(), calls=%async_computation.8 | async-start | bytes 3604480 | tf_op jit(solution)/shard_map/all_gather | solution.py:573
  12.5 324.2 %all-gather.14.cloned.1.call-start = ((), (), s32[]{:S(2)}) async-start(), calls=%async_computation.9 | async-start | bytes 7208960 | tf_op jit(solution)/shard_map/all_gather | solution.py:573
  12.9 19.2 %collective-permute-start.3 = (bf16[256,1408]{1,0:T(8,128)(2,1)S(1)}, bf16[256,1408]{1,0:T(8,128)(2,1)}, u32[]{:S(2)}, u32[]{:S(2)}) collective-permute-start(bf16[256,1408]{1,0:T(8,128)(2,1)S(1)} %bitcast.103), channel_id=1, source_target_pairs={{0,4},{4,0},{8,12},{12,8},{16,20},{20,16},{24,28},{28,24},{1,5},{5... | collective-permute-start | bytes 2162696 | tf_op jit(solution)/shard_map/ppermute | solution.py:271
  21.1 26.3 %collective-permute-start.1 = (bf16[1024,512]{1,0:T(8,128)(2,1)S(1)}, bf16[1024,512]{1,0:T(8,128)(2,1)}, u32[]{:S(2)}, u32[]{:S(2)}) collective-permute-start(bf16[1024,512]{1,0:T(8,128)(2,1)S(1)} %pad_maximum_fusion.2.refs_0_), channel_id=1, source_target_pairs={{0,2},{1,3},{2,0},{3,1},{4,6},{5,7},{6,4},{7,5},{8,10},{9,11},{10,... | collective-permute-start | bytes 3145736 | tf_op jit(solution)/shard_map/ppermute | solution.py:271
  32.2 36.1 %collective-permute-start.5 = (bf16[1024,512]{1,0:T(8,128)(2,1)S(1)}, bf16[1024,512]{1,0:T(8,128)(2,1)S(1)}, u32[]{:S(2)}, u32[]{:S(2)}) collective-permute-start(bf16[1024,512]{1,0:T(8,128)(2,1)S(1)} %fusion.9.refs_0_), channel_id=1, source_target_pairs={{0,2},{1,3},{2,0},{3,1},{4,6},{5,7},{6,4},{7,5},{8,10},{9,11},{10,... | collective-permute-start | bytes 3145736 | tf_op jit(solution)/shard_map/ppermute | solution.py:271
  33.9 35.1 %collective-permute-start = (bf16[1024,512]{1,0:T(8,128)(2,1)S(1)}, bf16[1024,512]{1,0:T(8,128)(2,1)}, u32[]{:S(2)}, u32[]{:S(2)}) collective-permute-start(bf16[1024,512]{1,0:T(8,128)(2,1)S(1)} %pad_maximum_fusion.2.refs_0_), channel_id=1, source_target_pairs={{0,1},{1,0},{2,3},{3,2},{4,5},{5,4},{6,7},{7,6},{8,9},{9,8},{10,11... | collective-permute-start | bytes 3145736 | tf_op jit(solution)/shard_map/ppermute | solution.py:271
  47.4 21.7 %collective-permute-start.2 = (bf16[1024,512]{1,0:T(8,128)(2,1)}, bf16[1024,512]{1,0:T(8,128)(2,1)}, u32[]{:S(2)}, u32[]{:S(2)}) collective-permute-start(bf16[1024,512]{1,0:T(8,128)(2,1)} %collective-permute-done.1.refs_2_), channel_id=1, source_target_pairs={{0,1},{1,0},{2,3},{3,2},{4,5},{5,4},{6,7},{7,6},{8,9},{9,8},{10,11... | collective-permute-start | bytes 3145736 | tf_op jit(solution)/shard_map/ppermute | solution.py:271
  47.4 26.8 %collective-permute-start.4 = (bf16[1024,512]{1,0:T(8,128)(2,1)S(1)}, bf16[1024,512]{1,0:T(8,128)(2,1)}, u32[]{:S(2)}, u32[]{:S(2)}) collective-permute-start(bf16[1024,512]{1,0:T(8,128)(2,1)S(1)} %fusion.9.refs_0_), channel_id=1, source_target_pairs={{0,1},{1,0},{2,3},{3,2},{4,5},{5,4},{6,7},{7,6},{8,9},{9,8},{10,11... | collective-permute-start | bytes 3145736 | tf_op jit(solution)/shard_map/ppermute | solution.py:271
  80.9 76.9 %collective-permute-start.7 = (bf16[1024,1664]{1,0:T(8,128)(2,1)}, bf16[1024,1664]{1,0:T(8,128)(2,1)}, u32[]{:S(2)}, u32[]{:S(2)}) collective-permute-start(bf16[1024,1664]{1,0:T(8,128)(2,1)} %all-gather.8.cloned.1.call-done.refs_1_.refs_3_), channel_id=1, source_target_pairs={{0,4},{4,0},{8,12},{12,8},{16,20},{20,16},{24,28},{28,24},{1,5},{5... | collective-permute-start | bytes 10223624 | tf_op jit(solution)/shard_map/ppermute | solution.py:271
  85.0 478.7 %reduce-scatter.8.cloned.1.call-start = ((), (), s32[]{:S(2)}) async-start(), calls=%async_computation.11 | async-start | bytes 6488064 | tf_op jit(solution)/shard_map/reduce_scatter | solution.py:594
  109.7 97.2 %collective-permute-start.8 = (bf16[1024,512]{1,0:T(8,128)(2,1)}, bf16[1024,512]{1,0:T(8,128)(2,1)}, u32[]{:S(2)}, u32[]{:S(2)}) collective-permute-start(bf16[1024,512]{1,0:T(8,128)(2,1)} %all-gather.6.cloned.1.call-done.refs_1_.refs_3_), channel_id=1, source_target_pairs={{0,4},{4,0},{8,12},{12,8},{16,20},{20,16},{24,28},{28,24},{1,5},{5... | collective-permute-start | bytes 3145736 | tf_op jit(solution)/shard_map/ppermute | solution.py:271
  170.5 78.0 %collective-permute-start.12 = (bf16[1024,1408]{1,0:T(8,128)(2,1)}, bf16[1024,1408]{1,0:T(8,128)(2,1)}, u32[]{:S(2)}, u32[]{:S(2)}) collective-permute-start(bf16[1024,1408]{1,0:T(8,128)(2,1)} %all-gather.10.cloned.1.call-done.refs_1_.refs_3_), channel_id=1, source_target_pairs={{0,4},{4,0},{8,12},{12,8},{16,20},{20,16},{24,28},{28,24},{1,5},{5... | collective-permute-start | bytes 8650760 | tf_op jit(solution)/shard_map/ppermute | solution.py:271
  221.0 25.4 %collective-permute-start.11 = (bf16[1024,512]{1,0:T(8,128)(2,1)}, bf16[1024,512]{1,0:T(8,128)(2,1)S(1)}, u32[]{:S(2)}, u32[]{:S(2)}) collective-permute-start(bf16[1024,512]{1,0:T(8,128)(2,1)} %get-tuple-element.88), channel_id=1, source_target_pairs={{0,2},{1,3},{2,0},{3,1},{4,6},{5,7},{6,4},{7,5},{8,10},{9,11},{10,... | collective-permute-start | bytes 3145736 | tf_op jit(solution)/shard_map/ppermute | solution.py:271
  229.3 73.5 %collective-permute-start.16 = (bf16[1024,1408]{1,0:T(8,128)(2,1)}, bf16[1024,1408]{1,0:T(8,128)(2,1)}, u32[]{:S(2)}, u32[]{:S(2)}) collective-permute-start(bf16[1024,1408]{1,0:T(8,128)(2,1)} %all-gather.12.cloned.1.call-done.refs_2_.refs_6_.refs_8_), channel_id=1, source_target_pairs={{0,4},{4,0},{8,12},{12,8},{16,20},{20,16},{24,28},{28,24},{1,5},{5... | collective-permute-start | bytes 8650760 | tf_op jit(solution)/shard_map/ppermute | solution.py:271
  249.9 24.5 %collective-permute-start.14 = (bf16[1024,512]{1,0:T(8,128)(2,1)S(1)}, bf16[1024,512]{1,0:T(8,128)(2,1)S(1)}, u32[]{:S(2)}, u32[]{:S(2)}) collective-permute-start(bf16[1024,512]{1,0:T(8,128)(2,1)S(1)} %fusion.7.refs_0_), channel_id=1, source_target_pairs={{0,2},{1,3},{2,0},{3,1},{4,6},{5,7},{6,4},{7,5},{8,10},{9,11},{10,... | collective-permute-start | bytes 3145736 | tf_op jit(solution)/shard_map/ppermute | solution.py:271
  251.3 23.7 %collective-permute-start.13 = (bf16[1024,512]{1,0:T(8,128)(2,1)S(1)}, bf16[1024,512]{1,0:T(8,128)(2,1)S(1)}, u32[]{:S(2)}, u32[]{:S(2)}) collective-permute-start(bf16[1024,512]{1,0:T(8,128)(2,1)S(1)} %fusion.7.refs_0_), channel_id=1, source_target_pairs={{0,1},{1,0},{2,3},{3,2},{4,5},{5,4},{6,7},{7,6},{8,9},{9,8},{10,11... | collective-permute-start | bytes 3145736 | tf_op jit(solution)/shard_map/ppermute | solution.py:271
  326.9 246.3 %reduce-scatter.6.cloned.1.call-start = ((), (), s32[]{:S(2)}) async-start(), calls=%async_computation.10 | async-start | bytes 3604480 | tf_op jit(solution)/shard_map/reduce_scatter | solution.py:577
  373.7 88.3 %collective-permute-start.27 = (bf16[1024,1408]{1,0:T(8,128)(2,1)}, bf16[1024,1408]{1,0:T(8,128)(2,1)}, u32[]{:S(2)}, u32[]{:S(2)}) collective-permute-start(bf16[1024,1408]{1,0:T(8,128)(2,1)} %rows.8), channel_id=1, source_target_pairs={{0,4},{4,0},{8,12},{12,8},{16,20},{20,16},{24,28},{28,24},{1,5},{5... | collective-permute-start | bytes 8650760 | tf_op jit(solution)/shard_map/ppermute | solution.py:271
  389.8 25.6 %collective-permute-start.21 = (bf16[1024,512]{1,0:T(8,128)(2,1)}, bf16[1024,512]{1,0:T(8,128)(2,1)}, u32[]{:S(2)}, u32[]{:S(2)}) collective-permute-start(bf16[1024,512]{1,0:T(8,128)(2,1)} %get-tuple-element.106), channel_id=1, source_target_pairs={{0,2},{1,3},{2,0},{3,1},{4,6},{5,7},{6,4},{7,5},{8,10},{9,11},{10,... | collective-permute-start | bytes 3145736 | tf_op jit(solution)/shard_map/ppermute | solution.py:271
  418.9 43.1 %collective-permute-start.23 = (bf16[1024,512]{1,0:T(8,128)(2,1)S(1)}, bf16[1024,512]{1,0:T(8,128)(2,1)}, u32[]{:S(2)}, u32[]{:S(2)}) collective-permute-start(bf16[1024,512]{1,0:T(8,128)(2,1)S(1)} %get-tuple-element.173.refs_0_), channel_id=1, source_target_pairs={{0,2},{1,3},{2,0},{3,1},{4,6},{5,7},{6,4},{7,5},{8,10},{9,11},{10,... | collective-permute-start | bytes 3145736 | tf_op jit(solution)/shard_map/ppermute | solution.py:271
  469.7 177.0 %reduce-scatter.10.cloned.1.call-start = ((), (), s32[]{:S(2)}) async-start(), calls=%async_computation.12 | async-start | bytes 3604480 | tf_op jit(solution)/shard_map/reduce_scatter | solution.py:577
  469.8 91.5 %collective-permute-start.28 = (bf16[1024,1408]{1,0:T(8,128)(2,1)}, bf16[1024,1408]{1,0:T(8,128)(2,1)}, u32[]{:S(2)}, u32[]{:S(2)}) collective-permute-start(bf16[1024,1408]{1,0:T(8,128)(2,1)} %copy-done.21), channel_id=1, source_target_pairs={{0,4},{4,0},{8,12},{12,8},{16,20},{20,16},{24,28},{28,24},{1,5},{5... | collective-permute-start | bytes 8650760 | tf_op jit(solution)/shard_map/ppermute | solution.py:271
  537.6 14.6 %collective-permute-start.31 = (bf16[1024,512]{1,0:T(8,128)(2,1)}, bf16[1024,512]{1,0:T(8,128)(2,1)}, u32[]{:S(2)}, u32[]{:S(2)}) collective-permute-start(bf16[1024,512]{1,0:T(8,128)(2,1)} %get-tuple-element.117), channel_id=1, source_target_pairs={{0,1},{1,0},{2,3},{3,2},{4,5},{5,4},{6,7},{7,6},{8,9},{9,8},{10,11... | collective-permute-start | bytes 3145736 | tf_op jit(solution)/shard_map/ppermute | solution.py:271
  538.1 25.6 %collective-permute-start.26 = (bf16[1024,512]{1,0:T(8,128)(2,1)}, bf16[1024,512]{1,0:T(8,128)(2,1)}, u32[]{:S(2)}, u32[]{:S(2)}) collective-permute-start(bf16[1024,512]{1,0:T(8,128)(2,1)} %rows.10), channel_id=1, source_target_pairs={{0,4},{4,0},{8,12},{12,8},{16,20},{20,16},{24,28},{28,24},{1,5},{5... | collective-permute-start | bytes 3145736 | tf_op jit(solution)/shard_map/ppermute | solution.py:271
  571.4 119.3 %reduce-scatter.14.cloned.1.call-start = ((), (), s32[]{:S(2)}) async-start(), calls=%async_computation.14 | async-start | bytes 1310720 | tf_op jit(solution)/shard_map/reduce_scatter | solution.py:577
  571.4 75.4 %collective-permute-start.25 = (bf16[1024,1664]{1,0:T(8,128)(2,1)}, bf16[1024,1664]{1,0:T(8,128)(2,1)}, u32[]{:S(2)}, u32[]{:S(2)}) collective-permute-start(bf16[1024,1664]{1,0:T(8,128)(2,1)} %copy-done.19), channel_id=1, source_target_pairs={{0,4},{4,0},{8,12},{12,8},{16,20},{20,16},{24,28},{28,24},{1,5},{5... | collective-permute-start | bytes 10223624 | tf_op jit(solution)/shard_map/ppermute | solution.py:271
  571.8 24.7 %collective-permute-start.33 = (bf16[1024,512]{1,0:T(8,128)(2,1)}, bf16[1024,512]{1,0:T(8,128)(2,1)}, u32[]{:S(2)}, u32[]{:S(2)}) collective-permute-start(bf16[1024,512]{1,0:T(8,128)(2,1)} %get-tuple-element.126), channel_id=1, source_target_pairs={{0,2},{1,3},{2,0},{3,1},{4,6},{5,7},{6,4},{7,5},{8,10},{9,11},{10,... | collective-permute-start | bytes 3145736 | tf_op jit(solution)/shard_map/ppermute | solution.py:271
  577.4 145.3 %reduce-scatter.12.cloned.1.call-start = ((), (), s32[]{:S(2)}) async-start(), calls=%async_computation.13 | async-start | bytes 4259840 | tf_op jit(solution)/shard_map/reduce_scatter | solution.py:577
  682.8 25.2 %collective-permute-start.40 = (bf16[1024,512]{1,0:T(8,128)(2,1)}, bf16[1024,512]{1,0:T(8,128)(2,1)}, u32[]{:S(2)}, u32[]{:S(2)}) collective-permute-start(bf16[1024,512]{1,0:T(8,128)(2,1)} %get-tuple-element.135), channel_id=1, source_target_pairs={{0,2},{1,3},{2,0},{3,1},{4,6},{5,7},{6,4},{7,5},{8,10},{9,11},{10,... | collective-permute-start | bytes 3145736 | tf_op jit(solution)/shard_map/ppermute | solution.py:271
  (83 other events, 1062.1 us)
Sparse Core Ops, SparseCore 0:
  10.4 70.5 all-gather.7
  83.1 26.5 all-gather.5
  111.2 58.6 all-gather.9
  171.4 57.8 all-gather.11
  231.3 105.3 all-gather.13
  340.2 129.3 reduce-scatter.7
  471.8 54.7 reduce-scatter.5
  571.5 55.8 reduce-scatter.9
  630.3 27.0 reduce-scatter.13
  659.6 62.9 reduce-scatter.11

commit v6 on v5

--- a/solution.py
+++ b/solution.py
@@ -548,9 +548,9 @@
         start += part
 
 
-def rows_call(left, right, first, parts, tile, gots=()):
-    rows, width, count = left.shape[0], right.shape[1], sum(parts)
-    specs = [pl.BlockSpec((rows, tile), lambda i: (0, first + i)), whole(right.shape)]
+def rows_call(left, right, first, parts, tile, gots=(), width=None):
+    rows, width, count = left.shape[0], width or right.shape[1], sum(parts)
+    specs = [pl.BlockSpec((rows, tile), lambda i: (0, first + i)), whole((rows, width))]
     start = 0
     for _, part in zip(gots, parts):
         specs.append(pl.BlockSpec((tile, width), lambda i, s=start, p=part: (jnp.clip(i - s, 0, p - 1), 0)))
@@ -594,19 +594,24 @@
     return lax.psum_scatter(part, "row", scatter_dimension=0, tiled=True, axis_index_groups=[even + odd])
 
 
-def trade_rows(left, right, parts=(2,)):
+def trade_rows(left, right, parts=(2,), width=None):
     tile = left.shape[1] // 2 // sum(parts)
     sent, first = [], sum(parts)
     for part in parts:
-        sent.append(rows_call(left, right, first, (part,), tile))
+        sent.append(rows_call(left, right, first, (part,), tile, width=width))
         first += part
     return sent, [swap(part, "row", 1) for part in sent]
+
+
+def got_width(gots):
+    return gots[0].shape[1]
 
 
 def own_rows(left, right, gots, *earlier):
     first = after(gots[0], *gots[1:], *earlier)
     tile = 512 if len(gots) == 1 else min(got.shape[0] for got in gots)
-    return rows_call(left, right, 0, tuple(got.shape[0] // tile for got in gots), tile, [first, *gots[1:]])
+    parts = tuple(got.shape[0] // tile for got in gots)
+    return rows_call(left, right, 0, parts, tile, [first, *gots[1:]], got_width(gots))
 
 
 def flip(first, second):
@@ -710,7 +715,8 @@
     low, gconv, ghead, inner_in = mixer_backward(proj, conv, gain, mixed_cot, kept, heads, dh)
     in_sum = ColSum([(low, w_in)], block)
     sent = in_sum.send(1)
-    low_sent, low_got = trade_rows(after(normed, *sent), low)
+    low_sent, low_got = trade_rows(after(normed, *sent), low, width=3 * hd)
+    beta_part = by_place(dot(low[:, 3 * hd :], after(normed, *low_sent), 0, 0)[: beta_weight.shape[1]], chunk)
     inner_in = sum_all(inner_in.reshape(rows // 128, 128), "col").reshape(rows, 1) / factor_in
     in_sum.send_last(inner_in, *low_sent)
     up_rows = own_rows(normed_mid, up_cot, up_got, *out_got, in_sum.base, grad_down)
@@ -727,7 +733,7 @@
 
     sizes = [feat, feat, dh]
     wide = sum_all(jnp.concatenate([own_cols(gin_part), own_cols(gmid_part), ghead[0]]).reshape(-1, 128), "col")
-    small = jnp.concatenate([wide, gconv.reshape(-1, 128)], 0)
+    small = jnp.concatenate([wide, gconv.reshape(-1, 128), beta_part.reshape(-1, 128)], 0)
     bits = bits_down(lax.axis_size("row"))
     for bit in bits[:-1]:
         small = small + swap(small, "row", bit)
@@ -743,7 +749,7 @@
 
     sizes = [feat, feat, dh]
     wide = sum_all(jnp.concatenate([own_cols(gin_part), own_cols(gmid_part), ghead[0]]).reshape(-1, 128), "col")
-    small = jnp.concatenate([wide, gconv.reshape(-1, 128)], 0)
+    small = jnp.concatenate([wide, gconv.reshape(-1, 128), beta_part.reshape(-1, 128)], 0)
     bits = bits_down(lax.axis_size("row"))
     for bit in bits[:-1]:
         small = small + swap(small, "row", bit)
@@ -754,7 +760,10 @@
     result.send_last(*sent)
     layer_out = (middle + live * result.total()).astype(bf16)
     small = small + swap(small, "row", bits[-1])
-    wide, gconv = small[: wide.shape[0]].reshape(-1), small[wide.shape[0] :].reshape(gconv.shape)
+    cuts = [wide.shape[0], wide.shape[0] + gconv.size // 128]
+    wide, gconv = small[: cuts[0]].reshape(-1), small[cuts[0] : cuts[1]].reshape(gconv.shape)
+    beta_sum = small[cuts[1] :].reshape(beta_part.shape)
+    grad_beta = lax.dynamic_slice_in_dim(beta_sum, lax.axis_index("row") * chunk, chunk, 1).T
     g_low = grad_low.astype(f32)
     return (
         by_place(layer_out, chunk),
@@ -766,7 +775,7 @@
         gconv[:, :hd],
         gconv[:, hd : 2 * hd],
         gconv[:, 2 * hd :],
-        g_low[:, 3 * hd : 3 * hd + beta_weight.shape[1]],
+        grad_beta,
         wide[2 * feat :],
         grad_out.astype(f32).T,
         wide[feat : 2 * feat],

time: 739 us -> 734 us (level)
  waiting for transfers between devices: 341 us -> 333 us
    ppermute x42, waiting for transfers between devices: 285 us -> 277 us  [swap(): return lax.ppermute(x, axis, [(i, i ^ bit) for i in range(n)])]
    unnamed x144 -> x141, local copies, waits for them, and re-layouts: 42.8 us -> 42.1 us
  transfers between devices with their start and end apart: 52 -> 52, of which waited for: 29 -> 29; matrix products, arithmetic and copies ran while one was open for 7% -> 8% of each run, Pallas kernels for 35% -> 35%
where the time goes in v6:
time: 734 us; the launch traced here: 729 us
  waiting for transfers between devices  333 us (45%)
  Pallas kernels  257 us (35%)
  local copies, waits for them, and re-layouts  52.7 us (7%)
  starting transfers between devices  32.7 us (4%)
  other arithmetic  32.3 us (4%)
  between operations  16 us (2%)
    ppermute x42, waiting for transfers between devices, swap(): return lax.ppermute(x, axis, [(i, i ^ bit) for i in range(n)])  277 us
    pallas_call x13, Pallas kernels, tile_call(): pl.pallas_call(kernel, grid=grid, in_specs=specs, out_specs=out_specs, ou...  95.9 us
    pallas_call x9, Pallas kernels, tile_call(): pl.pallas_call(kernel, grid_spec=grid_spec, out_shape=outs, **params)  71.1 us
    all_gather x5, waiting for transfers between devices, gather_parity(): lax.all_gather(shard, 'row', axis=0, tiled=True, axis_index_groups=parity...  43.9 us
    unnamed x141, local copies, waits for them, and re-layouts  42.1 us
    pallas_call x1, Pallas kernels, mixer_backward(): pl.pallas_call(functools.partial(bwd_kernel, heads, dh), grid=(steps,), i...  37.5 us
    pallas_call x1, Pallas kernels, mixer_forward(): pl.pallas_call(functools.partial(fwd_kernel, heads, dh), grid=(steps,), i...  34.2 us
    ppermute x42, starting transfers between devices, swap(): return lax.ppermute(x, axis, [(i, i ^ bit) for i in range(n)])  31.9 us
  transfers between devices with their start and end apart: 52, of which 29 were waited for; matrix products, arithmetic and copies ran while one was open for 8% of the time, Pallas kernels for 35%

profile of v6, /device:TPU:0, one launch (start us, length us, event | category | flops | bytes accessed | tf_op | source)
XLA Modules:
  0.0 728.5 jit_solution(17819107875171870366)
XLA Ops:
  23.7 8.4 %collective-permute-done.3 = bf16[256,1408]{1,0:T(8,128)(2,1)} collective-permute-done((bf16[256,1408]{1,0:T(8,128)(2,1)S(1)}, bf16[256,1408]{1,0:T(8,128)(2,1)}, u32[]{:S(2)}, u32[]{:S(2)}) %collective-permute-start.3) | collective-permute-done | bytes 720928 | tf_op jit(solution)/shard_map/ppermute | solution.py:271
  33.9 13.4 %collective-permute-done.1.refs_2_ = bf16[1024,512]{1,0:T(8,128)(2,1)} collective-permute-done((bf16[1024,512]{1,0:T(8,128)(2,1)S(1)}, bf16[1024,512]{1,0:T(8,128)(2,1)}, u32[]{:S(2)}, u32[]{:S(2)}) %collective-permute-start.1) | collective-permute-done | bytes 1048608 | tf_op jit(solution)/shard_map/ppermute | solution.py:271
  47.9 20.4 %collective-permute-done.5.refs_2_ = bf16[1024,512]{1,0:T(8,128)(2,1)S(1)} collective-permute-done((bf16[1024,512]{1,0:T(8,128)(2,1)S(1)}, bf16[1024,512]{1,0:T(8,128)(2,1)S(1)}, u32[]{:S(2)}, u32[]{:S(2)}) %collective-permute-start.5) | collective-permute-done | bytes 1048608 | tf_op jit(solution)/shard_map/ppermute | solution.py:271
  85.2 24.5 %all-gather.6.cloned.1.call-done.refs_1_.refs_3_ = bf16[1024,512]{1,0:T(8,128)(2,1)} async-done(((bf16[256,512]{1,0:T(8,128)(2,1)}), bf16[1024,512]{1,0:T(8,128)(2,1)}) %all-gather.6.cloned.1.call-update) | async-done | bytes 1048592 | tf_op jit(solution)/shard_map/all_gather | solution.py:573
  111.1 46.7 %collective-permute-done.7.refs_3_.refs_2_.refs_4_ = bf16[1024,1664]{1,0:T(8,128)(2,1)} collective-permute-done((bf16[1024,1664]{1,0:T(8,128)(2,1)}, bf16[1024,1664]{1,0:T(8,128)(2,1)}, u32[]{:S(2)}, u32[]{:S(2)}) %collective-permute-start.7) | collective-permute-done | bytes 3407904 | tf_op jit(solution)/shard_map/ppermute | solution.py:271
  157.9 12.6 %halves.3.x_ref.prev_ref = f32[1024,1664]{1,0:T(8,128)} custom-call(bf16[1024,2048]{1,0:T(8,128)(2,1)} %get-tuple-element.130.refs_0_.refs_2_.left_ref, bf16[1024,1664]{1,0:T(8,128)(2,1)S(1)} %copy-done, bf16[1024,2048]{1,0:T(8,128)(2,1)} %get-tuple-element.130.refs_0_.refs_2_.left_ref, bf16[1024,1664]{1,0:T(8,128)(2,1)} %collective-permute-done.7.refs_3_.refs_2_.refs_4_), custom_call_target="tpu_custom_call" | custom-call | flops 1048576 | bytes 262144 | tf_op jit(solution)/shard_map/halves/pallas_call | solution.py:401
  172.7 34.2 %mixer_forward.1 = (bf16[1024,512]{1,0:T(8,128)(2,1)}, f32[1024,512]{1,0:T(8,128)}, f32[1024,512]{1,0:T(8,128)}, f32[8,4,128,128]{3,2,1,0:T(8,128)}, f32[8,4,128,128]{3,2,1,0:T(8,128)}) custom-call(f32[1024,1664]{1,0:T(8,128)} %halves.3.x_ref.prev_ref, f32[4,1536]{1,0:T(4,128)} %copy-done.54, f32[1,128]{1,0:T(1,128)} %bitcast.126), custom_call_target="tpu_custom_call" | custom-call | flops 1048576 | bytes 262144 | tf_op jit(solution)/shard_map/mixer_forward/pallas_call | solution.py:202
  222.5 6.8 all-gather.12.cloned.1.call-done.refs_2_.refs_6_.refs_8_
  230.7 15.7 %collective-permute-done.11 = bf16[1024,512]{1,0:T(8,128)(2,1)S(1)} collective-permute-done((bf16[1024,512]{1,0:T(8,128)(2,1)}, bf16[1024,512]{1,0:T(8,128)(2,1)S(1)}, u32[]{:S(2)}, u32[]{:S(2)}) %collective-permute-start.11) | collective-permute-done | bytes 1048608 | tf_op jit(solution)/shard_map/ppermute | solution.py:271
  251.3 23.0 %collective-permute-done.14.refs_2_ = bf16[1024,512]{1,0:T(8,128)(2,1)S(1)} collective-permute-done((bf16[1024,512]{1,0:T(8,128)(2,1)S(1)}, bf16[1024,512]{1,0:T(8,128)(2,1)S(1)}, u32[]{:S(2)}, u32[]{:S(2)}) %collective-permute-start.14) | collective-permute-done | bytes 1048608 | tf_op jit(solution)/shard_map/ppermute | solution.py:271
  282.3 9.4 %halves.4.refs_4_ = bf16[1024,1408]{1,0:T(8,128)(2,1)S(1)} custom-call(bf16[1024,2048]{1,0:T(8,128)(2,1)} %get-tuple-element.108.refs_0_.refs_2_.refs_1_.left_ref, bf16[1024,1408]{1,0:T(8,128)(2,1)S(1)} %copy-done.1, bf16[1024,2048]{1,0:T(8,128)(2,1)} %get-tuple-element.108.refs_0_.refs_2_.refs_1_.left_ref, ...), custom_call_target="tpu_custom_call" | custom-call | flops 1048576 | bytes 262144 | tf_op jit(solution)/shard_map/halves/pallas_call | solution.py:401
  293.3 9.5 %collective-permute-done.16.refs_3_.refs_7_.refs_9_ = bf16[1024,1408]{1,0:T(8,128)(2,1)} collective-permute-done((bf16[1024,1408]{1,0:T(8,128)(2,1)}, bf16[1024,1408]{1,0:T(8,128)(2,1)}, u32[]{:S(2)}, u32[]{:S(2)}) %collective-permute-start.16) | collective-permute-done | bytes 2883616 | tf_op jit(solution)/shard_map/ppermute | solution.py:271
  302.7 11.3 %hidden.1 = (bf16[1024,1408]{1,0:T(8,128)(2,1)S(1)}, bf16[1024,1408]{1,0:T(8,128)(2,1)S(1)}) custom-call(bf16[1024,2048]{1,0:T(8,128)(2,1)} %get-tuple-element.108.refs_0_.refs_2_.refs_1_.left_ref, bf16[1024,2048]{1,0:T(8,128)(2,1)} %get-tuple-element.108.refs_0_.refs_2_.refs_1_.left_ref, ...), custom_call_target="tpu_custom_call" | custom-call | flops 1048576 | bytes 262144 | tf_op jit(solution)/shard_map/hidden/pallas_call | solution.py:401
  315.6 9.7 %all_rows.1 = bf16[2048,1408]{1,0:T(8,128)(2,1)} custom-call(s32[1]{0:T(128)} %bitcast.22.odd_ref, bf16[1024,2048]{1,0:T(8,128)(2,1)} %join.2.left_ref.refs_0_.refs_1_, bf16[1024,1408]{1,0:T(8,128)(2,1)S(1)} %get-tuple-element.135.right_ref.refs_0_), custom_call_target="tpu_custom_call" | custom-call | flops 1048576 | bytes 262144 | tf_op jit(solution)/shard_map/all_rows/pallas_call | solution.py:405
  326.9 9.7 %all-gather.14.cloned.1.call-done = bf16[2048,1408]{1,0:T(8,128)(2,1)} async-done(((bf16[512,1408]{1,0:T(8,128)(2,1)}), bf16[2048,1408]{1,0:T(8,128)(2,1)}) %all-gather.14.cloned.1.call-update) | async-done | bytes 5767184 | tf_op jit(solution)/shard_map/all_gather | solution.py:573
  336.7 14.7 %cots.1 = (bf16[1024,1408]{1,0:T(8,128)(2,1)S(1)}, bf16[1024,1408]{1,0:T(8,128)(2,1)}, f32[1024,1]{1,0:T(8,128)S(1)}) custom-call(bf16[1024,2048]{1,0:T(8,128)(2,1)} %join.2.left_ref.refs_0_.refs_1_, bf16[1024,2048]{1,0:T(8,128)(2,1)} %join.2.left_ref.refs_0_.refs_1_, bf16[4,2,256,1408]{3,2,1,0:T(8,128)(2,1)} %bitcast.92, ...), custom_call_target="tpu_custom_call" | custom-call | flops 1048576 | bytes 262144 | tf_op jit(solution)/shard_map/cots/pallas_call | solution.py:401
  351.4 11.8 %piece.10 = (bf16[1024,512]{1,0:T(8,128)(2,1)}, bf16[1024,512]{1,0:T(8,128)(2,1)}) custom-call(s32[2]{0:T(128)S(1)} %pad_add_fusion.1.me_ref, bf16[1024,1408]{1,0:T(8,128)(2,1)S(1)} %get-tuple-element.105.refs_0_.right_ref, bf16[1024,1408]{1,0:T(8,128)(2,1)} %all-gather.10.cloned.1.call-done.refs_1_.refs_3_, ...), custom_call_target="tpu_custom_call" | custom-call | flops 1048576 | bytes 262144 | tf_op jit(solution)/shard_map/piece/pallas_call | solution.py:405
  375.8 12.7 %piece.11 = (bf16[1024,512]{1,0:T(8,128)(2,1)}, f32[1024,512]{1,0:T(8,128)S(1)}) custom-call(s32[2]{0:T(128)S(1)} %pad_add_fusion.me_ref, bf16[1024,1408]{1,0:T(8,128)(2,1)} %copy-done.4, bf16[1024,1408]{1,0:T(8,128)(2,1)} %all-gather.10.cloned.1.call-done.refs_1_.refs_3_, bf16[1024,1408]{1,0:T(8,128)(2,1)} %collective-permute-done.12.refs_3_.refs_2_.refs_4_, ...), custom_call_target="tpu_custom_call" | custom-call | flops 1048576 | bytes 262144 | tf_op jit(solution)/shard_map/piece/pallas_call | solution.py:405
  398.2 17.1 %collective-permute-done.21 = bf16[1024,512]{1,0:T(8,128)(2,1)} collective-permute-done((bf16[1024,512]{1,0:T(8,128)(2,1)}, bf16[1024,512]{1,0:T(8,128)(2,1)}, u32[]{:S(2)}, u32[]{:S(2)}) %collective-permute-start.21) | collective-permute-done | bytes 1048608 | tf_op jit(solution)/shard_map/ppermute | solution.py:271
  420.3 41.7 %collective-permute-done.27.refs_0_ = bf16[1024,1408]{1,0:T(8,128)(2,1)} collective-permute-done((bf16[1024,1408]{1,0:T(8,128)(2,1)}, bf16[1024,1408]{1,0:T(8,128)(2,1)}, u32[]{:S(2)}, u32[]{:S(2)}) %collective-permute-start.27) | collective-permute-done | bytes 2883616 | tf_op jit(solution)/shard_map/ppermute | solution.py:271
  490.6 37.5 %mixer_backward.1 = (bf16[1024,1664]{1,0:T(8,128)(2,1)}, f32[4,1536]{1,0:T(4,128)}, f32[1,128]{1,0:T(1,128)}, f32[1024,1]{1,0:T(8,128)}) custom-call(f32[1024,1664]{1,0:T(8,128)} %halves.3.x_ref.prev_ref, f32[1024,1664]{1,0:T(8,128)} %halves.3.x_ref.prev_ref, f32[4,1536]{1,0:T(4,128)} %copy-done.54, f32[1,128]{1,0:T(1,128)} %bitcast.127, ...), custom_call_target="tpu_custom_call" | custom-call | flops 1048576 | bytes 262144 | tf_op jit(solution)/shard_map/mixer_backward/pallas_call | solution.py:234
  530.1 7.5 %piece.12 = (bf16[1024,512]{1,0:T(8,128)(2,1)}, bf16[1024,512]{1,0:T(8,128)(2,1)}) custom-call(s32[2]{0:T(128)S(1)} %pad_add_fusion.1.me_ref, bf16[1024,1664]{1,0:T(8,128)(2,1)S(1)} %copy-done.2, bf16[1024,1664]{1,0:T(8,128)(2,1)} %all-gather.8.cloned.1.call-done.refs_1_.refs_3_, bf16[1024,1664]{1,0:T(8,128)(2,1)} %collective-permute-done.7.refs_3_.refs_2_.refs_4_, ...), custom_call_target="tpu_custom_call" | custom-call | flops 1048576 | bytes 262144 | tf_op jit(solution)/shard_map/piece/pallas_call | solution.py:405
  551.5 7.8 %piece.13 = (bf16[1024,512]{1,0:T(8,128)(2,1)}, f32[1024,512]{1,0:T(8,128)S(1)}) custom-call(s32[2]{0:T(128)S(1)} %pad_add_fusion.me_ref, bf16[1024,1664]{1,0:T(8,128)(2,1)} %get-tuple-element.123.refs_0_.right_ref, bf16[1024,1664]{1,0:T(8,128)(2,1)} %all-gather.8.cloned.1.call-done.refs_1_.refs_3_, ...), custom_call_target="tpu_custom_call" | custom-call | flops 1048576 | bytes 262144 | tf_op jit(solution)/shard_map/piece/pallas_call | solution.py:405
  582.4 13.9 %collective-permute-done.33 = bf16[1024,512]{1,0:T(8,128)(2,1)} collective-permute-done((bf16[1024,512]{1,0:T(8,128)(2,1)}, bf16[1024,512]{1,0:T(8,128)(2,1)}, u32[]{:S(2)}, u32[]{:S(2)}) %collective-permute-start.33) | collective-permute-done | bytes 1048608 | tf_op jit(solution)/shard_map/ppermute | solution.py:271
  605.7 10.2 %collective-permute-done.36 = f32[145,128]{1,0:T(8,128)S(1)} collective-permute-done((f32[145,128]{1,0:T(8,128)S(1)}, f32[145,128]{1,0:T(8,128)S(1)}, u32[]{:S(2)}, u32[]{:S(2)}) %collective-permute-start.36) | collective-permute-done | bytes 74272 | tf_op jit(solution)/shard_map/ppermute | solution.py:271
  616.0 8.5 %collective-permute-done.37 = f32[145,128]{1,0:T(8,128)S(1)} collective-permute-done((f32[145,128]{1,0:T(8,128)S(1)}, f32[145,128]{1,0:T(8,128)S(1)}, u32[]{:S(2)}, u32[]{:S(2)}) %collective-permute-start.37) | collective-permute-done | bytes 74272 | tf_op jit(solution)/shard_map/ppermute | solution.py:271
  624.6 17.7 %collective-permute-done.25.refs_0_ = bf16[1024,1536]{1,0:T(8,128)(2,1)} collective-permute-done((bf16[1024,1536]{1,0:T(8,128)(2,1)}, bf16[1024,1536]{1,0:T(8,128)(2,1)}, u32[]{:S(2)}, u32[]{:S(2)}) %collective-permute-start.25) | collective-permute-done | bytes 3145760 | tf_op jit(solution)/shard_map/ppermute | solution.py:271
  642.3 7.0 rows.15
  652.8 6.8 piece.14
  673.1 6.5 piece.15
  692.7 11.8 %collective-permute-done.40 = bf16[1024,512]{1,0:T(8,128)(2,1)} collective-permute-done((bf16[1024,512]{1,0:T(8,128)(2,1)}, bf16[1024,512]{1,0:T(8,128)(2,1)}, u32[]{:S(2)}, u32[]{:S(2)}) %collective-permute-start.40) | collective-permute-done | bytes 1048608 | tf_op jit(solution)/shard_map/ppermute | solution.py:271
  708.3 10.9 %reduce-scatter.12.cloned.1.call-done = bf16[256,1536]{1,0:T(8,128)(2,1)} async-done(((bf16[1024,1536]{1,0:T(8,128)(2,1)}), bf16[256,1536]{1,0:T(8,128)(2,1)}) %reduce-scatter.12.cloned.1.call-update) | async-done | bytes 786448 | tf_op jit(solution)/shard_map/reduce_scatter | solution.py:577
  (332 shorter events, 213.2 us)
Async XLA Ops:
  7.2 73.8 %all-gather.8.cloned.1.call-start = ((), (), s32[]{:S(2)}) async-start(), calls=%async_computation.6 | async-start | bytes 4259840 | tf_op jit(solution)/shard_map/all_gather | solution.py:573
  10.3 99.4 %all-gather.6.cloned.1.call-start = ((), (), s32[]{:S(2)}) async-start(), calls=%async_computation.5 | async-start | bytes 1310720 | tf_op jit(solution)/shard_map/all_gather | solution.py:573
  11.2 159.3 %all-gather.10.cloned.1.call-start = ((), (), s32[]{:S(2)}) async-start(), calls=%async_computation.7 | async-start | bytes 3604480 | tf_op jit(solution)/shard_map/all_gather | solution.py:573
  11.9 217.3 %all-gather.12.cloned.1.call-start = ((), (), s32[]{:S(2)}) async-start(), calls=%async_computation.8 | async-start | bytes 3604480 | tf_op jit(solution)/shard_map/all_gather | solution.py:573
  12.5 324.2 %all-gather.14.cloned.1.call-start = ((), (), s32[]{:S(2)}) async-start(), calls=%async_computation.9 | async-start | bytes 7208960 | tf_op jit(solution)/shard_map/all_gather | solution.py:573
  12.9 19.2 %collective-permute-start.3 = (bf16[256,1408]{1,0:T(8,128)(2,1)S(1)}, bf16[256,1408]{1,0:T(8,128)(2,1)}, u32[]{:S(2)}, u32[]{:S(2)}) collective-permute-start(bf16[256,1408]{1,0:T(8,128)(2,1)S(1)} %bitcast.106), channel_id=1, source_target_pairs={{0,4},{4,0},{8,12},{12,8},{16,20},{20,16},{24,28},{28,24},{1,5},{5... | collective-permute-start | bytes 2162696 | tf_op jit(solution)/shard_map/ppermute | solution.py:271
  21.1 26.3 %collective-permute-start.1 = (bf16[1024,512]{1,0:T(8,128)(2,1)S(1)}, bf16[1024,512]{1,0:T(8,128)(2,1)}, u32[]{:S(2)}, u32[]{:S(2)}) collective-permute-start(bf16[1024,512]{1,0:T(8,128)(2,1)S(1)} %pad_maximum_fusion.2.refs_0_), channel_id=1, source_target_pairs={{0,2},{1,3},{2,0},{3,1},{4,6},{5,7},{6,4},{7,5},{8,10},{9,11},{10,... | collective-permute-start | bytes 3145736 | tf_op jit(solution)/shard_map/ppermute | solution.py:271
  32.2 36.1 %collective-permute-start.5 = (bf16[1024,512]{1,0:T(8,128)(2,1)S(1)}, bf16[1024,512]{1,0:T(8,128)(2,1)S(1)}, u32[]{:S(2)}, u32[]{:S(2)}) collective-permute-start(bf16[1024,512]{1,0:T(8,128)(2,1)S(1)} %fusion.9.refs_0_), channel_id=1, source_target_pairs={{0,2},{1,3},{2,0},{3,1},{4,6},{5,7},{6,4},{7,5},{8,10},{9,11},{10,... | collective-permute-start | bytes 3145736 | tf_op jit(solution)/shard_map/ppermute | solution.py:271
  33.9 35.1 %collective-permute-start = (bf16[1024,512]{1,0:T(8,128)(2,1)S(1)}, bf16[1024,512]{1,0:T(8,128)(2,1)}, u32[]{:S(2)}, u32[]{:S(2)}) collective-permute-start(bf16[1024,512]{1,0:T(8,128)(2,1)S(1)} %pad_maximum_fusion.2.refs_0_), channel_id=1, source_target_pairs={{0,1},{1,0},{2,3},{3,2},{4,5},{5,4},{6,7},{7,6},{8,9},{9,8},{10,11... | collective-permute-start | bytes 3145736 | tf_op jit(solution)/shard_map/ppermute | solution.py:271
  47.4 21.7 %collective-permute-start.2 = (bf16[1024,512]{1,0:T(8,128)(2,1)}, bf16[1024,512]{1,0:T(8,128)(2,1)}, u32[]{:S(2)}, u32[]{:S(2)}) collective-permute-start(bf16[1024,512]{1,0:T(8,128)(2,1)} %collective-permute-done.1.refs_2_), channel_id=1, source_target_pairs={{0,1},{1,0},{2,3},{3,2},{4,5},{5,4},{6,7},{7,6},{8,9},{9,8},{10,11... | collective-permute-start | bytes 3145736 | tf_op jit(solution)/shard_map/ppermute | solution.py:271
  47.4 26.8 %collective-permute-start.4 = (bf16[1024,512]{1,0:T(8,128)(2,1)S(1)}, bf16[1024,512]{1,0:T(8,128)(2,1)}, u32[]{:S(2)}, u32[]{:S(2)}) collective-permute-start(bf16[1024,512]{1,0:T(8,128)(2,1)S(1)} %fusion.9.refs_0_), channel_id=1, source_target_pairs={{0,1},{1,0},{2,3},{3,2},{4,5},{5,4},{6,7},{7,6},{8,9},{9,8},{10,11... | collective-permute-start | bytes 3145736 | tf_op jit(solution)/shard_map/ppermute | solution.py:271
  80.9 76.9 %collective-permute-start.7 = (bf16[1024,1664]{1,0:T(8,128)(2,1)}, bf16[1024,1664]{1,0:T(8,128)(2,1)}, u32[]{:S(2)}, u32[]{:S(2)}) collective-permute-start(bf16[1024,1664]{1,0:T(8,128)(2,1)} %all-gather.8.cloned.1.call-done.refs_1_.refs_3_), channel_id=1, source_target_pairs={{0,4},{4,0},{8,12},{12,8},{16,20},{20,16},{24,28},{28,24},{1,5},{5... | collective-permute-start | bytes 10223624 | tf_op jit(solution)/shard_map/ppermute | solution.py:271
  85.0 478.7 %reduce-scatter.8.cloned.1.call-start = ((), (), s32[]{:S(2)}) async-start(), calls=%async_computation.11 | async-start | bytes 6488064 | tf_op jit(solution)/shard_map/reduce_scatter | solution.py:594
  109.7 97.2 %collective-permute-start.8 = (bf16[1024,512]{1,0:T(8,128)(2,1)}, bf16[1024,512]{1,0:T(8,128)(2,1)}, u32[]{:S(2)}, u32[]{:S(2)}) collective-permute-start(bf16[1024,512]{1,0:T(8,128)(2,1)} %all-gather.6.cloned.1.call-done.refs_1_.refs_3_), channel_id=1, source_target_pairs={{0,4},{4,0},{8,12},{12,8},{16,20},{20,16},{24,28},{28,24},{1,5},{5... | collective-permute-start | bytes 3145736 | tf_op jit(solution)/shard_map/ppermute | solution.py:271
  170.5 78.0 %collective-permute-start.12 = (bf16[1024,1408]{1,0:T(8,128)(2,1)}, bf16[1024,1408]{1,0:T(8,128)(2,1)}, u32[]{:S(2)}, u32[]{:S(2)}) collective-permute-start(bf16[1024,1408]{1,0:T(8,128)(2,1)} %all-gather.10.cloned.1.call-done.refs_1_.refs_3_), channel_id=1, source_target_pairs={{0,4},{4,0},{8,12},{12,8},{16,20},{20,16},{24,28},{28,24},{1,5},{5... | collective-permute-start | bytes 8650760 | tf_op jit(solution)/shard_map/ppermute | solution.py:271
  221.0 25.4 %collective-permute-start.11 = (bf16[1024,512]{1,0:T(8,128)(2,1)}, bf16[1024,512]{1,0:T(8,128)(2,1)S(1)}, u32[]{:S(2)}, u32[]{:S(2)}) collective-permute-start(bf16[1024,512]{1,0:T(8,128)(2,1)} %get-tuple-element.89), channel_id=1, source_target_pairs={{0,2},{1,3},{2,0},{3,1},{4,6},{5,7},{6,4},{7,5},{8,10},{9,11},{10,... | collective-permute-start | bytes 3145736 | tf_op jit(solution)/shard_map/ppermute | solution.py:271
  229.3 73.5 %collective-permute-start.16 = (bf16[1024,1408]{1,0:T(8,128)(2,1)}, bf16[1024,1408]{1,0:T(8,128)(2,1)}, u32[]{:S(2)}, u32[]{:S(2)}) collective-permute-start(bf16[1024,1408]{1,0:T(8,128)(2,1)} %all-gather.12.cloned.1.call-done.refs_2_.refs_6_.refs_8_), channel_id=1, source_target_pairs={{0,4},{4,0},{8,12},{12,8},{16,20},{20,16},{24,28},{28,24},{1,5},{5... | collective-permute-start | bytes 8650760 | tf_op jit(solution)/shard_map/ppermute | solution.py:271
  249.9 24.5 %collective-permute-start.14 = (bf16[1024,512]{1,0:T(8,128)(2,1)S(1)}, bf16[1024,512]{1,0:T(8,128)(2,1)S(1)}, u32[]{:S(2)}, u32[]{:S(2)}) collective-permute-start(bf16[1024,512]{1,0:T(8,128)(2,1)S(1)} %fusion.7.refs_0_), channel_id=1, source_target_pairs={{0,2},{1,3},{2,0},{3,1},{4,6},{5,7},{6,4},{7,5},{8,10},{9,11},{10,... | collective-permute-start | bytes 3145736 | tf_op jit(solution)/shard_map/ppermute | solution.py:271
  251.3 23.7 %collective-permute-start.13 = (bf16[1024,512]{1,0:T(8,128)(2,1)S(1)}, bf16[1024,512]{1,0:T(8,128)(2,1)S(1)}, u32[]{:S(2)}, u32[]{:S(2)}) collective-permute-start(bf16[1024,512]{1,0:T(8,128)(2,1)S(1)} %fusion.7.refs_0_), channel_id=1, source_target_pairs={{0,1},{1,0},{2,3},{3,2},{4,5},{5,4},{6,7},{7,6},{8,9},{9,8},{10,11... | collective-permute-start | bytes 3145736 | tf_op jit(solution)/shard_map/ppermute | solution.py:271
  326.9 251.3 %reduce-scatter.6.cloned.1.call-start = ((), (), s32[]{:S(2)}) async-start(), calls=%async_computation.10 | async-start | bytes 3604480 | tf_op jit(solution)/shard_map/reduce_scatter | solution.py:577
  373.7 88.3 %collective-permute-start.27 = (bf16[1024,1408]{1,0:T(8,128)(2,1)}, bf16[1024,1408]{1,0:T(8,128)(2,1)}, u32[]{:S(2)}, u32[]{:S(2)}) collective-permute-start(bf16[1024,1408]{1,0:T(8,128)(2,1)} %rows.8), channel_id=1, source_target_pairs={{0,4},{4,0},{8,12},{12,8},{16,20},{20,16},{24,28},{28,24},{1,5},{5... | collective-permute-start | bytes 8650760 | tf_op jit(solution)/shard_map/ppermute | solution.py:271
  389.8 25.6 %collective-permute-start.21 = (bf16[1024,512]{1,0:T(8,128)(2,1)}, bf16[1024,512]{1,0:T(8,128)(2,1)}, u32[]{:S(2)}, u32[]{:S(2)}) collective-permute-start(bf16[1024,512]{1,0:T(8,128)(2,1)} %get-tuple-element.107), channel_id=1, source_target_pairs={{0,2},{1,3},{2,0},{3,1},{4,6},{5,7},{6,4},{7,5},{8,10},{9,11},{10,... | collective-permute-start | bytes 3145736 | tf_op jit(solution)/shard_map/ppermute | solution.py:271
  418.9 43.1 %collective-permute-start.23 = (bf16[1024,512]{1,0:T(8,128)(2,1)S(1)}, bf16[1024,512]{1,0:T(8,128)(2,1)}, u32[]{:S(2)}, u32[]{:S(2)}) collective-permute-start(bf16[1024,512]{1,0:T(8,128)(2,1)S(1)} %get-tuple-element.175.refs_0_), channel_id=1, source_target_pairs={{0,2},{1,3},{2,0},{3,1},{4,6},{5,7},{6,4},{7,5},{8,10},{9,11},{10,... | collective-permute-start | bytes 3145736 | tf_op jit(solution)/shard_map/ppermute | solution.py:271
  469.6 172.7 %reduce-scatter.10.cloned.1.call-start = ((), (), s32[]{:S(2)}) async-start(), calls=%async_computation.12 | async-start | bytes 3604480 | tf_op jit(solution)/shard_map/reduce_scatter | solution.py:577
  469.6 91.0 %collective-permute-start.28 = (bf16[1024,1408]{1,0:T(8,128)(2,1)}, bf16[1024,1408]{1,0:T(8,128)(2,1)}, u32[]{:S(2)}, u32[]{:S(2)}) collective-permute-start(bf16[1024,1408]{1,0:T(8,128)(2,1)} %copy-done.21), channel_id=1, source_target_pairs={{0,4},{4,0},{8,12},{12,8},{16,20},{20,16},{24,28},{28,24},{1,5},{5... | collective-permute-start | bytes 8650760 | tf_op jit(solution)/shard_map/ppermute | solution.py:271
  537.6 13.9 %collective-permute-start.31 = (bf16[1024,512]{1,0:T(8,128)(2,1)}, bf16[1024,512]{1,0:T(8,128)(2,1)}, u32[]{:S(2)}, u32[]{:S(2)}) collective-permute-start(bf16[1024,512]{1,0:T(8,128)(2,1)} %get-tuple-element.118), channel_id=1, source_target_pairs={{0,1},{1,0},{2,3},{3,2},{4,5},{5,4},{6,7},{7,6},{8,9},{9,8},{10,11... | collective-permute-start | bytes 3145736 | tf_op jit(solution)/shard_map/ppermute | solution.py:271
  538.1 25.5 %collective-permute-start.26 = (bf16[1024,512]{1,0:T(8,128)(2,1)}, bf16[1024,512]{1,0:T(8,128)(2,1)}, u32[]{:S(2)}, u32[]{:S(2)}) collective-permute-start(bf16[1024,512]{1,0:T(8,128)(2,1)} %rows.10), channel_id=1, source_target_pairs={{0,4},{4,0},{8,12},{12,8},{16,20},{20,16},{24,28},{28,24},{1,5},{5... | collective-permute-start | bytes 3145736 | tf_op jit(solution)/shard_map/ppermute | solution.py:271
  571.2 115.0 %reduce-scatter.14.cloned.1.call-start = ((), (), s32[]{:S(2)}) async-start(), calls=%async_computation.14 | async-start | bytes 1310720 | tf_op jit(solution)/shard_map/reduce_scatter | solution.py:577
  571.5 24.8 %collective-permute-start.33 = (bf16[1024,512]{1,0:T(8,128)(2,1)}, bf16[1024,512]{1,0:T(8,128)(2,1)}, u32[]{:S(2)}, u32[]{:S(2)}) collective-permute-start(bf16[1024,512]{1,0:T(8,128)(2,1)} %get-tuple-element.127), channel_id=1, source_target_pairs={{0,2},{1,3},{2,0},{3,1},{4,6},{5,7},{6,4},{7,5},{8,10},{9,11},{10,... | collective-permute-start | bytes 3145736 | tf_op jit(solution)/shard_map/ppermute | solution.py:271
  573.0 69.3 %collective-permute-start.25 = (bf16[1024,1536]{1,0:T(8,128)(2,1)}, bf16[1024,1536]{1,0:T(8,128)(2,1)}, u32[]{:S(2)}, u32[]{:S(2)}) collective-permute-start(bf16[1024,1536]{1,0:T(8,128)(2,1)} %copy-done.19), channel_id=1, source_target_pairs={{0,4},{4,0},{8,12},{12,8},{16,20},{20,16},{24,28},{28,24},{1,5},{5... | collective-permute-start | bytes 9437192 | tf_op jit(solution)/shard_map/ppermute | solution.py:271
  582.4 136.8 %reduce-scatter.12.cloned.1.call-start = ((), (), s32[]{:S(2)}) async-start(), calls=%async_computation.13 | async-start | bytes 3932160 | tf_op jit(solution)/shard_map/reduce_scatter | solution.py:577
  679.6 24.9 %collective-permute-start.40 = (bf16[1024,512]{1,0:T(8,128)(2,1)}, bf16[1024,512]{1,0:T(8,128)(2,1)}, u32[]{:S(2)}, u32[]{:S(2)}) collective-permute-start(bf16[1024,512]{1,0:T(8,128)(2,1)} %get-tuple-element.137), channel_id=1, source_target_pairs={{0,2},{1,3},{2,0},{3,1},{4,6},{5,7},{6,4},{7,5},{8,10},{9,11},{10,... | collective-permute-start | bytes 3145736 | tf_op jit(solution)/shard_map/ppermute | solution.py:271
  (82 other events, 1062.7 us)
Sparse Core Ops, SparseCore 0:
  10.4 70.5 all-gather.7
  83.1 26.5 all-gather.5
  111.2 58.6 all-gather.9
  171.4 57.8 all-gather.11
  231.3 105.3 all-gather.13
  340.2 129.3 reduce-scatter.7
  471.8 54.7 reduce-scatter.5
  571.4 57.2 reduce-scatter.9
  630.9 26.9 reduce-scatter.13
  660.2 58.8 reduce-scatter.11

commit v7 on v6

--- a/solution.py
+++ b/solution.py
@@ -300,9 +300,9 @@
         self.kept, self.got = list(range(lax.axis_size("col"))), {}
 
     def pieces(self, js, dtypes, earlier):
-        (left, pair), rest = self.terms[0], self.terms[1:]
+        (left, *pair), rest = self.terms[0], self.terms[1:]
         gots = [self.got.pop(j, None) for j in js]
-        return piece_call([(after(left, *earlier), pair)] + rest, self.block, js, gots, dtypes)
+        return piece_call([(after(left, *earlier), *pair)] + rest, self.block, js, gots, dtypes)
 
     def send(self, bit, *earlier):
         js = [j for j in self.kept if j & bit]
@@ -456,6 +456,35 @@
     return dot(refs[0][...], flat(refs[2])) + dot(refs[1][...], flat(refs[3]))
 
 
+def proj_kernel(*refs):
+    cut = refs[2].shape[1]
+    for start, first in ((0, 2), (cut, 4)):
+        total = dot(refs[0][...], refs[first][...]) + dot(refs[1][...], refs[first + 1][...])
+        refs[6][:, start : start + total.shape[1]] = total
+
+
+def proj_call(left, pair, narrow):
+    rows, half, width = left.shape[0], left.shape[1] // 2, pair[0].shape[1] + narrow[0].shape[1]
+    arrays = [left, left, *pair, *narrow]
+    specs = [half_tile(half, 0), half_tile(half, 1)] + [whole(a.shape) for a in arrays[2:]]
+    return tile_call(proj_kernel, arrays, specs, jax.ShapeDtypeStruct((rows, width), f32), row_tile(width),
+                     (rows // TILE,), "proj")
+
+
+def gather_narrow(shard):
+    n, row = lax.axis_size("row"), lax.axis_index("row")
+    rows, width = shard.shape
+    stack = shard.T[None]
+    for bit in reversed(bits_down(n)):
+        stack = jnp.concatenate([stack, swap(stack, "row", bit)], 0)
+    for bit in bits_down(n):
+        parts = stack.reshape(n // (2 * bit), 2, bit, width, rows)
+        parts = jnp.where((row & bit) != 0, parts[:, ::-1], parts)
+        stack = parts.reshape(n, width, rows)
+    parts = stack.reshape(n // 2, 2, width, rows).transpose(1, 0, 3, 2).reshape(2, -1, width)
+    return flip(*jnp.pad(parts, ((0, 0), (0, 0), (0, 128 - width))))
+
+
 def hidden_kernel(*refs):
     gate_ref, up_ref, hidden_ref = refs[4:]
     up = both(refs)
@@ -518,9 +547,9 @@
     rows = terms[0][0].shape[0]
     me = jnp.stack([lax.axis_index("col") ^ j for j in js]).astype(jnp.int32)
     arrays, specs = [], []
-    for left, pair in terms:
+    for left, pair, *place in terms:
         arrays.append(left)
-        specs.append(row_tile(left.shape[1]))
+        specs.append(half_tile(pair[0].shape[-1], place[0] if place else 0))
         for n in range(len(js)):
             arrays += pair
             specs += [block_spec(w, p, n, block) for p, w in enumerate(pair)]
@@ -644,8 +673,7 @@
     feat = lax.axis_size("col") * width
     live = live_column(lengths[0], rows)
     live_low = live.astype(bf16)
-    beta_pad = jnp.pad(beta_weight, ((0, 0), (0, 128 - beta_weight.shape[1])))
-    in_mine = gather_parity(jnp.concatenate([q_weight, k_weight, v_weight, beta_pad], 1))
+    in_mine = gather_parity(jnp.concatenate([q_weight, k_weight, v_weight], 1))
     out_mine = gather_parity(out_weight.T)
     gate_mine = gather_parity(gate_weight)
     up_mine = gather_parity(up_weight)
@@ -668,9 +696,10 @@
     half = feat // 2
     normed, factor_in = join_norm(spread_cols(tokens), norm_in)
     ffn_cot = join(spread_cols(after(cotangent * live_low, down_side)))
-    in_mine = after(in_mine, normed, ffn_cot)
+    w_beta = gather_narrow(beta_weight)
+    in_mine = after(in_mine, normed, ffn_cot, *w_beta)
     in_other, out_other = swap(in_mine, "row", 1), swap(out_mine, "row", 1)
-    proj = halves(after(normed, out_mine), [(0, in_mine), (1, in_other)])
+    proj = proj_call(after(normed, out_mine), (in_mine, in_other), w_beta)
     gate_mine = after(gate_mine, proj)
     gate_other = swap(gate_mine, "row", 1)
     proj = after(proj, gate_mine)
@@ -713,7 +742,7 @@
     out_sent, out_got = trade_rows(after(branch_cot, mixed_cot), mixed)
     mixed_cot = after(mixed_cot, *out_sent)
     low, gconv, ghead, inner_in = mixer_backward(proj, conv, gain, mixed_cot, kept, heads, dh)
-    in_sum = ColSum([(low, w_in)], block)
+    in_sum = ColSum([(low, w_in), (low, w_beta, 3 * hd // 128)], block)
     sent = in_sum.send(1)
     low_sent, low_got = trade_rows(after(normed, *sent), low, width=3 * hd)
     beta_part = by_place(dot(low[:, 3 * hd :], after(normed, *low_sent), 0, 0)[: beta_weight.shape[1]], chunk)

time: 734 us -> 727 us (level)
  waiting for transfers between devices: 333 us -> 313 us
    all_gather x5, waiting for transfers between devices: 43.9 us -> 25 us  [gather_parity(): lax.all_gather(shard, 'row', axis=0, tiled=True, axis_index_groups=parity...]
    ppermute x42 -> x45, starting transfers between devices: 31.9 us -> 37.7 us  [swap(): return lax.ppermute(x, axis, [(i, i ^ bit) for i in range(n)])]
    ppermute x42 -> x45, waiting for transfers between devices: 277 us -> 277 us  [swap(): return lax.ppermute(x, axis, [(i, i ^ bit) for i in range(n)])]
    unnamed x141 -> x148, local copies, waits for them, and re-layouts: 42.1 us -> 42 us
  transfers between devices with their start and end apart: 52 -> 55, of which waited for: 29 -> 30; matrix products, arithmetic and copies ran while one was open for 8% -> 9% of each run, Pallas kernels for 35% -> 36%
where the time goes in v7:
time: 727 us; the launch traced here: 722 us
  waiting for transfers between devices  313 us (43%)
  Pallas kernels  257 us (35%)
  local copies, waits for them, and re-layouts  54.8 us (8%)
  starting transfers between devices  38.5 us (5%)
  other arithmetic  37.7 us (5%)
  between operations  16 us (2%)
    ppermute x45, waiting for transfers between devices, swap(): return lax.ppermute(x, axis, [(i, i ^ bit) for i in range(n)])  277 us
    pallas_call x13, Pallas kernels, tile_call(): pl.pallas_call(kernel, grid=grid, in_specs=specs, out_specs=out_specs, ou...  96.6 us
    pallas_call x9, Pallas kernels, tile_call(): pl.pallas_call(kernel, grid_spec=grid_spec, out_shape=outs, **params)  70.6 us
    unnamed x148, local copies, waits for them, and re-layouts  42 us
    ppermute x45, starting transfers between devices, swap(): return lax.ppermute(x, axis, [(i, i ^ bit) for i in range(n)])  37.7 us
    pallas_call x1, Pallas kernels, mixer_backward(): pl.pallas_call(functools.partial(bwd_kernel, heads, dh), grid=(steps,), i...  37.7 us
    pallas_call x1, Pallas kernels, mixer_forward(): pl.pallas_call(functools.partial(fwd_kernel, heads, dh), grid=(steps,), i...  34.3 us
    all_gather x5, waiting for transfers between devices, gather_parity(): lax.all_gather(shard, 'row', axis=0, tiled=True, axis_index_groups=parity...  25 us
  transfers between devices with their start and end apart: 55, of which 30 were waited for; matrix products, arithmetic and copies ran while one was open for 9% of the time, Pallas kernels for 36%

profile of v7, /device:TPU:0, one launch (start us, length us, event | category | flops | bytes accessed | tf_op | source)
XLA Modules:
  0.0 722.1 jit_solution(6640660211721856222)
XLA Ops:
  49.6 21.0 %collective-permute-done.5.refs_2_ = bf16[1024,512]{1,0:T(8,128)(2,1)} collective-permute-done((bf16[1024,512]{1,0:T(8,128)(2,1)S(1)}, bf16[1024,512]{1,0:T(8,128)(2,1)}, u32[]{:S(2)}, u32[]{:S(2)}) %collective-permute-start.5) | collective-permute-done | bytes 1048608 | tf_op jit(solution)/shard_map/ppermute | solution.py:271
  87.3 18.1 %all-gather.6.cloned.1.call-done.refs_1_.refs_3_ = bf16[1024,512]{1,0:T(8,128)(2,1)} async-done(((bf16[256,512]{1,0:T(8,128)(2,1)}), bf16[1024,512]{1,0:T(8,128)(2,1)}) %all-gather.6.cloned.1.call-update) | async-done | bytes 1048592 | tf_op jit(solution)/shard_map/all_gather | solution.py:602
  106.9 51.3 %collective-permute-done.10.refs_3_.refs_2_.refs_4_ = bf16[1024,1536]{1,0:T(8,128)(2,1)} collective-permute-done((bf16[1024,1536]{1,0:T(8,128)(2,1)}, bf16[1024,1536]{1,0:T(8,128)(2,1)}, u32[]{:S(2)}, u32[]{:S(2)}) %collective-permute-start.10) | collective-permute-done | bytes 3145760 | tf_op jit(solution)/shard_map/ppermute | solution.py:271
  160.1 12.6 %proj.1.x_ref.prev_ref = f32[1024,1664]{1,0:T(8,128)} custom-call(bf16[1024,2048]{1,0:T(8,128)(2,1)} %get-tuple-element.130.refs_0_.refs_1_.left_ref, bf16[1024,2048]{1,0:T(8,128)(2,1)} %get-tuple-element.130.refs_0_.refs_1_.left_ref, bf16[1024,1536]{1,0:T(8,128)(2,1)S(1)} %copy-done, bf16[1024,1536]{1,0:T(8,128)(2,1)} %collective-permute-done.10.refs_3_.refs_2_.refs_4_, ...), custom_call_target="tpu_custom_call" | custom-call | flops 1048576 | bytes 262144 | tf_op jit(solution)/shard_map/proj/pallas_call | solution.py:401
  173.7 34.3 %mixer_forward.1 = (bf16[1024,512]{1,0:T(8,128)(2,1)}, f32[1024,512]{1,0:T(8,128)}, f32[1024,512]{1,0:T(8,128)}, f32[8,4,128,128]{3,2,1,0:T(8,128)}, f32[8,4,128,128]{3,2,1,0:T(8,128)}) custom-call(f32[1024,1664]{1,0:T(8,128)} %proj.1.x_ref.prev_ref, f32[4,1536]{1,0:T(4,128)} %copy-done.57, f32[1,128]{1,0:T(1,128)} %bitcast.149), custom_call_target="tpu_custom_call" | custom-call | flops 1048576 | bytes 262144 | tf_op jit(solution)/shard_map/mixer_forward/pallas_call | solution.py:202
  226.5 19.8 %collective-permute-done.14 = bf16[1024,512]{1,0:T(8,128)(2,1)S(1)} collective-permute-done((bf16[1024,512]{1,0:T(8,128)(2,1)}, bf16[1024,512]{1,0:T(8,128)(2,1)S(1)}, u32[]{:S(2)}, u32[]{:S(2)}) %collective-permute-start.14) | collective-permute-done | bytes 1048608 | tf_op jit(solution)/shard_map/ppermute | solution.py:271
  251.4 22.8 %collective-permute-done.17.refs_2_ = bf16[1024,512]{1,0:T(8,128)(2,1)S(1)} collective-permute-done((bf16[1024,512]{1,0:T(8,128)(2,1)S(1)}, bf16[1024,512]{1,0:T(8,128)(2,1)S(1)}, u32[]{:S(2)}, u32[]{:S(2)}) %collective-permute-start.17) | collective-permute-done | bytes 1048608 | tf_op jit(solution)/shard_map/ppermute | solution.py:271
  282.0 9.7 %halves.2.refs_4_ = bf16[1024,1408]{1,0:T(8,128)(2,1)S(1)} custom-call(bf16[1024,2048]{1,0:T(8,128)(2,1)} %get-tuple-element.108.refs_0_.refs_2_.refs_1_.left_ref, bf16[1024,1408]{1,0:T(8,128)(2,1)S(1)} %copy-done.2, bf16[1024,2048]{1,0:T(8,128)(2,1)} %get-tuple-element.108.refs_0_.refs_2_.refs_1_.left_ref, ...), custom_call_target="tpu_custom_call" | custom-call | flops 1048576 | bytes 262144 | tf_op jit(solution)/shard_map/halves/pallas_call | solution.py:401
  293.4 10.5 %collective-permute-done.19.refs_3_.refs_7_.refs_9_ = bf16[1024,1408]{1,0:T(8,128)(2,1)} collective-permute-done((bf16[1024,1408]{1,0:T(8,128)(2,1)}, bf16[1024,1408]{1,0:T(8,128)(2,1)}, u32[]{:S(2)}, u32[]{:S(2)}) %collective-permute-start.19) | collective-permute-done | bytes 2883616 | tf_op jit(solution)/shard_map/ppermute | solution.py:271
  303.9 11.2 %hidden.1 = (bf16[1024,1408]{1,0:T(8,128)(2,1)S(1)}, bf16[1024,1408]{1,0:T(8,128)(2,1)S(1)}) custom-call(bf16[1024,2048]{1,0:T(8,128)(2,1)} %get-tuple-element.108.refs_0_.refs_2_.refs_1_.left_ref, bf16[1024,2048]{1,0:T(8,128)(2,1)} %get-tuple-element.108.refs_0_.refs_2_.refs_1_.left_ref, ...), custom_call_target="tpu_custom_call" | custom-call | flops 1048576 | bytes 262144 | tf_op jit(solution)/shard_map/hidden/pallas_call | solution.py:401
  316.7 9.7 %all_rows.1 = bf16[2048,1408]{1,0:T(8,128)(2,1)} custom-call(s32[1]{0:T(128)} %bitcast.33.odd_ref, bf16[1024,2048]{1,0:T(8,128)(2,1)} %join.2.left_ref.refs_0_.refs_1_, bf16[1024,1408]{1,0:T(8,128)(2,1)S(1)} %get-tuple-element.135.right_ref.refs_0_), custom_call_target="tpu_custom_call" | custom-call | flops 1048576 | bytes 262144 | tf_op jit(solution)/shard_map/all_rows/pallas_call | solution.py:405
  332.4 14.2 %cots.1 = (bf16[1024,1408]{1,0:T(8,128)(2,1)S(1)}, bf16[1024,1408]{1,0:T(8,128)(2,1)}, f32[1024,1]{1,0:T(8,128)S(1)}) custom-call(bf16[1024,2048]{1,0:T(8,128)(2,1)} %join.2.left_ref.refs_0_.refs_1_, bf16[1024,2048]{1,0:T(8,128)(2,1)} %join.2.left_ref.refs_0_.refs_1_, bf16[4,2,256,1408]{3,2,1,0:T(8,128)(2,1)} %bitcast.107, ...), custom_call_target="tpu_custom_call" | custom-call | flops 1048576 | bytes 262144 | tf_op jit(solution)/shard_map/cots/pallas_call | solution.py:401
  347.5 11.9 %piece.10 = (bf16[1024,512]{1,0:T(8,128)(2,1)}, bf16[1024,512]{1,0:T(8,128)(2,1)}) custom-call(s32[2]{0:T(128)S(1)} %pad_add_fusion.1.me_ref, bf16[1024,1408]{1,0:T(8,128)(2,1)S(1)} %get-tuple-element.105.refs_0_.right_ref, bf16[1024,1408]{1,0:T(8,128)(2,1)} %all-gather.10.cloned.1.call-done.refs_1_.refs_3_, ...), custom_call_target="tpu_custom_call" | custom-call | flops 1048576 | bytes 262144 | tf_op jit(solution)/shard_map/piece/pallas_call | solution.py:405
  364.8 6.1 rows.8
  374.0 12.7 %piece.11 = (bf16[1024,512]{1,0:T(8,128)(2,1)}, f32[1024,512]{1,0:T(8,128)S(1)}) custom-call(s32[2]{0:T(128)S(1)} %pad_add_fusion.me_ref, bf16[1024,1408]{1,0:T(8,128)(2,1)} %copy-done.5, bf16[1024,1408]{1,0:T(8,128)(2,1)} %all-gather.10.cloned.1.call-done.refs_1_.refs_3_, bf16[1024,1408]{1,0:T(8,128)(2,1)} %collective-permute-done.15.refs_3_.refs_2_.refs_4_, ...), custom_call_target="tpu_custom_call" | custom-call | flops 1048576 | bytes 262144 | tf_op jit(solution)/shard_map/piece/pallas_call | solution.py:405
  396.5 17.2 %collective-permute-done.24 = bf16[1024,512]{1,0:T(8,128)(2,1)} collective-permute-done((bf16[1024,512]{1,0:T(8,128)(2,1)}, bf16[1024,512]{1,0:T(8,128)(2,1)}, u32[]{:S(2)}, u32[]{:S(2)}) %collective-permute-start.24) | collective-permute-done | bytes 1048608 | tf_op jit(solution)/shard_map/ppermute | solution.py:271
  418.6 40.6 %collective-permute-done.30.refs_0_ = bf16[1024,1408]{1,0:T(8,128)(2,1)} collective-permute-done((bf16[1024,1408]{1,0:T(8,128)(2,1)}, bf16[1024,1408]{1,0:T(8,128)(2,1)}, u32[]{:S(2)}, u32[]{:S(2)}) %collective-permute-start.30) | collective-permute-done | bytes 2883616 | tf_op jit(solution)/shard_map/ppermute | solution.py:271
  459.2 7.1 rows.12
  486.0 37.7 %mixer_backward.1 = (bf16[1024,1664]{1,0:T(8,128)(2,1)}, f32[4,1536]{1,0:T(4,128)}, f32[1,128]{1,0:T(1,128)}, f32[1024,1]{1,0:T(8,128)}) custom-call(f32[1024,1664]{1,0:T(8,128)} %proj.1.x_ref.prev_ref, f32[1024,1664]{1,0:T(8,128)} %proj.1.x_ref.prev_ref, f32[4,1536]{1,0:T(4,128)} %copy-done.57, f32[1,128]{1,0:T(1,128)} %bitcast.150, ...), custom_call_target="tpu_custom_call" | custom-call | flops 1048576 | bytes 262144 | tf_op jit(solution)/shard_map/mixer_backward/pallas_call | solution.py:234
  523.7 7.5 %piece.12 = (bf16[1024,512]{1,0:T(8,128)(2,1)}, bf16[1024,512]{1,0:T(8,128)(2,1)}) custom-call(s32[2]{0:T(128)S(1)} %pad_add_fusion.1.me_ref, bf16[1024,1664]{1,0:T(8,128)(2,1)} %get-tuple-element.123.refs_0_.refs_5_.right_ref, bf16[1024,1536]{1,0:T(8,128)(2,1)S(1)} %copy-done.1, bf16[1024,1536]{1,0:T(8,128)(2,1)} %collective-permute-done.10.refs_3_.refs_2_.refs_4_, ...), custom_call_target="tpu_custom_call" | custom-call | flops 1048576 | bytes 262144 | tf_op jit(solution)/shard_map/piece/pallas_call | solution.py:405
  537.4 6.0 rows.11
  545.6 8.4 %piece.13 = (bf16[1024,512]{1,0:T(8,128)(2,1)}, f32[1024,512]{1,0:T(8,128)S(1)}) custom-call(s32[2]{0:T(128)S(1)} %pad_add_fusion.me_ref, bf16[1024,1664]{1,0:T(8,128)(2,1)} %get-tuple-element.123.refs_0_.refs_5_.right_ref, bf16[1024,1536]{1,0:T(8,128)(2,1)} %all-gather.8.cloned.1.call-done.refs_2_.refs_1_.refs_3_, ...), custom_call_target="tpu_custom_call" | custom-call | flops 1048576 | bytes 262144 | tf_op jit(solution)/shard_map/piece/pallas_call | solution.py:405
  557.3 5.9 rows.13
  576.5 13.4 %collective-permute-done.36 = bf16[1024,512]{1,0:T(8,128)(2,1)} collective-permute-done((bf16[1024,512]{1,0:T(8,128)(2,1)}, bf16[1024,512]{1,0:T(8,128)(2,1)}, u32[]{:S(2)}, u32[]{:S(2)}) %collective-permute-start.36) | collective-permute-done | bytes 1048608 | tf_op jit(solution)/shard_map/ppermute | solution.py:271
  600.2 9.1 %collective-permute-done.39 = f32[145,128]{1,0:T(8,128)S(1)} collective-permute-done((f32[145,128]{1,0:T(8,128)S(1)}, f32[145,128]{1,0:T(8,128)S(1)}, u32[]{:S(2)}, u32[]{:S(2)}) %collective-permute-start.39) | collective-permute-done | bytes 74272 | tf_op jit(solution)/shard_map/ppermute | solution.py:271
  609.4 8.5 %collective-permute-done.40 = f32[145,128]{1,0:T(8,128)S(1)} collective-permute-done((f32[145,128]{1,0:T(8,128)S(1)}, f32[145,128]{1,0:T(8,128)S(1)}, u32[]{:S(2)}, u32[]{:S(2)}) %collective-permute-start.40) | collective-permute-done | bytes 74272 | tf_op jit(solution)/shard_map/ppermute | solution.py:271
  617.9 18.1 %collective-permute-done.28.refs_0_ = bf16[1024,1536]{1,0:T(8,128)(2,1)} collective-permute-done((bf16[1024,1536]{1,0:T(8,128)(2,1)}, bf16[1024,1536]{1,0:T(8,128)(2,1)}, u32[]{:S(2)}, u32[]{:S(2)}) %collective-permute-start.28) | collective-permute-done | bytes 3145760 | tf_op jit(solution)/shard_map/ppermute | solution.py:271
  636.0 7.0 rows.15
  646.5 6.8 piece.14
  667.4 6.5 piece.15
  686.8 12.3 %collective-permute-done.43 = bf16[1024,512]{1,0:T(8,128)(2,1)} collective-permute-done((bf16[1024,512]{1,0:T(8,128)(2,1)}, bf16[1024,512]{1,0:T(8,128)(2,1)}, u32[]{:S(2)}, u32[]{:S(2)}) %collective-permute-start.43) | collective-permute-done | bytes 1048608 | tf_op jit(solution)/shard_map/ppermute | solution.py:271
  703.0 9.7 %reduce-scatter.12.cloned.1.call-done = bf16[256,1536]{1,0:T(8,128)(2,1)} async-done(((bf16[1024,1536]{1,0:T(8,128)(2,1)}), bf16[256,1536]{1,0:T(8,128)(2,1)}) %reduce-scatter.12.cloned.1.call-update) | async-done | bytes 786448 | tf_op jit(solution)/shard_map/reduce_scatter | solution.py:606
  (353 shorter events, 218.5 us)
Async XLA Ops:
  7.2 79.8 %all-gather.8.cloned.1.call-start = ((), (), s32[]{:S(2)}) async-start(), calls=%async_computation.6 | async-start | bytes 3932160 | tf_op jit(solution)/shard_map/all_gather | solution.py:602
  9.4 96.0 %all-gather.6.cloned.1.call-start = ((), (), s32[]{:S(2)}) async-start(), calls=%async_computation.5 | async-start | bytes 1310720 | tf_op jit(solution)/shard_map/all_gather | solution.py:602
  10.3 162.4 %all-gather.10.cloned.1.call-start = ((), (), s32[]{:S(2)}) async-start(), calls=%async_computation.7 | async-start | bytes 3604480 | tf_op jit(solution)/shard_map/all_gather | solution.py:602
  11.1 214.0 %all-gather.12.cloned.1.call-start = ((), (), s32[]{:S(2)}) async-start(), calls=%async_computation.8 | async-start | bytes 3604480 | tf_op jit(solution)/shard_map/all_gather | solution.py:602
  11.6 320.8 %all-gather.14.cloned.1.call-start = ((), (), s32[]{:S(2)}) async-start(), calls=%async_computation.9 | async-start | bytes 7208960 | tf_op jit(solution)/shard_map/all_gather | solution.py:602
  12.0 19.2 %collective-permute-start.3 = (bf16[256,1408]{1,0:T(8,128)(2,1)S(1)}, bf16[256,1408]{1,0:T(8,128)(2,1)}, u32[]{:S(2)}, u32[]{:S(2)}) collective-permute-start(bf16[256,1408]{1,0:T(8,128)(2,1)S(1)} %bitcast.121), channel_id=1, source_target_pairs={{0,4},{4,0},{8,12},{12,8},{16,20},{20,16},{24,28},{28,24},{1,5},{5... | collective-permute-start | bytes 2162696 | tf_op jit(solution)/shard_map/ppermute | solution.py:271
  23.3 26.3 %collective-permute-start.1 = (bf16[1024,512]{1,0:T(8,128)(2,1)S(1)}, bf16[1024,512]{1,0:T(8,128)(2,1)}, u32[]{:S(2)}, u32[]{:S(2)}) collective-permute-start(bf16[1024,512]{1,0:T(8,128)(2,1)S(1)} %pad_maximum_fusion.2.refs_0_), channel_id=1, source_target_pairs={{0,2},{1,3},{2,0},{3,1},{4,6},{5,7},{6,4},{7,5},{8,10},{9,11},{10,... | collective-permute-start | bytes 3145736 | tf_op jit(solution)/shard_map/ppermute | solution.py:271
  31.3 39.3 %collective-permute-start.5 = (bf16[1024,512]{1,0:T(8,128)(2,1)S(1)}, bf16[1024,512]{1,0:T(8,128)(2,1)}, u32[]{:S(2)}, u32[]{:S(2)}) collective-permute-start(bf16[1024,512]{1,0:T(8,128)(2,1)S(1)} %fusion.7.refs_0_), channel_id=1, source_target_pairs={{0,2},{1,3},{2,0},{3,1},{4,6},{5,7},{6,4},{7,5},{8,10},{9,11},{10,... | collective-permute-start | bytes 3145736 | tf_op jit(solution)/shard_map/ppermute | solution.py:271
  34.5 43.3 %collective-permute-start = (bf16[1024,512]{1,0:T(8,128)(2,1)S(1)}, bf16[1024,512]{1,0:T(8,128)(2,1)}, u32[]{:S(2)}, u32[]{:S(2)}) collective-permute-start(bf16[1024,512]{1,0:T(8,128)(2,1)S(1)} %pad_maximum_fusion.2.refs_0_), channel_id=1, source_target_pairs={{0,1},{1,0},{2,3},{3,2},{4,5},{5,4},{6,7},{7,6},{8,9},{9,8},{10,11... | collective-permute-start | bytes 3145736 | tf_op jit(solution)/shard_map/ppermute | solution.py:271
  45.4 37.7 %collective-permute-start.4 = (bf16[1024,512]{1,0:T(8,128)(2,1)S(1)}, bf16[1024,512]{1,0:T(8,128)(2,1)}, u32[]{:S(2)}, u32[]{:S(2)}) collective-permute-start(bf16[1024,512]{1,0:T(8,128)(2,1)S(1)} %fusion.7.refs_0_), channel_id=1, source_target_pairs={{0,1},{1,0},{2,3},{3,2},{4,5},{5,4},{6,7},{7,6},{8,9},{9,8},{10,11... | collective-permute-start | bytes 3145736 | tf_op jit(solution)/shard_map/ppermute | solution.py:271
  49.6 28.3 %collective-permute-start.2 = (bf16[1024,512]{1,0:T(8,128)(2,1)}, bf16[1024,512]{1,0:T(8,128)(2,1)}, u32[]{:S(2)}, u32[]{:S(2)}) collective-permute-start(bf16[1024,512]{1,0:T(8,128)(2,1)} %collective-permute-done.1.refs_2_), channel_id=1, source_target_pairs={{0,1},{1,0},{2,3},{3,2},{4,5},{5,4},{6,7},{7,6},{8,9},{9,8},{10,11... | collective-permute-start | bytes 3145736 | tf_op jit(solution)/shard_map/ppermute | solution.py:271
  76.1 481.1 %reduce-scatter.8.cloned.1.call-start = ((), (), s32[]{:S(2)}) async-start(), calls=%async_computation.11 | async-start | bytes 6488064 | tf_op jit(solution)/shard_map/reduce_scatter | solution.py:623
  87.0 71.2 %collective-permute-start.10 = (bf16[1024,1536]{1,0:T(8,128)(2,1)}, bf16[1024,1536]{1,0:T(8,128)(2,1)}, u32[]{:S(2)}, u32[]{:S(2)}) collective-permute-start(bf16[1024,1536]{1,0:T(8,128)(2,1)} %all-gather.8.cloned.1.call-done.refs_2_.refs_1_.refs_3_), channel_id=1, source_target_pairs={{0,4},{4,0},{8,12},{12,8},{16,20},{20,16},{24,28},{28,24},{1,5},{5... | collective-permute-start | bytes 9437192 | tf_op jit(solution)/shard_map/ppermute | solution.py:271
  105.4 102.5 %collective-permute-start.11 = (bf16[1024,512]{1,0:T(8,128)(2,1)}, bf16[1024,512]{1,0:T(8,128)(2,1)S(1)}, u32[]{:S(2)}, u32[]{:S(2)}) collective-permute-start(bf16[1024,512]{1,0:T(8,128)(2,1)} %all-gather.6.cloned.1.call-done.refs_1_.refs_3_), channel_id=1, source_target_pairs={{0,4},{4,0},{8,12},{12,8},{16,20},{20,16},{24,28},{28,24},{1,5},{5... | collective-permute-start | bytes 3145736 | tf_op jit(solution)/shard_map/ppermute | solution.py:271
  172.7 75.6 %collective-permute-start.15 = (bf16[1024,1408]{1,0:T(8,128)(2,1)}, bf16[1024,1408]{1,0:T(8,128)(2,1)}, u32[]{:S(2)}, u32[]{:S(2)}) collective-permute-start(bf16[1024,1408]{1,0:T(8,128)(2,1)} %all-gather.10.cloned.1.call-done.refs_1_.refs_3_), channel_id=1, source_target_pairs={{0,4},{4,0},{8,12},{12,8},{16,20},{20,16},{24,28},{28,24},{1,5},{5... | collective-permute-start | bytes 8650760 | tf_op jit(solution)/shard_map/ppermute | solution.py:271
  220.9 25.4 %collective-permute-start.14 = (bf16[1024,512]{1,0:T(8,128)(2,1)}, bf16[1024,512]{1,0:T(8,128)(2,1)S(1)}, u32[]{:S(2)}, u32[]{:S(2)}) collective-permute-start(bf16[1024,512]{1,0:T(8,128)(2,1)} %get-tuple-element.89), channel_id=1, source_target_pairs={{0,2},{1,3},{2,0},{3,1},{4,6},{5,7},{6,4},{7,5},{8,10},{9,11},{10,... | collective-permute-start | bytes 3145736 | tf_op jit(solution)/shard_map/ppermute | solution.py:271
  225.0 78.9 %collective-permute-start.19 = (bf16[1024,1408]{1,0:T(8,128)(2,1)}, bf16[1024,1408]{1,0:T(8,128)(2,1)}, u32[]{:S(2)}, u32[]{:S(2)}) collective-permute-start(bf16[1024,1408]{1,0:T(8,128)(2,1)} %all-gather.12.cloned.1.call-done.refs_2_.refs_6_.refs_8_), channel_id=1, source_target_pairs={{0,4},{4,0},{8,12},{12,8},{16,20},{20,16},{24,28},{28,24},{1,5},{5... | collective-permute-start | bytes 8650760 | tf_op jit(solution)/shard_map/ppermute | solution.py:271
  249.6 24.5 %collective-permute-start.17 = (bf16[1024,512]{1,0:T(8,128)(2,1)S(1)}, bf16[1024,512]{1,0:T(8,128)(2,1)S(1)}, u32[]{:S(2)}, u32[]{:S(2)}) collective-permute-start(bf16[1024,512]{1,0:T(8,128)(2,1)S(1)} %fusion.6.refs_0_), channel_id=1, source_target_pairs={{0,2},{1,3},{2,0},{3,1},{4,6},{5,7},{6,4},{7,5},{8,10},{9,11},{10,... | collective-permute-start | bytes 3145736 | tf_op jit(solution)/shard_map/ppermute | solution.py:271
  251.3 23.4 %collective-permute-start.16 = (bf16[1024,512]{1,0:T(8,128)(2,1)S(1)}, bf16[1024,512]{1,0:T(8,128)(2,1)S(1)}, u32[]{:S(2)}, u32[]{:S(2)}) collective-permute-start(bf16[1024,512]{1,0:T(8,128)(2,1)S(1)} %fusion.6.refs_0_), channel_id=1, source_target_pairs={{0,1},{1,0},{2,3},{3,2},{4,5},{5,4},{6,7},{7,6},{8,9},{9,8},{10,11... | collective-permute-start | bytes 3145736 | tf_op jit(solution)/shard_map/ppermute | solution.py:271
  327.9 244.4 %reduce-scatter.6.cloned.1.call-start = ((), (), s32[]{:S(2)}) async-start(), calls=%async_computation.10 | async-start | bytes 3604480 | tf_op jit(solution)/shard_map/reduce_scatter | solution.py:606
  359.3 14.7 %collective-permute-start.22 = (bf16[1024,512]{1,0:T(8,128)(2,1)}, bf16[1024,512]{1,0:T(8,128)(2,1)}, u32[]{:S(2)}, u32[]{:S(2)}) collective-permute-start(bf16[1024,512]{1,0:T(8,128)(2,1)} %get-tuple-element.103), channel_id=1, source_target_pairs={{0,1},{1,0},{2,3},{3,2},{4,5},{5,4},{6,7},{7,6},{8,9},{9,8},{10,11... | collective-permute-start | bytes 3145736 | tf_op jit(solution)/shard_map/ppermute | solution.py:271
  370.9 88.4 %collective-permute-start.30 = (bf16[1024,1408]{1,0:T(8,128)(2,1)}, bf16[1024,1408]{1,0:T(8,128)(2,1)}, u32[]{:S(2)}, u32[]{:S(2)}) collective-permute-start(bf16[1024,1408]{1,0:T(8,128)(2,1)} %rows.8), channel_id=1, source_target_pairs={{0,4},{4,0},{8,12},{12,8},{16,20},{20,16},{24,28},{28,24},{1,5},{5... | collective-permute-start | bytes 8650760 | tf_op jit(solution)/shard_map/ppermute | solution.py:271
  388.0 25.6 %collective-permute-start.24 = (bf16[1024,512]{1,0:T(8,128)(2,1)}, bf16[1024,512]{1,0:T(8,128)(2,1)}, u32[]{:S(2)}, u32[]{:S(2)}) collective-permute-start(bf16[1024,512]{1,0:T(8,128)(2,1)} %get-tuple-element.107), channel_id=1, source_target_pairs={{0,2},{1,3},{2,0},{3,1},{4,6},{5,7},{6,4},{7,5},{8,10},{9,11},{10,... | collective-permute-start | bytes 3145736 | tf_op jit(solution)/shard_map/ppermute | solution.py:271
  417.1 42.1 %collective-permute-start.26 = (bf16[1024,512]{1,0:T(8,128)(2,1)S(1)}, bf16[1024,512]{1,0:T(8,128)(2,1)}, u32[]{:S(2)}, u32[]{:S(2)}) collective-permute-start(bf16[1024,512]{1,0:T(8,128)(2,1)S(1)} %get-tuple-element.175.refs_0_), channel_id=1, source_target_pairs={{0,2},{1,3},{2,0},{3,1},{4,6},{5,7},{6,4},{7,5},{8,10},{9,11},{10,... | collective-permute-start | bytes 3145736 | tf_op jit(solution)/shard_map/ppermute | solution.py:271
  466.3 169.6 %reduce-scatter.10.cloned.1.call-start = ((), (), s32[]{:S(2)}) async-start(), calls=%async_computation.12 | async-start | bytes 3604480 | tf_op jit(solution)/shard_map/reduce_scatter | solution.py:606
  466.4 89.0 %collective-permute-start.31 = (bf16[1024,1408]{1,0:T(8,128)(2,1)}, bf16[1024,1408]{1,0:T(8,128)(2,1)}, u32[]{:S(2)}, u32[]{:S(2)}) collective-permute-start(bf16[1024,1408]{1,0:T(8,128)(2,1)} %copy-done.25), channel_id=1, source_target_pairs={{0,4},{4,0},{8,12},{12,8},{16,20},{20,16},{24,28},{28,24},{1,5},{5... | collective-permute-start | bytes 8650760 | tf_op jit(solution)/shard_map/ppermute | solution.py:271
  531.7 25.6 %collective-permute-start.29 = (bf16[1024,512]{1,0:T(8,128)(2,1)}, bf16[1024,512]{1,0:T(8,128)(2,1)}, u32[]{:S(2)}, u32[]{:S(2)}) collective-permute-start(bf16[1024,512]{1,0:T(8,128)(2,1)} %rows.10), channel_id=1, source_target_pairs={{0,4},{4,0},{8,12},{12,8},{16,20},{20,16},{24,28},{28,24},{1,5},{5... | collective-permute-start | bytes 3145736 | tf_op jit(solution)/shard_map/ppermute | solution.py:271
  564.8 115.6 %reduce-scatter.14.cloned.1.call-start = ((), (), s32[]{:S(2)}) async-start(), calls=%async_computation.14 | async-start | bytes 1310720 | tf_op jit(solution)/shard_map/reduce_scatter | solution.py:606
  565.1 24.8 %collective-permute-start.36 = (bf16[1024,512]{1,0:T(8,128)(2,1)}, bf16[1024,512]{1,0:T(8,128)(2,1)}, u32[]{:S(2)}, u32[]{:S(2)}) collective-permute-start(bf16[1024,512]{1,0:T(8,128)(2,1)} %get-tuple-element.127), channel_id=1, source_target_pairs={{0,2},{1,3},{2,0},{3,1},{4,6},{5,7},{6,4},{7,5},{8,10},{9,11},{10,... | collective-permute-start | bytes 3145736 | tf_op jit(solution)/shard_map/ppermute | solution.py:271
  566.6 69.4 %collective-permute-start.28 = (bf16[1024,1536]{1,0:T(8,128)(2,1)}, bf16[1024,1536]{1,0:T(8,128)(2,1)}, u32[]{:S(2)}, u32[]{:S(2)}) collective-permute-start(bf16[1024,1536]{1,0:T(8,128)(2,1)} %copy-done.23), channel_id=1, source_target_pairs={{0,4},{4,0},{8,12},{12,8},{16,20},{20,16},{24,28},{28,24},{1,5},{5... | collective-permute-start | bytes 9437192 | tf_op jit(solution)/shard_map/ppermute | solution.py:271
  576.4 136.3 %reduce-scatter.12.cloned.1.call-start = ((), (), s32[]{:S(2)}) async-start(), calls=%async_computation.13 | async-start | bytes 3932160 | tf_op jit(solution)/shard_map/reduce_scatter | solution.py:606
  673.9 25.2 %collective-permute-start.43 = (bf16[1024,512]{1,0:T(8,128)(2,1)}, bf16[1024,512]{1,0:T(8,128)(2,1)}, u32[]{:S(2)}, u32[]{:S(2)}) collective-permute-start(bf16[1024,512]{1,0:T(8,128)(2,1)} %get-tuple-element.137), channel_id=1, source_target_pairs={{0,2},{1,3},{2,0},{3,1},{4,6},{5,7},{6,4},{7,5},{8,10},{9,11},{10,... | collective-permute-start | bytes 3145736 | tf_op jit(solution)/shard_map/ppermute | solution.py:271
  (89 other events, 990.6 us)
Sparse Core Ops, SparseCore 0:
  10.2 66.4 all-gather.7
  78.9 26.4 all-gather.5
  107.0 58.6 all-gather.9
  167.1 57.8 all-gather.11
  227.0 105.3 all-gather.13
  335.9 129.3 reduce-scatter.7
  467.6 54.8 reduce-scatter.5
  564.9 57.3 reduce-scatter.9
  624.6 26.9 reduce-scatter.13
  653.8 58.8 reduce-scatter.11
